TPU v7x, 32 devices: a whole 2x2x4 slice. The times are simulated.
32 devices in a mesh: ens: 2 (over y), lon: 4 (over z), lat: 2 (over x), lev: 2 (over core).
Axes of the slice: x: 2, y: 2, z: 4, core: 2. Of those that a mesh axis runs over, the one named last changes fastest.
Arguments:
- fields: bfloat16 [32, 8, 32, 512], P('lev', 'ens', 'lat', 'lon'), parts along dimension 1, may hold values from -6 to 6
- arrival_cot: bfloat16 [32, 8, 32, 512], P('lev', 'ens', 'lat', 'lon'), parts along dimension 1, may hold values from -6 to 6
- weights: bfloat16 [2, 32, 4, 4, 4, 128], P('lev', 'lat', 'lon', 'ens'), parts along dimension 3, may hold values from -2 to 2
- departures: int32 [2, 32, 4, 4, 3], P('lev', 'lat', None, 'ens'), parts along dimension 3, may hold values from -1 to 15, as said below
- counts: int32 [2, 32, 8], P('lev', 'lat', 'ens'), parts along dimension 2, may hold values from 1 to 2
Outputs:
- source_cot: float32 [32, 8, 32, 512], P('lev', 'ens', 'lat', 'lon'), parts along dimension 1
- weight_cot: bfloat16 [2, 32, 4, 4, 4, 128], P('lev', 'lat', 'lon', 'ens'), parts along dimension 3
There are 2 independent parts, one for each index of `ens`. A program takes and returns all parts, laid end to end along the dimension named above; each array names one. Nothing has to cross between parts.
Inputs may be any that keep to these rules, and one draw needn't show every extreme that they name: `departures`: entry k of an arrival row block is used only for k below its count. A used entry names the arrival's own band (shift 0), one of the last 2 rows of the band above (shift -1) or one of the first 2 rows of the band below (shift 1), never a band beyond the first or last. Outside the first and last band a used entry names the arrival tile or one of its two neighbours on the loop of tiles. Over the used entries of one arrival tile, band and level group, no owner tile is named more than 11 times, and outside the first and last band the arrival's own tile is named exactly 11 times.
All inputs are finite; a program needn't handle non-finite values.
Results may differ from a plain program's by a relative error of at most 0.008.
Values may be sent and summed in bfloat16 or wider, within the bound.
No kernel may reach another device: no remote copies, remote signals or barrier semaphores. Data moves between devices by JAX's collectives and lax.ppermute only.
A program may use at most 64 MiB of HBM per device.

v0:
```python
import jax
import jax.numpy as jnp
from jax import lax
from jax.sharding import PartitionSpec as P

HR = 2
CAP = 11


source_gain = 1.0


def padded_2(shard, sides, width):
    for axis, dim in sides:
        peers, length = (lax.axis_size(axis), shard.shape[dim])
        up = [(i, (i + 1) % peers) for i in range(peers - 1)]
        down = [(j, i) for i, j in up]
        last = lax.slice_in_dim(shard, length - width, length, axis=dim)
        initial = lax.slice_in_dim(shard, 0, width, axis=dim)
        before = lax.ppermute(last, axis, up)
        after = lax.ppermute(initial, axis, down)
        shard = jnp.concatenate([before, shard, after], axis=dim)
    return shard


def shifted_2(block, axis, distance):
    devices = range(lax.axis_size(axis))
    route = [(i - distance, i) for i in devices if i - distance in devices]
    return lax.ppermute(block, axis, route)


def spread_taps(block_rows):
    first = block_rows[..., :1]
    last = block_rows[..., -1:]
    return jnp.concatenate([first, block_rows, last, last], axis=-1)


def fold_taps(pieces):
    width = pieces[0].shape[-1]
    lead = [(0, 0)] * (pieces[0].ndim - 1)
    total = jnp.zeros(pieces[0].shape[:-1] + (width + 3,), jnp.float32)
    for tap, piece in enumerate(pieces):
        total = total + jnp.pad(piece, lead + [(tap, 3 - tap)])
    inner = total[..., 1 : width + 1]
    inner = inner.at[..., 0].add(total[..., 0])
    inner = inner.at[..., width - 1].add(total[..., width + 1] + total[..., width + 2])
    return inner


def local(fields, arrival_cot, weights, departures, counts):
    lev_dev, field_count, tile_rows, tile_cols = fields.shape
    channels = lev_dev * field_count
    tile_count = lax.axis_size("lon")
    my_tile = lax.axis_index("lon")
    per_row = weights.shape[3]
    tap_count = weights.shape[4]
    capacity = CAP
    ext_span = tile_rows + 2 * HR
    field_rows = fields.reshape(channels, tile_rows, tile_cols)
    cot_rows = arrival_cot.reshape(channels, tile_rows, tile_cols)
    mixing = weights.reshape(tile_rows, per_row, tap_count, tile_cols)
    block_list = departures.reshape(tile_rows, tile_count, per_row, 3)
    number = counts.reshape(tile_rows, tile_count)
    extended = padded_2(field_rows, (("lat", 1),), HR)
    owner_tile = block_list[..., 0]
    band_shift = block_list[..., 1]
    ext_row = HR + band_shift * tile_rows + block_list[..., 2]
    usable = jnp.arange(per_row, dtype=jnp.int32)[None, None, :] < number[..., None]
    served = jnp.transpose(usable & (owner_tile == my_tile), (1, 0, 2)).reshape(
        tile_count, tile_rows * per_row
    )
    served_rows = jnp.transpose(ext_row, (1, 0, 2)).reshape(tile_count, tile_rows * per_row)
    served_rank = jnp.cumsum(served.astype(jnp.int32), axis=1) - 1
    picked = served[..., None] & (
        served_rank[..., None] == jnp.arange(capacity, dtype=jnp.int32)[None, None, :]
    )
    send_row = jnp.sum(jnp.where(picked, served_rows[..., None], 0), axis=1)
    filled = jnp.any(picked, axis=1).reshape(-1)
    send_index = jnp.where(filled, send_row.reshape(-1), ext_span)
    mine_owner = lax.dynamic_index_in_dim(owner_tile, my_tile, 1, keepdims=False).reshape(-1)
    mine_usable = lax.dynamic_index_in_dim(usable, my_tile, 1, keepdims=False)
    flat_usable = mine_usable.reshape(-1)
    per_owner = flat_usable[:, None] & (
        mine_owner[:, None] == jnp.arange(tile_count, dtype=jnp.int32)[None, :]
    )
    owner_rank = jnp.cumsum(per_owner.astype(jnp.int32), axis=0) - 1
    my_slot = jnp.sum(jnp.where(per_owner, owner_rank, 0), axis=1)
    slot_index = jnp.where(flat_usable, mine_owner * capacity + my_slot, 0)
    packed = extended[:, jnp.where(filled, send_row.reshape(-1), 0), :]
    packed = jnp.where(filled[None, :, None], packed, jnp.zeros((), packed.dtype))
    arrived = lax.all_to_all(
        packed.reshape(channels, tile_count, capacity, tile_cols),
        "lon",
        split_axis=1,
        concat_axis=1,
        tiled=True,
    )
    blocks = arrived.reshape(channels, tile_count * capacity, tile_cols)[:, slot_index, :]
    blocks = jnp.where(flat_usable[None, :, None], blocks, jnp.zeros((), blocks.dtype))
    blocks = blocks.reshape(channels, tile_rows, per_row, tile_cols)
    padded = spread_taps(blocks)
    interp = jnp.zeros((channels, tile_rows, tile_cols), jnp.float32)
    for tap in range(tap_count):
        shifted = padded[..., tap : tap + tile_cols]
        interp = interp + jnp.einsum(
            "crka,rka->cra", shifted, mixing[:, :, tap, :], preferred_element_type=jnp.float32
        )
    slope_factor = 1.0 + source_gain * (1.0 - jnp.tanh(interp) ** 2)
    scaled = (cot_rows.astype(jnp.float32) * slope_factor).astype(jnp.bfloat16)
    pieces = []
    grads = []
    for tap in range(tap_count):
        pieces.append(
            jnp.einsum(
                "cra,rka->crka", scaled, mixing[:, :, tap, :], preferred_element_type=jnp.float32
            )
        )
        shifted = padded[..., tap : tap + tile_cols]
        grads.append(
            jnp.einsum("crka,cra->rka", shifted, scaled, preferred_element_type=jnp.float32)
        )
    term = fold_taps(pieces)
    term = jnp.where(mine_usable[None, :, :, None], term, 0.0).astype(jnp.bfloat16)
    weight_grad = jnp.stack(grads, axis=2).astype(jnp.bfloat16)
    return_index = jnp.where(flat_usable, slot_index, tile_count * capacity)
    outgoing = jnp.zeros((channels, tile_count * capacity, tile_cols), jnp.bfloat16)
    outgoing = outgoing.at[:, return_index, :].set(
        term.reshape(channels, tile_rows * per_row, tile_cols), mode="drop"
    )
    returned = lax.all_to_all(
        outgoing.reshape(channels, tile_count, capacity, tile_cols),
        "lon",
        split_axis=1,
        concat_axis=1,
        tiled=True,
    )
    band_sum = jnp.zeros((channels, ext_span, tile_cols), jnp.float32)
    band_sum = band_sum.at[:, send_index, :].add(
        returned.reshape(channels, tile_count * capacity, tile_cols).astype(jnp.float32),
        mode="drop",
    )
    from_below = shifted_2(band_sum[:, :HR, :].astype(jnp.bfloat16), "lat", -1).astype(jnp.float32)
    from_above = shifted_2(band_sum[:, tile_rows + HR :, :].astype(jnp.bfloat16), "lat", 1).astype(
        jnp.float32
    )
    source_rows = band_sum[:, HR : HR + tile_rows, :]
    source_rows = source_rows.at[:, :HR, :].add(from_above)
    source_rows = source_rows.at[:, tile_rows - HR :, :].add(from_below)
    return (
        source_rows.reshape(lev_dev, field_count, tile_rows, tile_cols),
        weight_grad.reshape(weights.shape),
    )


def solution(mesh):
    return jax.shard_map(
        local,
        mesh=mesh,
        in_specs=(
            P("lev", "ens", "lat", "lon"),
            P("lev", "ens", "lat", "lon"),
            P("lev", "lat", "lon", "ens", None, None),
            P("lev", "lat", None, "ens", None),
            P("lev", "lat", "ens"),
        ),
        out_specs=(P("lev", "ens", "lat", "lon"), P("lev", "lat", "lon", "ens", None, None)),
        check_vma=False,
    )
```

profile of v0, /device:TPU:0, one launch (start us, length us, event | category | flops | bytes accessed | tf_op | source)
XLA Modules:
  0.0 101.0 jit_solution(15171460558104783857)
XLA Ops:
  0.6 1.1 %copy.71 = bf16[16,4,16,128]{3,1,0,2:T(4,128)(2,1)S(1)} copy(bf16[16,4,16,128]{3,2,1,0:T(8,128)(2,1)} %param.13) | data formatting | bytes 524288 | tf_op args[0]
  1.7 4.8 %collective-permute-start = (bf16[64,2,128]{2,0,1:T(8,128)(2,1)S(1)}, bf16[64,2,128]{2,0,1:T(8,128)(2,1)S(1)}, u32[]{:S(2)}, u32[]{:S(2)}) collective-permute-start(bf16[64,2,128]{2,0,1:T(8,128)(2,1)S(1)} %get-tuple-element.82), channel_id=1, source_target_pairs={{0,2},{1,3},{4,6},{5,7},{8,10},{9,11},{12,14},{13,15},{16,18},{17,... | collective-permute-start | bytes 98312 | tf_op jit(solution)/shard_map/ppermute | solution.py:20
  6.6 1.3 %collective-permute-start.1 = (bf16[64,2,128]{2,0,1:T(8,128)(2,1)S(1)}, bf16[64,2,128]{2,0,1:T(8,128)(2,1)S(1)}, u32[]{:S(2)}, u32[]{:S(2)}) collective-permute-start(bf16[64,2,128]{2,0,1:T(8,128)(2,1)S(1)} %get-tuple-element.83), channel_id=1, source_target_pairs={{2,0},{3,1},{6,4},{7,5},{10,8},{11,9},{14,12},{15,13},{18,16},{19,... | collective-permute-start | bytes 98312 | tf_op jit(solution)/shard_map/ppermute | solution.py:21
  7.9 0.7 copy.191
  8.6 0.7 fusion.18
  9.3 0.1 copy.61
  9.4 0.1 and.37
  9.5 0.2 reduce_window_sum.22
  9.9 0.3 fusion.11
  10.2 0.3 select_reduce_fusion
  10.7 0.1 copy.70
  10.8 1.6 %collective-permute-done.1 = bf16[64,2,128]{2,0,1:T(8,128)(2,1)S(1)} collective-permute-done((bf16[64,2,128]{2,0,1:T(8,128)(2,1)S(1)}, bf16[64,2,128]{2,0,1:T(8,128)(2,1)S(1)}, u32[]{:S(2)}, u32[]{:S(2)}) %collective-permute-start.1) | collective-permute-done | bytes 32800 | tf_op jit(solution)/shard_map/ppermute | solution.py:21
  12.4 0.7 gather_fusion
  13.1 1.0 broadcast_select_fusion
  14.1 4.9 %all-to-all-start = ((bf16[64,4,11,128]{3,0,2,1:T(8,128)(2,1)}), bf16[64,4,11,128]{3,0,2,1:T(8,128)(2,1)S(1)}, u32[]{:S(2)}, u32[]{:S(2)}) async-start(bf16[64,4,11,128]{3,0,2,1:T(8,128)(2,1)} %broadcast_select_fusion), calls=%async_computation | async-start | bytes 1441792 | tf_op jit(solution)/shard_map/all_to_all | solution.py:91
  19.0 0.1 copy.65
  19.1 0.1 and.40
  19.2 0.1 reshape.395
  19.7 0.1 mul.34
  20.0 0.2 select_reduce_fusion.1
  20.2 16.1 %all-to-all-done = bf16[64,4,11,128]{3,0,2,1:T(8,128)(2,1)S(1)} async-done(((bf16[64,4,11,128]{3,0,2,1:T(8,128)(2,1)}), bf16[64,4,11,128]{3,0,2,1:T(8,128)(2,1)S(1)}, u32[]{:S(2)}, u32[]{:S(2)}) %all-to-all-start) | async-done | bytes 720928 | tf_op jit(solution)/shard_map/all_to_all | solution.py:91
  36.3 0.6 gather_fusion.1
  36.9 0.1 broadcast_select_fusion.1
  37.0 0.2 fusion.25
  37.3 1.1 %multiply_reduce_fusion.5 = (f32[16,128,64]{1,2,0:T(8,128)S(1)}, f32[16,128,64]{1,2,0:T(8,128)S(1)}, f32[16,128,64]{1,2,0:T(8,128)S(1)}, f32[16,128,64]{1,2,0:T(8,128)S(1)}) fusion(f32[16,128,2]{1,2,0:T(2,128)S(1)} %copy.148, bf16[64,16,2,1]{3,0,2,1:T(8,128)(2,1)S(1)} %get-tuple-element.79, bf16[64,16,2,128]{3,0,2,1:T(8,128)(2,1)S(1)} %broadcast_select_fusion.1, ...), kind=kLoop, calls=%fused_computation.14 | loop fusion | flops 6029312 | bytes 2695168
  38.4 2.0 %bitcast_convert_fusion = (f32[16,128,64]{1,0,2:T(8,128)}, bf16[64,16,128]{2,1,0:T(8,128)(2,1)S(1)}) fusion(f32[16,128,64]{1,2,0:T(8,128)S(1)} %get-tuple-element.65, f32[16,128,64]{1,2,0:T(8,128)S(1)} %get-tuple-element.64, f32[16,128,64]{1,2,0:T(8,128)S(1)} %get-tuple-element.67, f32[16,128,64]{1,2,0:T(8,128)S(1)} %get-tuple-element.66, ...), kind=kLoop, calls=%fused_computation.38 | loop fusion | flops 1179648 | bytes 3145728
  40.5 0.2 copy.74
  40.7 0.6 multiply_bitcast_fusion.3
  41.3 1.7 %pad_add_fusion = f32[64,16,2,131]{3,0,2,1:T(8,128)S(1)} fusion(f32[64,16,2,128]{3,0,2,1:T(8,128)S(1)} %get-tuple-element.77, f32[64,16,2,128]{3,0,2,1:T(8,128)S(1)} %get-tuple-element.76, f32[64,16,2,128]{3,0,2,1:T(8,128)S(1)} %get-tuple-element.75, f32[64,16,2,128]{3,0,2,1:T(8,128)S(1)} %get-tuple-element.74), kind=kLoop, calls=%fused_computation.4 | loop fusion | flops 804864 | bytes 5267456 | tf_op jit(solution)/shard_map/add | solution.py:43
  43.0 1.3 %slice.219 = f32[64,16,2,128]{3,0,2,1:T(8,128)} slice(f32[64,16,2,131]{3,0,2,1:T(8,128)S(1)} %pad_add_fusion), slice={[0:64], [0:16], [0:2], [1:129]} | slice | bytes 2097152 | tf_op jit(solution)/shard_map/slice | solution.py:44
  44.3 1.4 %slice_add_fusion.1 = f32[64,16,2,1]{3,0,2,1:T(8,128)} fusion(f32[64,16,2,131]{3,0,2,1:T(8,128)S(1)} %pad_add_fusion), kind=kLoop, calls=%fused_computation.8 | loop fusion | flops 2048 | bytes 24576 | tf_op jit(solution)/shard_map/add | solution.py:45
  45.7 3.6 %scatter-add.20 = f32[64,16,2,128]{3,0,2,1:T(8,128)} dynamic-update-slice(f32[64,16,2,128]{3,0,2,1:T(8,128)} %slice.219, f32[64,16,2,1]{3,0,2,1:T(8,128)} %slice_add_fusion.1, s32[]{:T(128)} %constant.148.clone.1, s32[]{:T(128)} %constant.148.clone.1, s32[]{:T(128)} %constant.148.clone.1, s32[]{:T(128)} %constant.148.clone.1) | dynamic-update-slice | bytes 16388 | tf_op jit(solution)/shard_map/scatter-add | solution.py:45
  49.3 3.1 %fusion = f32[64,16,2,1]{3,0,2,1:T(8,128)} fusion(f32[64,16,2,131]{3,0,2,1:T(8,128)S(1)} %pad_add_fusion, f32[64,16,2,128]{3,0,2,1:T(8,128)} %scatter-add.20), kind=kLoop, calls=%fused_computation.7 | loop fusion | flops 4096 | bytes 32768 | tf_op jit(solution)/shard_map/add | solution.py:46
  52.5 5.2 %scatter-add.21 = f32[64,16,2,128]{3,0,2,1:T(8,128)} dynamic-update-slice(f32[64,16,2,128]{3,0,2,1:T(8,128)} %scatter-add.20, f32[64,16,2,1]{3,0,2,1:T(8,128)} %fusion, s32[]{:T(128)} %constant.148.clone.1, s32[]{:T(128)} %constant.148.clone.1, s32[]{:T(128)} %constant.148.clone.1, s32[]{:T(128)} %constant.159.clone.1) | dynamic-update-slice | bytes 16388 | tf_op jit(solution)/shard_map/scatter-add | solution.py:46
  57.7 1.4 %select_convert_fusion = bf16[64,16,2,128]{3,0,2,1:T(8,128)(2,1)S(1)} fusion(f32[64,16,2,128]{3,0,2,1:T(8,128)} %scatter-add.21, pred[16,2]{1,0:T(8,128)(4,1)S(1)} %bitcast.159), kind=kLoop, calls=%fused_computation.17 | loop fusion | flops 262144 | bytes 1572896 | tf_op jit(solution)/shard_map/convert_element_type | solution.py:123
  59.1 1.0 %broadcast_in_dim.89 = bf16[64,44,128]{2,0,1:T(8,128)(2,1)} broadcast(bf16[]{:T(256)} %constant.154.clone.1), dimensions={} | broadcast | bytes 720898 | tf_op jit(solution)/shard_map/broadcast_in_dim | solution.py:126
  60.1 4.3 %scatter_fusion = bf16[64,44,128]{2,0,1:T(8,128)(2,1)} fusion(bf16[64,44,128]{2,0,1:T(8,128)(2,1)} %broadcast_in_dim.89, s32[32]{0:T(128)S(1)} %get-tuple-element.97, bf16[32,64,128]{2,1,0:T(8,128)(2,1)S(1)} %bitcast.150), kind=kCustom, calls=%fused_computation.2 | custom fusion | bytes 1572992 | tf_op jit(solution)/shard_map/scatter | solution.py:127
  64.4 3.7 %all-to-all-start.1 = ((bf16[64,4,11,128]{3,0,2,1:T(8,128)(2,1)}), bf16[64,4,11,128]{3,0,2,1:T(8,128)(2,1)S(1)}, u32[]{:S(2)}, u32[]{:S(2)}) async-start(bf16[64,4,11,128]{3,0,2,1:T(8,128)(2,1)} %bitcast.57), calls=%async_computation.1 | async-start | bytes 1441792 | tf_op jit(solution)/shard_map/all_to_all | solution.py:130
  68.3 0.2 copy.150
  68.5 1.3 %multiply_reduce_fusion.3 = (bf16[16,128,2]{1,2,0:T(2,128)(2,1)S(1)}, bf16[16,128,2]{1,2,0:T(2,128)(2,1)S(1)}, bf16[16,128,2]{1,2,0:T(2,128)(2,1)S(1)}, bf16[16,128,2]{1,2,0:T(2,128)(2,1)S(1)}) fusion(f32[16,128,64]{1,2,0:T(8,128)S(1)} %copy.150, bf16[64,16,2,128]{3,0,2,1:T(8,128)(2,1)S(1)} %broadcast_select_fusion.1, ...), kind=kLoop, calls=%fused_computation.12 | loop fusion | flops 6537216 | bytes 1089536
  69.8 16.3 %all-to-all-done.1 = bf16[64,4,11,128]{3,0,2,1:T(8,128)(2,1)S(1)} async-done(((bf16[64,4,11,128]{3,0,2,1:T(8,128)(2,1)}), bf16[64,4,11,128]{3,0,2,1:T(8,128)(2,1)S(1)}, u32[]{:S(2)}, u32[]{:S(2)}) %all-to-all-start.1) | async-done | bytes 720928 | tf_op jit(solution)/shard_map/all_to_all | solution.py:130
  86.1 0.2 convert_bitcast_fusion
  86.4 3.1 %scatter_fusion.1 = f32[64,20,128]{2,0,1:T(8,128)S(1)} fusion(f32[64,20,128]{2,0,1:T(8,128)S(1)} %broadcast_in_dim.83, s32[44]{0:T(128)S(1)} %fusion.19, f32[44,64,128]{2,1,0:T(8,128)S(1)} %convert_bitcast_fusion), kind=kCustom, calls=%fused_computation.3 | custom fusion | flops 360448 | bytes 4325552 | tf_op jit(solution)/shard_map/scatter-add | solution.py:138
  89.5 3.8 %collective-permute-start.2 = (bf16[64,2,128]{2,0,1:T(8,128)(2,1)S(1)}, bf16[64,2,128]{2,0,1:T(8,128)(2,1)S(1)}, u32[]{:S(2)}, u32[]{:S(2)}) collective-permute-start(bf16[64,2,128]{2,0,1:T(8,128)(2,1)S(1)} %get-tuple-element.81), channel_id=1, source_target_pairs={{0,2},{1,3},{4,6},{5,7},{8,10},{9,11},{12,14},{13,15},{16,18},{17,... | collective-permute-start | bytes 98312 | tf_op jit(solution)/shard_map/ppermute | solution.py:29
  93.4 0.6 copy.80
  94.1 1.3 %collective-permute-start.3 = (bf16[64,2,128]{2,0,1:T(8,128)(2,1)S(1)}, bf16[64,2,128]{2,0,1:T(8,128)(2,1)S(1)}, u32[]{:S(2)}, u32[]{:S(2)}) collective-permute-start(bf16[64,2,128]{2,0,1:T(8,128)(2,1)S(1)} %get-tuple-element.80), channel_id=1, source_target_pairs={{2,0},{3,1},{6,4},{7,5},{10,8},{11,9},{14,12},{15,13},{18,16},{19,... | collective-permute-start | bytes 98312 | tf_op jit(solution)/shard_map/ppermute | solution.py:29
  95.4 4.5 %collective-permute-done.3 = bf16[64,2,128]{2,0,1:T(8,128)(2,1)S(1)} collective-permute-done((bf16[64,2,128]{2,0,1:T(8,128)(2,1)S(1)}, bf16[64,2,128]{2,0,1:T(8,128)(2,1)S(1)}, u32[]{:S(2)}, u32[]{:S(2)}) %collective-permute-start.3) | collective-permute-done | bytes 32800 | tf_op jit(solution)/shard_map/ppermute | solution.py:29
  99.9 1.1 %copy.79 = f32[16,4,16,128]{3,2,1,0:T(8,128)} copy(f32[16,4,16,128]{3,1,0,2:T(4,128)S(1)} %bitcast.148) | data formatting | bytes 1048576
  (56 shorter events, 1.4 us)
Async XLA Ops:
  1.7 9.1 %collective-permute-start = (bf16[64,2,128]{2,0,1:T(8,128)(2,1)S(1)}, bf16[64,2,128]{2,0,1:T(8,128)(2,1)S(1)}, u32[]{:S(2)}, u32[]{:S(2)}) collective-permute-start(bf16[64,2,128]{2,0,1:T(8,128)(2,1)S(1)} %get-tuple-element.82), channel_id=1, source_target_pairs={{0,2},{1,3},{4,6},{5,7},{8,10},{9,11},{12,14},{13,15},{16,18},{17,... | collective-permute-start | bytes 98312 | tf_op jit(solution)/shard_map/ppermute | solution.py:20
  6.6 5.8 %collective-permute-start.1 = (bf16[64,2,128]{2,0,1:T(8,128)(2,1)S(1)}, bf16[64,2,128]{2,0,1:T(8,128)(2,1)S(1)}, u32[]{:S(2)}, u32[]{:S(2)}) collective-permute-start(bf16[64,2,128]{2,0,1:T(8,128)(2,1)S(1)} %get-tuple-element.83), channel_id=1, source_target_pairs={{2,0},{3,1},{6,4},{7,5},{10,8},{11,9},{14,12},{15,13},{18,16},{19,... | collective-permute-start | bytes 98312 | tf_op jit(solution)/shard_map/ppermute | solution.py:21
  12.4 7.4 %copy-start.4 = (bf16[1,16,1,2,4,128]{5,4,3,2,1,0:T(4,128)(2,1)S(1)}, bf16[1,16,1,2,4,128]{5,4,3,2,1,0:T(4,128)(2,1)}, u32[]{:S(2)}) copy-start(bf16[1,16,1,2,4,128]{5,4,3,2,1,0:T(4,128)(2,1)} %param.15) | copy-start | bytes 98308
  14.1 22.1 %all-to-all-start = ((bf16[64,4,11,128]{3,0,2,1:T(8,128)(2,1)}), bf16[64,4,11,128]{3,0,2,1:T(8,128)(2,1)S(1)}, u32[]{:S(2)}, u32[]{:S(2)}) async-start(bf16[64,4,11,128]{3,0,2,1:T(8,128)(2,1)} %broadcast_select_fusion), calls=%async_computation | async-start | bytes 1441792 | tf_op jit(solution)/shard_map/all_to_all | solution.py:91
  37.3 3.2 %copy-start = (bf16[64,16,2,1]{3,0,2,1:T(8,128)(2,1)}, bf16[64,16,2,1]{3,0,2,1:T(8,128)(2,1)S(1)}, u32[]{:S(2)}) copy-start(bf16[64,16,2,1]{3,0,2,1:T(8,128)(2,1)S(1)} %get-tuple-element.79) | copy-start | bytes 12292
  37.3 1.1 %copy-start.3 = (bf16[16,4,16,128]{3,2,1,0:T(8,128)(2,1)S(1)}, bf16[16,4,16,128]{3,2,1,0:T(8,128)(2,1)}, u32[]{:S(2)}) copy-start(bf16[16,4,16,128]{3,2,1,0:T(8,128)(2,1)} %param.14) | copy-start | bytes 786436
  59.1 9.2 %copy-start.2 = (f32[16,128,64]{1,0,2:T(8,128)S(1)}, f32[16,128,64]{1,0,2:T(8,128)}, u32[]{:S(2)}) copy-start(f32[16,128,64]{1,0,2:T(8,128)} %get-tuple-element.68) | copy-start | bytes 1572868
  60.1 8.4 %copy-start.1 = (bf16[64,16,2,1]{3,0,2,1:T(8,128)(2,1)S(1)}, bf16[64,16,2,1]{3,0,2,1:T(8,128)(2,1)}, u32[]{:S(2)}) copy-start(bf16[64,16,2,1]{3,0,2,1:T(8,128)(2,1)} %copy-done) | copy-start | bytes 12292
  64.4 21.7 %all-to-all-start.1 = ((bf16[64,4,11,128]{3,0,2,1:T(8,128)(2,1)}), bf16[64,4,11,128]{3,0,2,1:T(8,128)(2,1)S(1)}, u32[]{:S(2)}, u32[]{:S(2)}) async-start(bf16[64,4,11,128]{3,0,2,1:T(8,128)(2,1)} %bitcast.57), calls=%async_computation.1 | async-start | bytes 1441792 | tf_op jit(solution)/shard_map/all_to_all | solution.py:130
  89.5 5.8 %collective-permute-start.2 = (bf16[64,2,128]{2,0,1:T(8,128)(2,1)S(1)}, bf16[64,2,128]{2,0,1:T(8,128)(2,1)S(1)}, u32[]{:S(2)}, u32[]{:S(2)}) collective-permute-start(bf16[64,2,128]{2,0,1:T(8,128)(2,1)S(1)} %get-tuple-element.81), channel_id=1, source_target_pairs={{0,2},{1,3},{4,6},{5,7},{8,10},{9,11},{12,14},{13,15},{16,18},{17,... | collective-permute-start | bytes 98312 | tf_op jit(solution)/shard_map/ppermute | solution.py:29
  94.1 5.8 %collective-permute-start.3 = (bf16[64,2,128]{2,0,1:T(8,128)(2,1)S(1)}, bf16[64,2,128]{2,0,1:T(8,128)(2,1)S(1)}, u32[]{:S(2)}, u32[]{:S(2)}) collective-permute-start(bf16[64,2,128]{2,0,1:T(8,128)(2,1)S(1)} %get-tuple-element.80), channel_id=1, source_target_pairs={{2,0},{3,1},{6,4},{7,5},{10,8},{11,9},{14,12},{15,13},{18,16},{19,... | collective-permute-start | bytes 98312 | tf_op jit(solution)/shard_map/ppermute | solution.py:29
where the time goes:
time: 102 us; the launch traced here: 101 us
  waiting for transfers between devices  38.4 us (38%)
  local copies, waits for them, and re-layouts  22.7 us (22%)
  starting transfers between devices  19.8 us (19%)
  other arithmetic  19 us (19%)
  between operations  1.05 us (1%)
    all_to_all x1, waiting for transfers between devices, local(): lax.all_to_all(outgoing.reshape(channels, tile_count, capacity, tile_cols...  16.3 us
    all_to_all x1, waiting for transfers between devices, local(): lax.all_to_all(packed.reshape(channels, tile_count, capacity, tile_cols),...  16.1 us
    scatter-add x1, local copies, waits for them, and re-layouts, fold_taps(): inner.at[..., width - 1].add(total[..., width + 1] + total[..., width + 2])  5.2 us
    ppermute x2, starting transfers between devices, shifted_2(): return lax.ppermute(block, axis, route)  5.13 us
    all_to_all x1, starting transfers between devices, local(): lax.all_to_all(packed.reshape(channels, tile_count, capacity, tile_cols),...  4.87 us
    ppermute x1, starting transfers between devices, padded_2(): before = lax.ppermute(last, axis, up)  4.84 us
    ppermute x2, waiting for transfers between devices, shifted_2(): return lax.ppermute(block, axis, route)  4.48 us
    unnamed x3, other arithmetic  4.38 us
  transfers between devices with their start and end apart: 6, of which 4 were waited for; matrix products, arithmetic and copies ran while one was open for 6% of the time, Pallas kernels for 0%

commit v1 on v0

v1 whole, which is shorter than its diff:
```python
import functools

import jax
import jax.numpy as jnp
from jax import lax
from jax.experimental import pallas as pl
from jax.experimental.pallas import tpu as pltpu
from jax.sharding import PartitionSpec as P

HR = 2
CAP = 11
STRIDE = 16
SHIFT = 8
BF16 = jnp.bfloat16
F32 = jnp.float32
VMEM = pltpu.VMEM
SMEM = pltpu.SMEM


def whole(space):
    return pl.BlockSpec(memory_space=space)


def wrap(value, size):
    return jnp.where(value < 0, value + size, value)


def prepare_kernel(tiles, per_row, code_ref, fields_ref, rows_ref, send_ref, loc_ref, wide, taken):
    rows, channels, _ = rows_ref.shape
    me = lax.axis_index("lon")
    dump = rows + 2 * HR
    wide[...] = fields_ref[...].astype(F32)
    for r in range(rows):
        rows_ref[r] = wide[pl.ds(r, channels, stride=rows), :].astype(BF16)

    def serve(a, _):
        base = wrap(a - me, tiles) * STRIDE
        filled = jnp.int32(0)
        for r in range(rows):
            for k in range(per_row):
                code = code_ref[(r * tiles + a) * per_row + k]
                send_ref[base + filled] = code & ((1 << SHIFT) - 1)
                filled = filled + jnp.where((code >> SHIFT) == me, 1, 0)
        for s in range(CAP):
            send_ref[base + s] = jnp.where(s < filled, send_ref[base + s], dump)
        return 0

    lax.fori_loop(0, tiles, serve, 0)
    for d in range(tiles + 1):
        taken[d] = 0

    def place(r, _):
        for k in range(per_row):
            code = code_ref[(r * tiles + me) * per_row + k]
            owner = code >> SHIFT
            used = owner >= 0
            d = jnp.where(used, wrap(me - owner, tiles), tiles)
            slot = taken[d]
            taken[d] = slot + 1
            loc_ref[r * per_row + k] = jnp.where(used, d * CAP + slot, tiles * CAP)
        return 0

    lax.fori_loop(0, rows, place, 0)


def pack_kernel(tiles, send_ref, rows_ref, before_ref, after_ref, *rest):
    outs, (ext, wide) = rest[:tiles], rest[tiles:]
    rows, channels, _ = rows_ref.shape
    ext[HR : HR + rows] = rows_ref[...]
    for start, halo in ((0, before_ref), (HR + rows, after_ref)):
        wide[...] = halo[...].astype(F32)
        for h in range(HR):
            ext[start + h] = wide[pl.ds(h, channels, stride=HR), :].astype(BF16)
    for d in range(tiles):
        for s in range(CAP):
            outs[d][s] = ext[send_ref[d * STRIDE + s]]


def arrival_kernel(cot_ref, taps_ref, cot_rows_ref, folded_ref, wide):
    rows, channels, cols = cot_rows_ref.shape
    wide[...] = cot_ref[...].astype(F32)
    for r in range(rows):
        cot_rows_ref[r] = wide[pl.ds(r, channels, stride=rows), :].astype(BF16)
    w0, w1, w2, w3 = (taps_ref[j] for j in range(4))
    cell = lax.broadcasted_iota(jnp.int32, w0.shape, 1)
    first, last, late = cell == 0, cell == cols - 1, cell == cols - 2
    folded_ref[0] = jnp.where(first, 0.0, w0)
    folded_ref[1] = w1 + jnp.where(first, w0, 0.0) + jnp.where(last, w2 + w3, 0.0)
    folded_ref[2] = jnp.where(last, 0.0, w2) + jnp.where(late, w3, 0.0)
    folded_ref[3] = jnp.where(last | late, 0.0, w3)


def compute_kernel(tiles, per_row, loc_ref, folded_ref, cot_ref, *rest):
    arrived, rest = rest[:tiles], rest[tiles:]
    outs, rest = rest[:tiles], rest[tiles:]
    grad_ref, blocks, terms = rest
    rows, channels, cols = cot_ref.shape
    part = min(channels, 32)
    for d in range(tiles):
        blocks[d * CAP : (d + 1) * CAP] = arrived[d][...]
    blocks[tiles * CAP] = jnp.zeros((channels, cols), BF16)

    def row(r, _):
        index = [loc_ref[r * per_row + k] for k in range(per_row)]
        mix = [
            [folded_ref[j, pl.ds(r * per_row + k, 1), :] for j in range(4)] for k in range(per_row)
        ]
        grads = [[jnp.zeros((8, cols), F32) for _ in range(4)] for _ in range(per_row)]
        for lo in range(0, channels, part):
            shifted = []
            interp = jnp.zeros((part, cols), F32)
            for k in range(per_row):
                block = blocks[index[k], lo : lo + part].astype(F32)
                moved = [
                    pltpu.roll(block, 1, 1),
                    block,
                    pltpu.roll(block, cols - 1, 1),
                    pltpu.roll(block, cols - 2, 1),
                ]
                for j in range(4):
                    interp = interp + moved[j] * mix[k][j]
                shifted.append(moved)
            bent = jnp.tanh(interp)
            scaled = cot_ref[r, lo : lo + part].astype(F32) * (2.0 - bent * bent)
            scaled = scaled.astype(BF16).astype(F32)
            for k in range(per_row):
                pieces = [scaled * mix[k][j] for j in range(4)]
                term = (
                    pieces[1]
                    + pltpu.roll(pieces[0], cols - 1, 1)
                    + pltpu.roll(pieces[2], 1, 1)
                    + pltpu.roll(pieces[3], 2, 1)
                )
                terms[index[k], lo : lo + part] = term.astype(BF16)
                for j in range(4):
                    product = (shifted[k][j] * scaled).reshape(part // 8, 8, cols)
                    grads[k][j] = grads[k][j] + jnp.sum(product, axis=0)
        for k in range(per_row):
            for j in range(4):
                grad_ref[r, k * 4 + j : k * 4 + j + 1, :] = jnp.sum(grads[k][j], axis=0, keepdims=True)
        return 0

    lax.fori_loop(0, rows, row, 0)
    for d in range(tiles):
        outs[d][...] = terms[d * CAP : (d + 1) * CAP]


def gather_kernel(tiles, send_ref, *rest):
    returned, (rows_ref, first_ref, last_ref, total) = rest[:tiles], rest[tiles:]
    rows = rows_ref.shape[0]
    total[...] = jnp.zeros_like(total)
    for d in range(tiles):
        for s in range(CAP):
            at = send_ref[d * STRIDE + s]
            total[at] = total[at] + returned[d][s].astype(F32)
    rows_ref[...] = total[HR : HR + rows]
    first_ref[...] = total[0:HR].astype(BF16)
    last_ref[...] = total[HR + rows : HR + rows + HR].astype(BF16)


def finish_kernel(bands, rows_ref, above_ref, below_ref, out_ref):
    rows, channels, _ = rows_ref.shape
    band = lax.axis_index("lat")
    has_above = jnp.where(band > 0, 1, 0)
    has_below = jnp.where(band < bands - 1, 1, 0)
    for r in range(rows):
        value = rows_ref[r]
        if r < HR:
            value = value + jnp.where(has_above == 1, above_ref[r].astype(F32), 0.0)
        if r >= rows - HR:
            value = value + jnp.where(has_below == 1, below_ref[r - rows + HR].astype(F32), 0.0)
        out_ref[pl.ds(r, channels, stride=rows), :] = value


def swap_lat(to_above, to_below, bands):
    band = lax.axis_index("lat")
    if bands == 2:
        sent = jnp.where(band == 0, to_below, to_above)
        got = lax.ppermute(sent, "lat", [(0, 1), (1, 0)])
        return got, got
    down = [(i, i + 1) for i in range(bands - 1)]
    up = [(i + 1, i) for i in range(bands - 1)]
    return lax.ppermute(to_below, "lat", down), lax.ppermute(to_above, "lat", up)


def local(fields, arrival_cot, weights, departures, counts):
    lev_dev, field_count, rows, cols = fields.shape
    channels = lev_dev * field_count
    tiles = lax.axis_size("lon")
    bands = lax.axis_size("lat")
    my_tile = lax.axis_index("lon")
    per_row, taps = weights.shape[3], weights.shape[4]
    ext = rows + 2 * HR
    params = pltpu.CompilerParams(vmem_limit_bytes=48 * 1024 * 1024)

    def call(kernel, out_shape, in_specs, out_specs, scratch=(), name=None):
        return pl.pallas_call(
            kernel,
            out_shape=out_shape,
            in_specs=in_specs,
            out_specs=out_specs,
            scratch_shapes=list(scratch),
            compiler_params=params,
            name=name,
        )

    def array(shape, dtype):
        return jax.ShapeDtypeStruct(shape, dtype)

    to_above = fields[:, :, :HR].reshape(channels * HR, cols)
    to_below = fields[:, :, rows - HR :].reshape(channels * HR, cols)
    before, after = swap_lat(to_above, to_below, bands)

    lists = departures.reshape(rows, tiles, per_row, 3)
    number = counts.reshape(rows, tiles)
    usable = jnp.arange(per_row, dtype=jnp.int32)[None, None, :] < number[..., None]
    ext_row = HR + lists[..., 1] * rows + lists[..., 2]
    code = jnp.where(usable, (lists[..., 0] << SHIFT) + ext_row, -1).reshape(-1)

    row_blocks, send_rows, places = call(
        functools.partial(prepare_kernel, tiles, per_row),
        (
            array((rows, channels, cols), BF16),
            array((tiles * STRIDE,), jnp.int32),
            array((rows * per_row,), jnp.int32),
        ),
        [whole(SMEM), whole(VMEM)],
        (whole(VMEM), whole(SMEM), whole(SMEM)),
        [VMEM((channels * rows, cols), F32), SMEM((tiles + 1,), jnp.int32)],
        "prepare",
    )(code, fields.reshape(channels * rows, cols))

    slots = array((CAP, channels, cols), BF16)
    packed = call(
        functools.partial(pack_kernel, tiles),
        (slots,) * tiles,
        [whole(SMEM), whole(VMEM), whole(VMEM), whole(VMEM)],
        (whole(VMEM),) * tiles,
        [VMEM((ext + 1, channels, cols), BF16), VMEM((channels * HR, cols), F32)],
        "pack",
    )(send_rows, row_blocks, before, after)

    def moved(parts, sign):
        out = [parts[0]]
        for d in range(1, tiles):
            route = [(i, (i + sign * d) % tiles) for i in range(tiles)]
            out.append(lax.ppermute(parts[d], "lon", route))
        return out

    arrived = moved(packed, 1)

    mine = lax.dynamic_index_in_dim(usable, my_tile, 1, keepdims=False)
    mixing = weights.reshape(rows, per_row, taps, cols).astype(F32)
    mixing = jnp.where(mine[:, :, None, None], mixing, 0.0)
    mixing = jnp.transpose(mixing, (2, 0, 1, 3)).reshape(taps, rows * per_row, cols)
    cot_rows, folded = call(
        arrival_kernel,
        (array((rows, channels, cols), BF16), array(mixing.shape, F32)),
        [whole(VMEM)] * 2,
        (whole(VMEM),) * 2,
        [VMEM((channels * rows, cols), F32)],
        "arrival",
    )(arrival_cot.reshape(channels * rows, cols), mixing)

    *terms, grads = call(
        functools.partial(compute_kernel, tiles, per_row),
        (slots,) * tiles + (array((rows, per_row * taps, cols), F32),),
        [whole(SMEM)] + [whole(VMEM)] * (2 + tiles),
        (whole(VMEM),) * (tiles + 1),
        [VMEM((tiles * CAP + 1, channels, cols), BF16)] * 2,
        "compute",
    )(places, folded, cot_rows, *arrived)

    returned = moved(terms, -1)

    row_sums, to_above, to_below = call(
        functools.partial(gather_kernel, tiles),
        (
            array((rows, channels, cols), F32),
            array((HR, channels, cols), BF16),
            array((HR, channels, cols), BF16),
        ),
        [whole(SMEM)] + [whole(VMEM)] * tiles,
        (whole(VMEM),) * 3,
        [VMEM((ext + 1, channels, cols), F32)],
        "gather",
    )(send_rows, *returned)

    from_above, from_below = swap_lat(to_above, to_below, bands)

    source = call(
        functools.partial(finish_kernel, bands),
        array((channels * rows, cols), F32),
        [whole(VMEM)] * 3,
        whole(VMEM),
        (),
        "finish",
    )(row_sums, from_above, from_below)

    grads = grads.reshape(rows, per_row, taps, cols)
    g0, g1, g2, g3 = (grads[:, :, j] for j in range(4))
    cell = jnp.arange(cols)[None, None, :]
    g0 = jnp.where(cell == 0, g1, g0)
    g3 = jnp.where(cell == cols - 2, g2, g3)
    g3 = jnp.where(cell == cols - 1, g1, g3)
    g2 = jnp.where(cell == cols - 1, g1, g2)
    weight_grad = jnp.stack([g0, g1, g2, g3], axis=2)
    weight_grad = jnp.where(mine[:, :, None, None], weight_grad, 0.0).astype(BF16)
    return source.reshape(fields.shape), weight_grad.reshape(weights.shape)


def solution(mesh):
    return jax.shard_map(
        local,
        mesh=mesh,
        in_specs=(
            P("lev", "ens", "lat", "lon"),
            P("lev", "ens", "lat", "lon"),
            P("lev", "lat", "lon", "ens", None, None),
            P("lev", "lat", None, "ens", None),
            P("lev", "lat", "ens"),
        ),
        out_specs=(P("lev", "ens", "lat", "lon"), P("lev", "lat", "lon", "ens", None, None)),
        check_vma=False,
    )
```

time: 102 us -> 59 us (0.58)
  local copies, waits for them, and re-layouts: 22.7 us -> 0.75 us
  other arithmetic: 19 us -> 4.11 us
  waiting for transfers between devices: 38.4 us -> 28.6 us
  Pallas kernels: 0 us -> 9.37 us
  starting transfers between devices: 19.8 us -> 15.3 us
    all_to_all x2 -> x0, waiting for transfers between devices: 32.4 us -> none  [the longest x1 16.3 us: local(): lax.all_to_all(outgoing.reshape(channels, tile_count, capacity, tile_cols...]
    ppermute x4 -> x8, waiting for transfers between devices: 6.05 us -> 28.6 us  [the longest x6 25.9 us: moved(): out.append(lax.ppermute(parts[d], 'lon', route))]
    pallas_call x0 -> x6, Pallas kernels: none -> 9.37 us  [the longest x1 4.5 us: local(): call(functools.partial(compute_kernel, tiles, per_row), (slots,) * tiles...]
    scatter-add x2 -> x0, local copies, waits for them, and re-layouts: 8.85 us -> none  [the longest x1 5.2 us: fold_taps(): inner.at[..., width - 1].add(total[..., width + 1] + total[..., width + 2])]
    all_to_all x2 -> x0, starting transfers between devices: 8.54 us -> none  [the longest x1 4.87 us: local(): lax.all_to_all(packed.reshape(channels, tile_count, capacity, tile_cols),...]
    add x3 -> x1, other arithmetic: 6.2 us -> 0.73 us  [local(): code = jnp.where(usable, (lists[..., 0] << SHIFT) + ext_row, -1).reshape(-1)]
    unnamed x3 -> x0, other arithmetic: 4.38 us -> none
    scatter x1 -> x0, local copies, waits for them, and re-layouts: 4.32 us -> none  [local(): outgoing.at[:, return_index, :]]
  transfers between devices with their start and end apart: 6 -> 8, of which waited for: 4 -> 5; matrix products, arithmetic and copies ran while one was open for 6% -> 6% of each run, Pallas kernels for 0% -> 4%
where the time goes in v1:
time: 59 us; the launch traced here: 58.8 us
  waiting for transfers between devices  28.6 us (48%)
  starting transfers between devices  15.3 us (26%)
  Pallas kernels  9.37 us (16%)
  other arithmetic  4.11 us (7%)
  between operations  0.78 us (1%)
  local copies, waits for them, and re-layouts  0.75 us (1%)
    ppermute x6, waiting for transfers between devices, moved(): out.append(lax.ppermute(parts[d], 'lon', route))  25.9 us
    ppermute x6, starting transfers between devices, moved(): out.append(lax.ppermute(parts[d], 'lon', route))  11.7 us
    pallas_call x1, Pallas kernels, local(): call(functools.partial(compute_kernel, tiles, per_row), (slots,) * tiles...  4.5 us
    ppermute x2, starting transfers between devices, swap_lat(): got = lax.ppermute(sent, 'lat', [(0, 1), (1, 0)])  3.61 us
    ppermute x2, waiting for transfers between devices, swap_lat(): got = lax.ppermute(sent, 'lat', [(0, 1), (1, 0)])  2.66 us
    pallas_call x1, Pallas kernels, local(): call(functools.partial(prepare_kernel, tiles, per_row), (array((rows, cha...  2.14 us
  transfers between devices with their start and end apart: 8, of which 5 were waited for; matrix products, arithmetic and copies ran while one was open for 6% of the time, Pallas kernels for 4%

profile of v1, /device:TPU:0, one launch (start us, length us, event | category | flops | bytes accessed | tf_op | source)
XLA Modules:
  0.0 58.8 jit_solution(15464319889113633177)
XLA Ops:
  0.6 0.0 copy-start
  0.6 1.1 %broadcast_select_fusion = bf16[16,4,2,128]{3,2,1,0:T(2,128)(2,1)S(1)} fusion(pred[]{:T(512)S(6)} %eq.37, bf16[16,4,16,128]{3,2,1,0:T(8,128)(2,1)} %param.5), kind=kLoop, calls=%fused_computation.4 | loop fusion | flops 16384 | bytes 98305 | tf_op jit(solution)/shard_map/jit(_where)/select_n | solution.py:178
  1.7 3.0 %collective-permute-start = (bf16[128,128]{1,0:T(8,128)(2,1)S(1)}, bf16[128,128]{1,0:T(8,128)(2,1)S(1)}, u32[]{:S(2)}, u32[]{:S(2)}) collective-permute-start(bf16[128,128]{1,0:T(8,128)(2,1)S(1)} %bitcast.46), channel_id=1, source_target_pairs={{0,2},{2,0},{1,3},{3,1},{4,6},{6,4},{5,7},{7,5},{8,10},{10,8},{9,1... | collective-permute-start | bytes 98312 | tf_op jit(solution)/shard_map/ppermute | solution.py:179
  4.7 0.7 %iota_compare_fusion = pred[16,4,2]{0,2,1:T(4,128)(4,1)S(1)} fusion(s32[16,4]{0,1:T(4,128)} %bitcast.48), kind=kLoop, calls=%fused_computation.14 | loop fusion | flops 128 | bytes 384 | tf_op jit(solution)/shard_map/lt | solution.py:216
  5.4 0.1 copy.19
  5.5 0.1 lt.27
  5.7 0.7 %fusion.2 = s32[16,4,2,1]{0,2,3,1:T(2,128)S(1)} fusion(s32[16,4,2,3]{0,2,3,1:T(2,128)} %bitcast.47), kind=kLoop, calls=%fused_computation.10 | loop fusion | flops 640 | bytes 2048 | tf_op jit(solution)/shard_map/add | solution.py:218
  6.4 0.1 copy.20
  6.5 0.1 add.28
  6.7 0.0 copy-start.1
  6.7 0.1 copy.21
  6.8 0.9 %fusion.1 = f32[4,16,2,128]{3,0,2,1:T(4,128)S(1)} fusion(bf16[1,16,1,2,4,128]{5,4,3,2,1,0:T(4,128)(2,1)} %param.7, pred[16,2]{1,0:T(8,128)(4,1)S(1)} %copy.21), kind=kLoop, calls=%fused_computation.3 | loop fusion | flops 32768 | bytes 98336 | tf_op jit(solution)/shard_map/transpose | solution.py:255
  7.7 0.0 copy-done
  7.7 2.1 %prepare.1 = (bf16[16,64,128]{2,1,0:T(8,128)(2,1)S(1)}, s32[64]{0:T(128)S(1)}, s32[32]{0:T(128)S(1)}) custom-call(s32[128]{0:T(128)S(1)} %broadcast_select_fusion.4.code_ref, bf16[1024,128]{1,0:T(8,128)(2,1)S(1)} %bitcast.33), custom_call_target="tpu_custom_call" | custom-call | tf_op jit(solution)/shard_map/prepare/pallas_call | solution.py:220
  9.9 0.0 copy-done.1
  9.9 0.2 arrival.1
  10.1 0.0 collective-permute-done.before_ref.after_ref
  10.1 0.6 %pack.1 = (bf16[11,64,128]{2,1,0:T(8,128)(2,1)S(1)}, bf16[11,64,128]{2,1,0:T(8,128)(2,1)S(1)}, bf16[11,64,128]{2,1,0:T(8,128)(2,1)S(1)}, bf16[11,64,128]{2,1,0:T(8,128)(2,1)S(1)}) custom-call(s32[64]{0:T(128)S(1)} %get-tuple-element.19.send_ref, bf16[16,64,128]{2,1,0:T(8,128)(2,1)S(1)} %get-tuple-element.23.rows_ref, ...), custom_call_target="tpu_custom_call" | custom-call | tf_op jit(solution)/shard_map/pack/pallas_call | solution.py:234
  10.7 1.6 %collective-permute-start.1 = (bf16[11,64,128]{2,1,0:T(8,128)(2,1)S(1)}, bf16[11,64,128]{2,1,0:T(8,128)(2,1)S(1)}, u32[]{:S(2)}, u32[]{:S(2)}) collective-permute-start(bf16[11,64,128]{2,1,0:T(8,128)(2,1)S(1)} %get-tuple-element.25), channel_id=1, source_target_pairs={{0,4},{4,8},{8,12},{12,0},{1,5},{5,9},{9,13},{13,1},{2,6},{6,10},{... | collective-permute-start | bytes 540680 | tf_op jit(solution)/shard_map/ppermute | solution.py:247
  12.4 2.6 %collective-permute-start.2 = (bf16[11,64,128]{2,1,0:T(8,128)(2,1)S(1)}, bf16[11,64,128]{2,1,0:T(8,128)(2,1)S(1)}, u32[]{:S(2)}, u32[]{:S(2)}) collective-permute-start(bf16[11,64,128]{2,1,0:T(8,128)(2,1)S(1)} %get-tuple-element.26), channel_id=1, source_target_pairs={{0,8},{4,12},{8,0},{12,4},{1,9},{5,13},{9,1},{13,5},{2,10},{6,14},... | collective-permute-start | bytes 540680 | tf_op jit(solution)/shard_map/ppermute | solution.py:247
  14.9 1.3 %collective-permute-start.3 = (bf16[11,64,128]{2,1,0:T(8,128)(2,1)S(1)}, bf16[11,64,128]{2,1,0:T(8,128)(2,1)S(1)}, u32[]{:S(2)}, u32[]{:S(2)}) collective-permute-start(bf16[11,64,128]{2,1,0:T(8,128)(2,1)S(1)} %get-tuple-element.27), channel_id=1, source_target_pairs={{0,12},{4,0},{8,4},{12,8},{1,13},{5,1},{9,5},{13,9},{2,14},{6,2},{... | collective-permute-start | bytes 540680 | tf_op jit(solution)/shard_map/ppermute | solution.py:247
  16.3 3.8 %collective-permute-done.1.rest_1_ = bf16[11,64,128]{2,1,0:T(8,128)(2,1)S(1)} collective-permute-done((bf16[11,64,128]{2,1,0:T(8,128)(2,1)S(1)}, bf16[11,64,128]{2,1,0:T(8,128)(2,1)S(1)}, u32[]{:S(2)}, u32[]{:S(2)}) %collective-permute-start.1) | collective-permute-done | bytes 180256 | tf_op jit(solution)/shard_map/ppermute | solution.py:247
  20.2 6.3 %collective-permute-done.2.rest_2_ = bf16[11,64,128]{2,1,0:T(8,128)(2,1)S(1)} collective-permute-done((bf16[11,64,128]{2,1,0:T(8,128)(2,1)S(1)}, bf16[11,64,128]{2,1,0:T(8,128)(2,1)S(1)}, u32[]{:S(2)}, u32[]{:S(2)}) %collective-permute-start.2) | collective-permute-done | bytes 180256 | tf_op jit(solution)/shard_map/ppermute | solution.py:247
  26.5 0.0 collective-permute-done.3.rest_3_
  26.5 4.5 %compute.1 = (bf16[11,64,128]{2,1,0:T(8,128)(2,1)S(1)}, bf16[11,64,128]{2,1,0:T(8,128)(2,1)S(1)}, bf16[11,64,128]{2,1,0:T(8,128)(2,1)S(1)}, bf16[11,64,128]{2,1,0:T(8,128)(2,1)S(1)}, f32[16,8,128]{2,1,0:T(8,128)S(1)}) custom-call(s32[32]{0:T(128)S(1)} %get-tuple-element.20.loc_ref, f32[4,32,128]{2,1,0:T(8,128)S(1)} %get-tuple-element.21.folded_ref, ...), custom_call_target="tpu_custom_call" | custom-call | tf_op jit(solution)/shard_map/compute/pallas_call | solution.py:265
  31.0 5.5 %collective-permute-start.4 = (bf16[11,64,128]{2,1,0:T(8,128)(2,1)S(1)}, bf16[11,64,128]{2,1,0:T(8,128)(2,1)S(1)}, u32[]{:S(2)}, u32[]{:S(2)}) collective-permute-start(bf16[11,64,128]{2,1,0:T(8,128)(2,1)S(1)} %get-tuple-element.29), channel_id=1, source_target_pairs={{0,12},{4,0},{8,4},{12,8},{1,13},{5,1},{9,5},{13,9},{2,14},{6,2},{... | collective-permute-start | bytes 540680 | tf_op jit(solution)/shard_map/ppermute | solution.py:247
  36.5 0.4 collective-permute-start.5
  36.9 0.2 collective-permute-start.6
  37.2 4.3 %collective-permute-done.4.rest_1_ = bf16[11,64,128]{2,1,0:T(8,128)(2,1)S(1)} collective-permute-done((bf16[11,64,128]{2,1,0:T(8,128)(2,1)S(1)}, bf16[11,64,128]{2,1,0:T(8,128)(2,1)S(1)}, u32[]{:S(2)}, u32[]{:S(2)}) %collective-permute-start.4) | collective-permute-done | bytes 180256 | tf_op jit(solution)/shard_map/ppermute | solution.py:247
  41.5 11.4 %collective-permute-done.5.rest_2_ = bf16[11,64,128]{2,1,0:T(8,128)(2,1)S(1)} collective-permute-done((bf16[11,64,128]{2,1,0:T(8,128)(2,1)S(1)}, bf16[11,64,128]{2,1,0:T(8,128)(2,1)S(1)}, u32[]{:S(2)}, u32[]{:S(2)}) %collective-permute-start.5) | collective-permute-done | bytes 180256 | tf_op jit(solution)/shard_map/ppermute | solution.py:247
  52.9 0.0 collective-permute-done.6.rest_3_
  52.9 0.9 %gather.1 = (f32[16,64,128]{2,1,0:T(8,128)S(1)}, bf16[2,64,128]{2,1,0:T(8,128)(2,1)S(1)}, bf16[2,64,128]{2,1,0:T(8,128)(2,1)S(1)}) custom-call(s32[64]{0:T(128)S(1)} %get-tuple-element.19.send_ref, bf16[11,64,128]{2,1,0:T(8,128)(2,1)S(1)} %get-tuple-element.28.rest_0_, bf16[11,64,128]{2,1,0:T(8,128)(2,1)S(1)} %collective-permute-done.4.rest_1_, ...), custom_call_target="tpu_custom_call" | custom-call | tf_op jit(solution)/shard_map/gather/pallas_call | solution.py:276
  53.8 0.6 %collective-permute-start.7 = (bf16[2,64,128]{2,1,0:T(8,128)(2,1)S(1)}, bf16[2,64,128]{2,1,0:T(8,128)(2,1)S(1)}, u32[]{:S(2)}, u32[]{:S(2)}) collective-permute-start(bf16[2,64,128]{2,1,0:T(8,128)(2,1)S(1)} %broadcast_select_fusion.1), channel_id=1, source_target_pairs={{0,2},{2,0},{1,3},{3,1},{4,6},{6,4},{5,7},{7,5},{8,10},{10,8},{9,1... | collective-permute-start | bytes 98312 | tf_op jit(solution)/shard_map/ppermute | solution.py:179
  54.4 0.7 %fusion = bf16[1,16,1,2,4,128]{5,4,3,2,1,0:T(4,128)(2,1)} fusion(f32[1,16,1,2,1,128]{5,4,3,2,1,0:T(1,128)S(1)} %bitcast.40, f32[1,16,1,2,1,128]{5,4,3,2,1,0:T(1,128)S(1)} %bitcast.39, bf16[1,16,1,2,1,128]{5,4,3,2,1,0:T(2,128)(2,1)S(1)} %slice_bitcast_fusion, f32[1,16,1,2,1,128]{5,4,3,2,1,0:T(1,128)S(1)} %bitcast.41, pred[16,2]{1,0:T(8,128)(4,1)S(1)} %copy.21), kind=kLoop, calls=%fused_computation.1 | loop fusion | flops 147456 | bytes 90144 | tf_op jit(solution)/shard_map/convert_element_type | solution.py:308
  55.1 2.7 %collective-permute-done.7.above_ref.below_ref = bf16[2,64,128]{2,1,0:T(8,128)(2,1)S(1)} collective-permute-done((bf16[2,64,128]{2,1,0:T(8,128)(2,1)S(1)}, bf16[2,64,128]{2,1,0:T(8,128)(2,1)S(1)}, u32[]{:S(2)}, u32[]{:S(2)}) %collective-permute-start.7) | collective-permute-done | bytes 32800 | tf_op jit(solution)/shard_map/ppermute | solution.py:179
  57.8 1.0 %finish.1 = f32[1024,128]{1,0:T(8,128)} custom-call(f32[16,64,128]{2,1,0:T(8,128)S(1)} %get-tuple-element.32.rows_ref, bf16[2,64,128]{2,1,0:T(8,128)(2,1)S(1)} %collective-permute-done.7.above_ref.below_ref, bf16[2,64,128]{2,1,0:T(8,128)(2,1)S(1)} %collective-permute-done.7.above_ref.below_ref), custom_call_target="tpu_custom_call" | custom-call | tf_op jit(solution)/shard_map/finish/pallas_call | solution.py:291
  (9 shorter events, 0.2 us)
Async XLA Ops:
  0.6 7.1 %copy-start = (bf16[16,4,16,128]{3,2,1,0:T(8,128)(2,1)S(1)}, bf16[16,4,16,128]{3,2,1,0:T(8,128)(2,1)}, u32[]{:S(2)}) copy-start(bf16[16,4,16,128]{3,2,1,0:T(8,128)(2,1)} %param.5) | copy-start | bytes 786436
  1.7 8.4 %collective-permute-start = (bf16[128,128]{1,0:T(8,128)(2,1)S(1)}, bf16[128,128]{1,0:T(8,128)(2,1)S(1)}, u32[]{:S(2)}, u32[]{:S(2)}) collective-permute-start(bf16[128,128]{1,0:T(8,128)(2,1)S(1)} %bitcast.46), channel_id=1, source_target_pairs={{0,2},{2,0},{1,3},{3,1},{4,6},{6,4},{5,7},{7,5},{8,10},{10,8},{9,1... | collective-permute-start | bytes 98312 | tf_op jit(solution)/shard_map/ppermute | solution.py:179
  6.7 3.2 %copy-start.1 = (bf16[16,4,16,128]{3,2,1,0:T(8,128)(2,1)S(1)}, bf16[16,4,16,128]{3,2,1,0:T(8,128)(2,1)}, u32[]{:S(2)}) copy-start(bf16[16,4,16,128]{3,2,1,0:T(8,128)(2,1)} %param.6) | copy-start | bytes 786436
  10.7 9.4 %collective-permute-start.1 = (bf16[11,64,128]{2,1,0:T(8,128)(2,1)S(1)}, bf16[11,64,128]{2,1,0:T(8,128)(2,1)S(1)}, u32[]{:S(2)}, u32[]{:S(2)}) collective-permute-start(bf16[11,64,128]{2,1,0:T(8,128)(2,1)S(1)} %get-tuple-element.25), channel_id=1, source_target_pairs={{0,4},{4,8},{8,12},{12,0},{1,5},{5,9},{9,13},{13,1},{2,6},{6,10},{... | collective-permute-start | bytes 540680 | tf_op jit(solution)/shard_map/ppermute | solution.py:247
  12.4 14.1 %collective-permute-start.2 = (bf16[11,64,128]{2,1,0:T(8,128)(2,1)S(1)}, bf16[11,64,128]{2,1,0:T(8,128)(2,1)S(1)}, u32[]{:S(2)}, u32[]{:S(2)}) collective-permute-start(bf16[11,64,128]{2,1,0:T(8,128)(2,1)S(1)} %get-tuple-element.26), channel_id=1, source_target_pairs={{0,8},{4,12},{8,0},{12,4},{1,9},{5,13},{9,1},{13,5},{2,10},{6,14},... | collective-permute-start | bytes 540680 | tf_op jit(solution)/shard_map/ppermute | solution.py:247
  14.9 11.5 %collective-permute-start.3 = (bf16[11,64,128]{2,1,0:T(8,128)(2,1)S(1)}, bf16[11,64,128]{2,1,0:T(8,128)(2,1)S(1)}, u32[]{:S(2)}, u32[]{:S(2)}) collective-permute-start(bf16[11,64,128]{2,1,0:T(8,128)(2,1)S(1)} %get-tuple-element.27), channel_id=1, source_target_pairs={{0,12},{4,0},{8,4},{12,8},{1,13},{5,1},{9,5},{13,9},{2,14},{6,2},{... | collective-permute-start | bytes 540680 | tf_op jit(solution)/shard_map/ppermute | solution.py:247
  31.0 10.5 %collective-permute-start.4 = (bf16[11,64,128]{2,1,0:T(8,128)(2,1)S(1)}, bf16[11,64,128]{2,1,0:T(8,128)(2,1)S(1)}, u32[]{:S(2)}, u32[]{:S(2)}) collective-permute-start(bf16[11,64,128]{2,1,0:T(8,128)(2,1)S(1)} %get-tuple-element.29), channel_id=1, source_target_pairs={{0,12},{4,0},{8,4},{12,8},{1,13},{5,1},{9,5},{13,9},{2,14},{6,2},{... | collective-permute-start | bytes 540680 | tf_op jit(solution)/shard_map/ppermute | solution.py:247
  36.5 16.4 %collective-permute-start.5 = (bf16[11,64,128]{2,1,0:T(8,128)(2,1)S(1)}, bf16[11,64,128]{2,1,0:T(8,128)(2,1)S(1)}, u32[]{:S(2)}, u32[]{:S(2)}) collective-permute-start(bf16[11,64,128]{2,1,0:T(8,128)(2,1)S(1)} %get-tuple-element.30), channel_id=1, source_target_pairs={{0,8},{4,12},{8,0},{12,4},{1,9},{5,13},{9,1},{13,5},{2,10},{6,14},... | collective-permute-start | bytes 540680 | tf_op jit(solution)/shard_map/ppermute | solution.py:247
  36.9 16.0 %collective-permute-start.6 = (bf16[11,64,128]{2,1,0:T(8,128)(2,1)S(1)}, bf16[11,64,128]{2,1,0:T(8,128)(2,1)S(1)}, u32[]{:S(2)}, u32[]{:S(2)}) collective-permute-start(bf16[11,64,128]{2,1,0:T(8,128)(2,1)S(1)} %get-tuple-element.31), channel_id=1, source_target_pairs={{0,4},{4,8},{8,12},{12,0},{1,5},{5,9},{9,13},{13,1},{2,6},{6,10},{... | collective-permute-start | bytes 540680 | tf_op jit(solution)/shard_map/ppermute | solution.py:247
  53.8 4.0 %collective-permute-start.7 = (bf16[2,64,128]{2,1,0:T(8,128)(2,1)S(1)}, bf16[2,64,128]{2,1,0:T(8,128)(2,1)S(1)}, u32[]{:S(2)}, u32[]{:S(2)}) collective-permute-start(bf16[2,64,128]{2,1,0:T(8,128)(2,1)S(1)} %broadcast_select_fusion.1), channel_id=1, source_target_pairs={{0,2},{2,0},{1,3},{3,1},{4,6},{6,4},{5,7},{7,5},{8,10},{10,8},{9,1... | collective-permute-start | bytes 98312 | tf_op jit(solution)/shard_map/ppermute | solution.py:179

commit v2 on v1

v2 whole, which is shorter than its diff:
```python
import functools

import jax
import jax.numpy as jnp
from jax import lax
from jax.experimental import pallas as pl
from jax.experimental.pallas import tpu as pltpu
from jax.sharding import PartitionSpec as P

HR = 2
CAP = 11
EARLY = 3
SHARED = 5
SPARE = CAP - SHARED
SLOTS = EARLY + SHARED + SPARE
STRIDE = 16
TRASH = STRIDE - 2
COUNT = STRIDE - 1
BF16 = jnp.bfloat16
F32 = jnp.float32
VMEM = pltpu.VMEM
SMEM = pltpu.SMEM


def whole(space):
    return pl.BlockSpec(memory_space=space)


def wrap(value, size):
    return jnp.where(value < 0, value + size, value)


def decode(lists_ref, number_ref, r, a, k, rows):
    used = k < number_ref[0, r, a]
    owner = jnp.where(used, lists_ref[0, r, a, k, 0], -1)
    shift = lists_ref[0, r, a, k, 1]
    return owner, HR + shift * rows + lists_ref[0, r, a, k, 2], shift == 0


def prepare_kernel(tiles, bands, per_row, lists_ref, number_ref, fields_ref, *rest):
    rows_ref, send_ref, *rest = rest
    edges = rest[: 1 if bands == 2 else 2]
    early = rest[len(edges) : len(edges) + tiles - 1]
    wide = rest[-1]
    rows, channels, _ = rows_ref.shape
    me = lax.axis_index("lon")
    dump = rows + 2 * HR
    for i in range(tiles * STRIDE):
        send_ref[i] = dump

    def serve(a):
        base = wrap(a - me, tiles) * STRIDE
        near = jnp.int32(0)
        other = jnp.int32(0)
        for r in range(rows):
            for k in range(per_row):
                owner, row, own_band = decode(lists_ref, number_ref, r, a, k, rows)
                hit = owner == me
                ahead = hit & own_band & (near < EARLY)
                slot = jnp.where(ahead, near, EARLY + other)
                send_ref[base + jnp.where(hit, slot, TRASH)] = row
                near = near + jnp.where(ahead, 1, 0)
                other = other + jnp.where(hit, 1, 0) - jnp.where(ahead, 1, 0)
        send_ref[base + COUNT] = other

    if tiles <= 4:
        for a in range(tiles):
            serve(a)
    else:
        pl.loop(0, tiles)(serve)
    wide[...] = fields_ref[...].astype(F32)
    for r in range(rows):
        rows_ref[r] = wide[pl.ds(r, channels, stride=rows), :].astype(BF16)
    if bands == 2:
        start = jnp.where(lax.axis_index("lat") == 0, rows - HR, 0)
        edges[0][...] = rows_ref[pl.ds(start, HR)]
    else:
        edges[0][...] = rows_ref[0:HR]
        edges[1][...] = rows_ref[rows - HR : rows]
    for d in range(1, tiles):
        for s in range(EARLY):
            row = send_ref[d * STRIDE + s]
            early[d - 1][s] = rows_ref[jnp.where(row == dump, 0, row - HR)]


def pack_kernel(tiles, send_ref, rows_ref, before_ref, after_ref, *rest):
    shared, (own, spare, ext) = rest[: tiles - 1], rest[tiles - 1 :]
    rows = rows_ref.shape[0]
    ext[0:HR] = before_ref[...]
    ext[HR : HR + rows] = rows_ref[...]
    ext[HR + rows : HR + rows + HR] = after_ref[...]
    for d in range(1, tiles):
        for s in range(SHARED):
            shared[d - 1][s] = ext[send_ref[d * STRIDE + EARLY + s]]
    for s in range(SLOTS):
        own[s] = ext[send_ref[s]]
    for d in range(1, tiles):

        @pl.when(send_ref[d * STRIDE + COUNT] > SHARED)
        def _():
            for s in range(SPARE):
                spare[d - 1, s] = ext[send_ref[d * STRIDE + EARLY + SHARED + s]]


def arrival_kernel(
    tiles, per_row, lists_ref, number_ref, cot_ref, taps_ref, cot_rows_ref, mix_ref, place_ref, wide, near, other
):
    rows, channels, cols = cot_rows_ref.shape
    me = lax.axis_index("lon")
    for d in range(tiles + 1):
        near[d] = 0
        other[d] = 0

    def place(r):
        for k in range(per_row):
            owner, _, own_band = decode(lists_ref, number_ref, r, me, k, rows)
            used = owner >= 0
            d = jnp.where(used, wrap(me - owner, tiles), tiles)
            ahead = own_band & (near[d] < EARLY)
            slot = d * SLOTS + jnp.where(ahead, near[d], EARLY + other[d])
            place_ref[r * per_row + k] = jnp.where(used, slot, tiles * SLOTS)
            near[d] = near[d] + jnp.where(ahead, 1, 0)
            other[d] = other[d] + jnp.where(ahead, 0, 1)

    pl.loop(0, rows)(place)
    for d in range(tiles):
        place_ref[rows * per_row + d] = other[d]

    wide[...] = cot_ref[...].astype(F32)
    for r in range(rows):
        cot_rows_ref[r] = wide[pl.ds(r, channels, stride=rows), :].astype(BF16)
    w0, w1, w2, w3 = (taps_ref[j] for j in range(4))
    cell = lax.broadcasted_iota(jnp.int32, w0.shape, 1)
    first, last, late = cell == 0, cell == cols - 1, cell == cols - 2
    mix_ref[0] = pltpu.roll(jnp.where(first, 0.0, w0), cols - 1, 1)
    mix_ref[1] = w1 + jnp.where(first, w0, 0.0) + jnp.where(last, w2 + w3, 0.0)
    mix_ref[2] = pltpu.roll(jnp.where(last, 0.0, w2) + jnp.where(late, w3, 0.0), 1, 1)
    mix_ref[3] = pltpu.roll(jnp.where(last | late, 0.0, w3), 2, 1)


def compute_kernel(tiles, per_row, place_ref, mix_ref, cot_ref, own_ref, *rest):
    n = tiles - 1
    early, shared, spare, rest = rest[:n], rest[n : 2 * n], rest[2 * n], rest[2 * n + 1 :]
    own_out, early_out, rest = rest[0], rest[1 : n + 1], rest[n + 1 :]
    shared_out, (spare_out, grad_ref, blocks, terms) = rest[:n], rest[n:]
    rows, channels, cols = cot_ref.shape
    part = min(channels, 32)
    blocks[0:SLOTS] = own_ref[...]
    for d in range(1, tiles):
        base = d * SLOTS
        blocks[base : base + EARLY] = early[d - 1][...]
        blocks[base + EARLY : base + EARLY + SHARED] = shared[d - 1][...]

        @pl.when(place_ref[rows * per_row + d] > SHARED)
        def _():
            blocks[base + EARLY + SHARED : base + SLOTS] = spare[d - 1]

    blocks[tiles * SLOTS] = jnp.zeros((channels, cols), BF16)

    def row(r, _):
        index = [place_ref[r * per_row + k] for k in range(per_row)]
        mix = [[mix_ref[j, pl.ds(r * per_row + k, 1), :] for j in range(4)] for k in range(per_row)]
        for lo in range(0, channels, part):
            block = [blocks[index[k], lo : lo + part].astype(F32) for k in range(per_row)]
            tap = [sum(block[k] * mix[k][j] for k in range(per_row)) for j in range(4)]
            interp = (tap[1] + pltpu.roll(tap[0], 1, 1)) + (
                pltpu.roll(tap[2], cols - 1, 1) + pltpu.roll(tap[3], cols - 2, 1)
            )
            bent = jnp.tanh(interp)
            scaled = cot_ref[r, lo : lo + part].astype(F32) * (2.0 - bent * bent)
            scaled = scaled.astype(BF16).astype(F32)
            moved = [
                pltpu.roll(scaled, cols - 1, 1),
                scaled,
                pltpu.roll(scaled, 1, 1),
                pltpu.roll(scaled, 2, 1),
            ]
            for k in range(per_row):
                term = (moved[0] * mix[k][0] + moved[1] * mix[k][1]) + (
                    moved[2] * mix[k][2] + moved[3] * mix[k][3]
                )
                terms[index[k], lo : lo + part] = term.astype(BF16)
                for j in range(4):
                    at = (r * per_row + k) * 4 + j
                    product = jnp.sum((block[k] * moved[j]).reshape(part // 8, 8, cols), axis=0)
                    grad_ref[at] = product if lo == 0 else grad_ref[at] + product
        return 0

    lax.fori_loop(0, rows, row, 0, unroll=4)
    own_out[...] = terms[0:SLOTS]
    for d in range(1, tiles):
        base = d * SLOTS
        early_out[d - 1][...] = terms[base : base + EARLY]
        shared_out[d - 1][...] = terms[base + EARLY : base + EARLY + SHARED]

        @pl.when(place_ref[rows * per_row + d] > SHARED)
        def _():
            spare_out[d - 1] = terms[base + EARLY + SHARED : base + SLOTS]


def add_own_kernel(send_ref, own_ref, total_ref):
    total_ref[...] = jnp.zeros_like(total_ref)
    for s in range(SLOTS):
        at = send_ref[s]
        total_ref[at] = total_ref[at] + own_ref[s].astype(F32)


def add_shared_kernel(tiles, bands, send_ref, start_ref, spare_ref, *rest):
    shared, (total_ref, *edges) = rest[: tiles - 1], rest[tiles - 1 :]
    ext = total_ref.shape[0] - 1
    total_ref[...] = start_ref[...]
    for d in range(1, tiles):
        for s in range(SHARED):
            at = send_ref[d * STRIDE + EARLY + s]
            total_ref[at] = total_ref[at] + shared[d - 1][s].astype(F32)

        @pl.when(send_ref[d * STRIDE + COUNT] > SHARED)
        def _():
            for s in range(SPARE):
                at = send_ref[d * STRIDE + EARLY + SHARED + s]
                total_ref[at] = total_ref[at] + spare_ref[d - 1, s].astype(F32)

    if bands == 2:
        start = jnp.where(lax.axis_index("lat") == 0, ext - HR, 0)
        edges[0][...] = total_ref[pl.ds(start, HR)].astype(BF16)
    else:
        edges[0][...] = total_ref[0:HR].astype(BF16)
        edges[1][...] = total_ref[ext - HR : ext].astype(BF16)


def finish_kernel(tiles, bands, rows, send_ref, start_ref, above_ref, below_ref, *rest):
    early, (out_ref, total) = rest[: tiles - 1], rest[tiles - 1 :]
    channels = start_ref.shape[1]
    total[...] = start_ref[...]
    for d in range(1, tiles):
        for s in range(EARLY):
            at = send_ref[d * STRIDE + s]
            total[at] = total[at] + early[d - 1][s].astype(F32)
    band = lax.axis_index("lat")
    for r in range(rows):
        value = total[HR + r]
        if r < HR:
            value = value + jnp.where(band > 0, above_ref[r].astype(F32), 0.0)
        if r >= rows - HR:
            value = value + jnp.where(band < bands - 1, below_ref[r - rows + HR].astype(F32), 0.0)
        out_ref[pl.ds(r, channels, stride=rows), :] = value


def swap_lat(edges, bands):
    if bands == 2:
        got = lax.ppermute(edges[0], "lat", [(0, 1), (1, 0)])
        return got, got
    down = [(i, i + 1) for i in range(bands - 1)]
    up = [(i + 1, i) for i in range(bands - 1)]
    return lax.ppermute(edges[1], "lat", down), lax.ppermute(edges[0], "lat", up)


def local(fields, arrival_cot, weights, departures, counts):
    lev_dev, field_count, rows, cols = fields.shape
    channels = lev_dev * field_count
    tiles = lax.axis_size("lon")
    bands = lax.axis_size("lat")
    my_tile = lax.axis_index("lon")
    per_row, taps = weights.shape[3], weights.shape[4]
    ext = rows + 2 * HR
    params = pltpu.CompilerParams(vmem_limit_bytes=48 * 1024 * 1024)

    def call(kernel, out_shape, in_specs, out_specs, scratch=(), name=None):
        return pl.pallas_call(
            kernel,
            out_shape=out_shape,
            in_specs=in_specs,
            out_specs=out_specs,
            scratch_shapes=list(scratch),
            compiler_params=params,
            name=name,
        )

    def array(*shape, dtype=BF16):
        return jax.ShapeDtypeStruct(shape, dtype)

    def moved(parts, sign):
        out = []
        for d, part in enumerate(parts, 1):
            route = [(i, (i + sign * d) % tiles) for i in range(tiles)]
            out.append(lax.ppermute(part, "lon", route))
        return out

    def moved_spare(needed, part, sign):
        def send(part):
            return jnp.stack(moved([part[d] for d in range(tiles - 1)], sign))

        return lax.cond(needed, send, lambda part: part, part)

    partners = tiles - 1
    edge = (array(HR, channels, cols),) * (1 if bands == 2 else 2)
    early_slots = (array(EARLY, channels, cols),) * partners
    shared_slots = (array(SHARED, channels, cols),) * partners
    spare_slots = array(partners, SPARE, channels, cols)
    own_slots = array(SLOTS, channels, cols)

    row_blocks, send_rows, *rest = call(
        functools.partial(prepare_kernel, tiles, bands, per_row),
        (array(rows, channels, cols), array(tiles * STRIDE, dtype=jnp.int32)) + edge + early_slots,
        [whole(SMEM), whole(SMEM), whole(VMEM)],
        (whole(VMEM), whole(SMEM)) + (whole(VMEM),) * (len(edge) + partners),
        [VMEM((channels * rows, cols), F32)],
        "prepare",
    )(departures, counts, fields.reshape(channels * rows, cols))
    edges, early = rest[: len(edge)], rest[len(edge) :]
    early = moved(early, 1)
    before, after = swap_lat(edges, bands)

    lists = departures.reshape(rows, tiles, per_row, 3)
    number = counts.reshape(rows, tiles)
    usable = jnp.arange(per_row, dtype=jnp.int32)[None, None, :] < number[..., None]
    named = usable[..., None] & (lists[..., 0][..., None] == jnp.arange(tiles, dtype=jnp.int32))
    own_band = (lists[..., 1] == 0)[..., None]
    near = jnp.sum(jnp.where(named & own_band, 1, 0), axis=(0, 2))
    far = jnp.sum(jnp.where(named & ~own_band, 1, 0), axis=(0, 2))
    apart = ~jnp.eye(tiles, dtype=bool)
    needed = jnp.any((far + jnp.maximum(near - EARLY, 0) > SHARED) & apart)

    *shared, own, spare = call(
        functools.partial(pack_kernel, tiles),
        shared_slots + (own_slots, spare_slots),
        [whole(SMEM)] + [whole(VMEM)] * 3,
        (whole(VMEM),) * (partners + 2),
        [VMEM((ext + 1, channels, cols), BF16)],
        "pack",
    )(send_rows, row_blocks, before, after)
    shared = moved(shared, 1)
    spare = moved_spare(needed, spare, 1)

    mine = lax.dynamic_index_in_dim(usable, my_tile, 1, keepdims=False)
    mixing = weights.reshape(rows, per_row, taps, cols).astype(F32)
    mixing = jnp.where(mine[:, :, None, None], mixing, 0.0)
    mixing = jnp.transpose(mixing, (2, 0, 1, 3)).reshape(taps, rows * per_row, cols)
    cot_rows, mix, places = call(
        functools.partial(arrival_kernel, tiles, per_row),
        (
            array(rows, channels, cols),
            array(*mixing.shape, dtype=F32),
            array(rows * per_row + tiles, dtype=jnp.int32),
        ),
        [whole(SMEM), whole(SMEM), whole(VMEM), whole(VMEM)],
        (whole(VMEM), whole(VMEM), whole(SMEM)),
        [VMEM((channels * rows, cols), F32)] + [SMEM((tiles + 1,), jnp.int32)] * 2,
        "arrival",
    )(departures, counts, arrival_cot.reshape(channels * rows, cols), mixing)

    own, *rest = call(
        functools.partial(compute_kernel, tiles, per_row),
        (own_slots,)
        + early_slots
        + shared_slots
        + (spare_slots, array(rows * per_row * taps, 8, cols, dtype=F32)),
        [whole(SMEM)] + [whole(VMEM)] * (4 + 2 * partners),
        (whole(VMEM),) * (3 + 2 * partners),
        [VMEM((tiles * SLOTS + 1, channels, cols), BF16)] * 2,
        "compute",
    )(places, mix, cot_rows, own, *early, *shared, spare)
    early, shared, (spare, grads) = rest[:partners], rest[partners : 2 * partners], rest[2 * partners :]

    shared = moved(shared, -1)
    spare = moved_spare(needed, spare, -1)
    early = moved(early, -1)

    sums = array(ext + 1, channels, cols, dtype=F32)
    total = call(add_own_kernel, sums, [whole(SMEM), whole(VMEM)], whole(VMEM), (), "add_own")(
        send_rows, own
    )
    total, *edges = call(
        functools.partial(add_shared_kernel, tiles, bands),
        (sums,) + edge,
        [whole(SMEM)] + [whole(VMEM)] * (2 + partners),
        (whole(VMEM),) * (1 + len(edge)),
        (),
        "add_shared",
    )(send_rows, total, spare, *shared)
    from_above, from_below = swap_lat(edges, bands)
    source = call(
        functools.partial(finish_kernel, tiles, bands, rows),
        array(channels * rows, cols, dtype=F32),
        [whole(SMEM)] + [whole(VMEM)] * (3 + partners),
        whole(VMEM),
        [VMEM((ext + 1, channels, cols), F32)],
        "finish",
    )(send_rows, total, from_above, from_below, *early)

    grads = jnp.sum(grads.reshape(rows, per_row, taps, 8, cols), axis=3)
    g0, g1, g2, g3 = (jnp.roll(grads[:, :, j], 1 - j, axis=-1) for j in range(4))
    cell = jnp.arange(cols)[None, None, :]
    g0 = jnp.where(cell == 0, g1, g0)
    g3 = jnp.where(cell == cols - 2, g2, g3)
    g3 = jnp.where(cell == cols - 1, g1, g3)
    g2 = jnp.where(cell == cols - 1, g1, g2)
    weight_grad = jnp.stack([g0, g1, g2, g3], axis=2)
    weight_grad = jnp.where(mine[:, :, None, None], weight_grad, 0.0).astype(BF16)
    return source.reshape(fields.shape), weight_grad.reshape(weights.shape)


def solution(mesh):
    return jax.shard_map(
        local,
        mesh=mesh,
        in_specs=(
            P("lev", "ens", "lat", "lon"),
            P("lev", "ens", "lat", "lon"),
            P("lev", "lat", "lon", "ens", None, None),
            P("lev", "lat", None, "ens", None),
            P("lev", "lat", "ens"),
        ),
        out_specs=(P("lev", "ens", "lat", "lon"), P("lev", "lat", "lon", "ens", None, None)),
        check_vma=False,
    )
```

time: 59 us -> 47.6 us (0.81)
  waiting for transfers between devices: 28.6 us -> 8.26 us
  starting transfers between devices: 15.3 us -> 20.8 us
  other arithmetic: 4.11 us -> 1.33 us
  local copies, waits for them, and re-layouts: 0.75 us -> 3.4 us
  Pallas kernels: 9.37 us -> 12 us
  between operations: 0.78 us -> 1.51 us
    ppermute x8 -> x14, waiting for transfers between devices: 28.6 us -> 8.26 us  [the longest x12 5.69 us: moved(): out.append(lax.ppermute(part, 'lon', route))]
    ppermute x8 -> x14, starting transfers between devices: 15.3 us -> 20.8 us  [the longest x12 17.2 us: moved(): out.append(lax.ppermute(part, 'lon', route))]
    pallas_call x6 -> x7, Pallas kernels: 9.37 us -> 12 us  [the longest x1 3.42 us: local(): call(functools.partial(prepare_kernel, tiles, bands, per_row), (array(row...]
    unnamed x4 -> x14, local copies, waits for them, and re-layouts: 0.01 us -> 2.53 us
    select_n x4 -> x0, other arithmetic: 1.1 us -> none  [the longest x2 1.07 us: swap_lat(): sent = jnp.where(band == 0, to_below, to_above)]
    transpose x1, other arithmetic: 0.86 us -> 0.1 us  [local(): jnp.transpose(mixing, (2, 0, 1, 3)).reshape(taps, rows * per_row, cols)]
    add x1 -> x0, other arithmetic: 0.73 us -> none  [local(): code = jnp.where(usable, (lists[..., 0] << SHIFT) + ext_row, -1).reshape(-1)]
    lt x1, other arithmetic: 0.69 us -> 0.01 us  [local(): jnp.arange(per_row, dtype=jnp.int32)[None, None, :] < number[..., None]]
  transfers between devices with their start and end apart: 8 -> 14, of which waited for: 5 -> 4; matrix products, arithmetic and copies ran while one was open for 6% -> 4% of each run, Pallas kernels for 4% -> 10%
where the time goes in v2:
time: 47.6 us; the launch traced here: 47.3 us
  starting transfers between devices  20.8 us (44%)
  Pallas kernels  12 us (25%)
  waiting for transfers between devices  8.26 us (17%)
  local copies, waits for them, and re-layouts  3.4 us (7%)
  between operations  1.51 us (3%)
  other arithmetic  1.33 us (3%)
    ppermute x12, starting transfers between devices, moved(): out.append(lax.ppermute(part, 'lon', route))  17.2 us
    ppermute x12, waiting for transfers between devices, moved(): out.append(lax.ppermute(part, 'lon', route))  5.69 us
    ppermute x2, starting transfers between devices, swap_lat(): got = lax.ppermute(edges[0], 'lat', [(0, 1), (1, 0)])  3.64 us
    pallas_call x1, Pallas kernels, local(): call(functools.partial(prepare_kernel, tiles, bands, per_row), (array(row...  3.42 us
    pallas_call x1, Pallas kernels, local(): call(functools.partial(arrival_kernel, tiles, per_row), (array(rows, chan...  2.82 us
    ppermute x2, waiting for transfers between devices, swap_lat(): got = lax.ppermute(edges[0], 'lat', [(0, 1), (1, 0)])  2.57 us
    unnamed x14, local copies, waits for them, and re-layouts  2.53 us
    pallas_call x1, Pallas kernels, local(): call(functools.partial(compute_kernel, tiles, per_row), (own_slots,) + ea...  2.07 us
  transfers between devices with their start and end apart: 14, of which 4 were waited for; matrix products, arithmetic and copies ran while one was open for 4% of the time, Pallas kernels for 10%

profile of v2, /device:TPU:0, one launch (start us, length us, event | category | flops | bytes accessed | tf_op | source)
XLA Modules:
  0.0 47.3 jit_solution(11964620609178150293)
XLA Ops:
  0.6 0.8 %copy.77.lists_ref = s32[1,16,4,2,3]{4,3,2,1,0:T(2,128)S(1)} copy(s32[1,16,4,2,3]{1,3,4,2,0:T(2,128)} %param.12) | data formatting | bytes 3072 | tf_op args[3]
  1.5 0.1 copy.78.number_ref
  1.6 0.9 %copy-done = bf16[16,4,16,128]{3,2,1,0:T(8,128)(2,1)S(1)} copy-done((bf16[16,4,16,128]{3,2,1,0:T(8,128)(2,1)S(1)}, bf16[16,4,16,128]{3,2,1,0:T(8,128)(2,1)}, u32[]{:S(2)}) %copy-start) | copy-done | bytes 262168
  2.5 3.4 %prepare.1 = (bf16[16,64,128]{2,1,0:T(8,128)(2,1)S(1)}, s32[64]{0:T(128)S(1)}, bf16[2,64,128]{2,1,0:T(8,128)(2,1)S(1)}, bf16[3,64,128]{2,1,0:T(8,128)(2,1)S(1)},...) custom-call(s32[1,16,4,2,3]{4,3,2,1,0:T(2,128)S(1)} %copy.77.lists_ref, ...), custom_call_target="tpu_custom_call" | custom-call | tf_op jit(solution)/shard_map/prepare/pallas_call | solution.py:302
  6.0 3.0 %collective-permute-start.6 = (bf16[2,64,128]{2,1,0:T(8,128)(2,1)S(1)}, bf16[2,64,128]{2,1,0:T(8,128)(2,1)S(1)}, u32[]{:S(2)}, u32[]{:S(2)}) collective-permute-start(bf16[2,64,128]{2,1,0:T(8,128)(2,1)S(1)} %get-tuple-element.42), channel_id=1, source_target_pairs={{0,2},{2,0},{1,3},{3,1},{4,6},{6,4},{5,7},{7,5},{8,10},{10,8},{9,1... | collective-permute-start | bytes 98312 | tf_op jit(solution)/shard_map/ppermute | solution.py:251
  9.0 1.6 %collective-permute-start.7 = (bf16[3,64,128]{2,1,0:T(8,128)(2,1)S(1)}, bf16[3,64,128]{2,1,0:T(8,128)(2,1)S(1)}, u32[]{:S(2)}, u32[]{:S(2)}) collective-permute-start(bf16[3,64,128]{2,1,0:T(8,128)(2,1)S(1)} %get-tuple-element.44), channel_id=1, source_target_pairs={{0,4},{4,8},{8,12},{12,0},{1,5},{5,9},{9,13},{13,1},{2,6},{6,10},{... | collective-permute-start | bytes 147464 | tf_op jit(solution)/shard_map/ppermute | solution.py:286
  10.5 2.6 %collective-permute-start.8 = (bf16[3,64,128]{2,1,0:T(8,128)(2,1)S(1)}, bf16[3,64,128]{2,1,0:T(8,128)(2,1)S(1)}, u32[]{:S(2)}, u32[]{:S(2)}) collective-permute-start(bf16[3,64,128]{2,1,0:T(8,128)(2,1)S(1)} %get-tuple-element.45), channel_id=1, source_target_pairs={{0,8},{4,12},{8,0},{12,4},{1,9},{5,13},{9,1},{13,5},{2,10},{6,14},... | collective-permute-start | bytes 147464 | tf_op jit(solution)/shard_map/ppermute | solution.py:286
  13.2 0.2 select_reduce_fusion
  13.4 0.6 %fusion.8 = pred[]{:T(512)} fusion(s32[4,4]{1,0:T(4,128)S(1)} %get-tuple-element.69, s32[4,4]{1,0:T(4,128)S(1)} %get-tuple-element.68), kind=kLoop, calls=%fused_computation.36 | loop fusion | flops 127 | bytes 129 | tf_op jit(solution)/shard_map/reduce_or | solution.py:322
  14.7 0.0 collective-permute-done.6.before_ref.after_ref
  14.7 0.6 %pack.1 = (bf16[5,64,128]{2,1,0:T(8,128)(2,1)S(1)}, bf16[5,64,128]{2,1,0:T(8,128)(2,1)S(1)}, bf16[5,64,128]{2,1,0:T(8,128)(2,1)S(1)}, bf16[14,64,128]{2,1,0:T(8,128)(2,1)S(1)}, bf16[3,6,64,128]{3,2,1,0:T(8,128)(2,1)S(1)}) custom-call(s32[64]{0:T(128)S(1)} %get-tuple-element.37.send_ref, bf16[16,64,128]{2,1,0:T(8,128)(2,1)S(1)} %get-tuple-element.41.rows_ref, ...), custom_call_target="tpu_custom_call" | custom-call | tf_op jit(solution)/shard_map/pack/pallas_call | solution.py:324
  15.4 0.0 copy-start.3
  15.4 0.0 copy-start.1
  15.4 1.4 %collective-permute-start.9 = (bf16[3,64,128]{2,1,0:T(8,128)(2,1)S(1)}, bf16[3,64,128]{2,1,0:T(8,128)(2,1)S(1)}, u32[]{:S(2)}, u32[]{:S(2)}) collective-permute-start(bf16[3,64,128]{2,1,0:T(8,128)(2,1)S(1)} %get-tuple-element.46), channel_id=1, source_target_pairs={{0,12},{4,0},{8,4},{12,8},{1,13},{5,1},{9,5},{13,9},{2,14},{6,2},{... | collective-permute-start | bytes 147464 | tf_op jit(solution)/shard_map/ppermute | solution.py:286
  16.8 0.1 copy.79
  16.9 0.1 fusion.1
  17.0 0.7 %collective-permute-start.10 = (bf16[5,64,128]{2,1,0:T(8,128)(2,1)S(1)}, bf16[5,64,128]{2,1,0:T(8,128)(2,1)S(1)}, u32[]{:S(2)}, u32[]{:S(2)}) collective-permute-start(bf16[5,64,128]{2,1,0:T(8,128)(2,1)S(1)} %get-tuple-element.47), channel_id=1, source_target_pairs={{0,4},{4,8},{8,12},{12,0},{1,5},{5,9},{9,13},{13,1},{2,6},{6,10},{... | collective-permute-start | bytes 245768 | tf_op jit(solution)/shard_map/ppermute | solution.py:286
  17.8 0.4 collective-permute-start.11
  18.2 0.0 collective-permute-done.7.rest_0_
  18.2 2.7 %collective-permute-start.12 = (bf16[5,64,128]{2,1,0:T(8,128)(2,1)S(1)}, bf16[5,64,128]{2,1,0:T(8,128)(2,1)S(1)}, u32[]{:S(2)}, u32[]{:S(2)}) collective-permute-start(bf16[5,64,128]{2,1,0:T(8,128)(2,1)S(1)} %get-tuple-element.49), channel_id=1, source_target_pairs={{0,12},{4,0},{8,4},{12,8},{1,13},{5,1},{9,5},{13,9},{2,14},{6,2},{... | collective-permute-start | bytes 245768 | tf_op jit(solution)/shard_map/ppermute | solution.py:286
  21.0 2.8 %arrival.1 = (bf16[16,64,128]{2,1,0:T(8,128)(2,1)S(1)}, f32[4,32,128]{2,1,0:T(8,128)S(1)}, s32[36]{0:T(128)S(1)}) custom-call(s32[1,16,4,2,3]{4,3,2,1,0:T(2,128)S(1)} %copy.77.lists_ref, s32[1,16,4]{2,1,0:T(8,128)S(1)} %copy.78.number_ref, bf16[1024,128]{1,0:T(8,128)(2,1)S(1)} %bitcast.67, f32[4,32,128]{2,1,0:T(8,128)S(1)} %bitcast.65), custom_call_target="tpu_custom_call" | custom-call | tf_op jit(solution)/shard_map/arrival/pallas_call | solution.py:339
  23.8 0.1 collective-permute-done.10.rest_3_
  23.9 1.9 %collective-permute-done.11.rest_4_ = bf16[5,64,128]{2,1,0:T(8,128)(2,1)S(1)} collective-permute-done((bf16[5,64,128]{2,1,0:T(8,128)(2,1)S(1)}, bf16[5,64,128]{2,1,0:T(8,128)(2,1)S(1)}, u32[]{:S(2)}, u32[]{:S(2)}) %collective-permute-start.11) | collective-permute-done | bytes 81952 | tf_op jit(solution)/shard_map/ppermute | solution.py:286
  25.8 2.1 %compute.1 = (bf16[14,64,128]{2,1,0:T(8,128)(2,1)S(1)}, bf16[3,64,128]{2,1,0:T(8,128)(2,1)S(1)}, bf16[3,64,128]{2,1,0:T(8,128)(2,1)S(1)}, bf16[3,64,128]{2,1,0:T...) custom-call(s32[36]{0:T(128)S(1)} %get-tuple-element.38.place_ref, ...), custom_call_target="tpu_custom_call" | custom-call | tf_op jit(solution)/shard_map/compute/pallas_call | solution.py:352
  27.9 0.1 reduce_sum.31
  28.1 0.1 slice.76
  28.2 0.1 slice_bitcast_fusion.8
  28.3 0.1 slice_bitcast_fusion.7
  28.3 0.1 copy.90
  28.4 0.1 copy.91
  28.6 0.1 copy.93
  28.7 0.1 copy.94
  28.8 2.6 %collective-permute-start.13 = (bf16[5,64,128]{2,1,0:T(8,128)(2,1)S(1)}, bf16[5,64,128]{2,1,0:T(8,128)(2,1)S(1)}, u32[]{:S(2)}, u32[]{:S(2)}) collective-permute-start(bf16[5,64,128]{2,1,0:T(8,128)(2,1)S(1)} %get-tuple-element.53), channel_id=1, source_target_pairs={{0,12},{4,0},{8,4},{12,8},{1,13},{5,1},{9,5},{13,9},{2,14},{6,2},{... | collective-permute-start | bytes 245768 | tf_op jit(solution)/shard_map/ppermute | solution.py:286
  31.4 0.3 collective-permute-start.14
  31.7 0.3 collective-permute-start.15
  32.0 3.5 %collective-permute-start.17 = (bf16[3,64,128]{2,1,0:T(8,128)(2,1)S(1)}, bf16[3,64,128]{2,1,0:T(8,128)(2,1)S(1)}, u32[]{:S(2)}, u32[]{:S(2)}) collective-permute-start(bf16[3,64,128]{2,1,0:T(8,128)(2,1)S(1)} %get-tuple-element.58), channel_id=1, source_target_pairs={{0,12},{4,0},{8,4},{12,8},{1,13},{5,1},{9,5},{13,9},{2,14},{6,2},{... | collective-permute-start | bytes 147464 | tf_op jit(solution)/shard_map/ppermute | solution.py:286
  35.5 0.8 %collective-permute-start.18 = (bf16[3,64,128]{2,1,0:T(8,128)(2,1)S(1)}, bf16[3,64,128]{2,1,0:T(8,128)(2,1)S(1)}, u32[]{:S(2)}, u32[]{:S(2)}) collective-permute-start(bf16[3,64,128]{2,1,0:T(8,128)(2,1)S(1)} %get-tuple-element.59), channel_id=1, source_target_pairs={{0,8},{4,12},{8,0},{12,4},{1,9},{5,13},{9,1},{13,5},{2,10},{6,14},... | collective-permute-start | bytes 147464 | tf_op jit(solution)/shard_map/ppermute | solution.py:286
  36.3 0.1 select_bitcast_fusion
  36.5 0.7 %add_own.1.start_ref = f32[21,64,128]{2,1,0:T(8,128)S(1)} custom-call(s32[64]{0:T(128)S(1)} %get-tuple-element.37.send_ref, bf16[14,64,128]{2,1,0:T(8,128)(2,1)S(1)} %get-tuple-element.51.own_ref), custom_call_target="tpu_custom_call" | custom-call | tf_op jit(solution)/shard_map/add_own/pallas_call | solution.py:370
  37.1 0.2 collective-permute-start.19
  37.3 3.6 %collective-permute-done.14.rest_1_ = bf16[5,64,128]{2,1,0:T(8,128)(2,1)S(1)} collective-permute-done((bf16[5,64,128]{2,1,0:T(8,128)(2,1)S(1)}, bf16[5,64,128]{2,1,0:T(8,128)(2,1)S(1)}, u32[]{:S(2)}, u32[]{:S(2)}) %collective-permute-start.14) | collective-permute-done | bytes 81952 | tf_op jit(solution)/shard_map/ppermute | solution.py:286
  41.0 0.7 %add_shared.1 = (f32[21,64,128]{2,1,0:T(8,128)S(1)}, bf16[2,64,128]{2,1,0:T(8,128)(2,1)S(1)}) custom-call(s32[64]{0:T(128)S(1)} %get-tuple-element.37.send_ref, f32[21,64,128]{2,1,0:T(8,128)S(1)} %add_own.1.start_ref, bf16[3,6,64,128]{3,2,1,0:T(8,128)(2,1)S(1)} %get-tuple-element.90.spare_ref, bf16[5,64,128]{2,1,0:T(8,128)(2,1)S(1)} %collective-permute-done.13.rest_0_, ...), custom_call_target="tpu_custom_call" | custom-call | tf_op jit(solution)/shard_map/add_shared/pallas_call | solution.py:373
  41.7 0.6 %collective-permute-start.16 = (bf16[2,64,128]{2,1,0:T(8,128)(2,1)S(1)}, bf16[2,64,128]{2,1,0:T(8,128)(2,1)S(1)}, u32[]{:S(2)}, u32[]{:S(2)}) collective-permute-start(bf16[2,64,128]{2,1,0:T(8,128)(2,1)S(1)} %get-tuple-element.57), channel_id=1, source_target_pairs={{0,2},{2,0},{1,3},{3,1},{4,6},{6,4},{5,7},{7,5},{8,10},{10,8},{9,1... | collective-permute-start | bytes 98312 | tf_op jit(solution)/shard_map/ppermute | solution.py:251
  42.3 0.1 fusion
  42.4 0.6 %copy.97 = bf16[1,16,1,2,4,128]{5,4,3,2,1,0:T(4,128)(2,1)} copy(bf16[1,16,1,2,4,128]{5,3,1,4,2,0:T(2,128)(2,1)S(1)} %fusion) | data formatting | bytes 65536
  43.0 0.0 collective-permute-done.19.rest_2_
  43.1 2.6 %collective-permute-done.16.above_ref.below_ref = bf16[2,64,128]{2,1,0:T(8,128)(2,1)S(1)} collective-permute-done((bf16[2,64,128]{2,1,0:T(8,128)(2,1)S(1)}, bf16[2,64,128]{2,1,0:T(8,128)(2,1)S(1)}, u32[]{:S(2)}, u32[]{:S(2)}) %collective-permute-start.16) | collective-permute-done | bytes 32800 | tf_op jit(solution)/shard_map/ppermute | solution.py:251
  45.6 1.7 %finish.1 = f32[1024,128]{1,0:T(8,128)} custom-call(s32[64]{0:T(128)S(1)} %get-tuple-element.37.send_ref, f32[21,64,128]{2,1,0:T(8,128)S(1)} %get-tuple-element.56.start_ref, bf16[2,64,128]{2,1,0:T(8,128)(2,1)S(1)} %collective-permute-done.16.above_ref.below_ref, bf16[2,64,128]{2,1,0:T(8,128)(2,1)S(1)} %collective-permute-done.16.above_ref.below_ref, ...), custom_call_target="tpu_custom_call" | custom-call | tf_op jit(solution)/shard_map/finish/pallas_call | solution.py:382
  (30 shorter events, 0.2 us)
Async XLA Ops:
  0.6 0.9 %copy-start.4 = (s32[1,16,4]{1,2,0:T(4,128)S(1)}, s32[1,16,4]{1,2,0:T(4,128)}, u32[]{:S(2)}) copy-start(s32[1,16,4]{1,2,0:T(4,128)} %param.13) | copy-start | bytes 772
  1.6 1.0 %copy-start = (bf16[16,4,16,128]{3,2,1,0:T(8,128)(2,1)S(1)}, bf16[16,4,16,128]{3,2,1,0:T(8,128)(2,1)}, u32[]{:S(2)}) copy-start(bf16[16,4,16,128]{3,2,1,0:T(8,128)(2,1)} %param.9) | copy-start | bytes 786436
  2.5 10.6 %copy-start.2 = (s32[1,16,4,2,3]{1,3,4,2,0:T(2,128)S(1)}, s32[1,16,4,2,3]{1,3,4,2,0:T(2,128)}, u32[]{:S(2)}) copy-start(s32[1,16,4,2,3]{1,3,4,2,0:T(2,128)} %param.12) | copy-start | bytes 4612
  6.0 8.8 %collective-permute-start.6 = (bf16[2,64,128]{2,1,0:T(8,128)(2,1)S(1)}, bf16[2,64,128]{2,1,0:T(8,128)(2,1)S(1)}, u32[]{:S(2)}, u32[]{:S(2)}) collective-permute-start(bf16[2,64,128]{2,1,0:T(8,128)(2,1)S(1)} %get-tuple-element.42), channel_id=1, source_target_pairs={{0,2},{2,0},{1,3},{3,1},{4,6},{6,4},{5,7},{7,5},{8,10},{10,8},{9,1... | collective-permute-start | bytes 98312 | tf_op jit(solution)/shard_map/ppermute | solution.py:251
  9.0 9.3 %collective-permute-start.7 = (bf16[3,64,128]{2,1,0:T(8,128)(2,1)S(1)}, bf16[3,64,128]{2,1,0:T(8,128)(2,1)S(1)}, u32[]{:S(2)}, u32[]{:S(2)}) collective-permute-start(bf16[3,64,128]{2,1,0:T(8,128)(2,1)S(1)} %get-tuple-element.44), channel_id=1, source_target_pairs={{0,4},{4,8},{8,12},{12,0},{1,5},{5,9},{9,13},{13,1},{2,6},{6,10},{... | collective-permute-start | bytes 147464 | tf_op jit(solution)/shard_map/ppermute | solution.py:286
  10.5 13.3 %collective-permute-start.8 = (bf16[3,64,128]{2,1,0:T(8,128)(2,1)S(1)}, bf16[3,64,128]{2,1,0:T(8,128)(2,1)S(1)}, u32[]{:S(2)}, u32[]{:S(2)}) collective-permute-start(bf16[3,64,128]{2,1,0:T(8,128)(2,1)S(1)} %get-tuple-element.45), channel_id=1, source_target_pairs={{0,8},{4,12},{8,0},{12,4},{1,9},{5,13},{9,1},{13,5},{2,10},{6,14},... | collective-permute-start | bytes 147464 | tf_op jit(solution)/shard_map/ppermute | solution.py:286
  15.4 1.5 %copy-start.3 = (bf16[1,16,1,2,4,128]{5,4,3,2,1,0:T(4,128)(2,1)S(1)}, bf16[1,16,1,2,4,128]{5,4,3,2,1,0:T(4,128)(2,1)}, u32[]{:S(2)}) copy-start(bf16[1,16,1,2,4,128]{5,4,3,2,1,0:T(4,128)(2,1)} %param.11) | copy-start | bytes 98308
  15.4 5.6 %copy-start.1 = (bf16[16,4,16,128]{3,2,1,0:T(8,128)(2,1)S(1)}, bf16[16,4,16,128]{3,2,1,0:T(8,128)(2,1)}, u32[]{:S(2)}) copy-start(bf16[16,4,16,128]{3,2,1,0:T(8,128)(2,1)} %param.10) | copy-start | bytes 786436
  15.4 8.4 %collective-permute-start.9 = (bf16[3,64,128]{2,1,0:T(8,128)(2,1)S(1)}, bf16[3,64,128]{2,1,0:T(8,128)(2,1)S(1)}, u32[]{:S(2)}, u32[]{:S(2)}) collective-permute-start(bf16[3,64,128]{2,1,0:T(8,128)(2,1)S(1)} %get-tuple-element.46), channel_id=1, source_target_pairs={{0,12},{4,0},{8,4},{12,8},{1,13},{5,1},{9,5},{13,9},{2,14},{6,2},{... | collective-permute-start | bytes 147464 | tf_op jit(solution)/shard_map/ppermute | solution.py:286
  17.0 6.9 %collective-permute-start.10 = (bf16[5,64,128]{2,1,0:T(8,128)(2,1)S(1)}, bf16[5,64,128]{2,1,0:T(8,128)(2,1)S(1)}, u32[]{:S(2)}, u32[]{:S(2)}) collective-permute-start(bf16[5,64,128]{2,1,0:T(8,128)(2,1)S(1)} %get-tuple-element.47), channel_id=1, source_target_pairs={{0,4},{4,8},{8,12},{12,0},{1,5},{5,9},{9,13},{13,1},{2,6},{6,10},{... | collective-permute-start | bytes 245768 | tf_op jit(solution)/shard_map/ppermute | solution.py:286
  17.8 8.0 %collective-permute-start.11 = (bf16[5,64,128]{2,1,0:T(8,128)(2,1)S(1)}, bf16[5,64,128]{2,1,0:T(8,128)(2,1)S(1)}, u32[]{:S(2)}, u32[]{:S(2)}) collective-permute-start(bf16[5,64,128]{2,1,0:T(8,128)(2,1)S(1)} %get-tuple-element.48), channel_id=1, source_target_pairs={{0,8},{4,12},{8,0},{12,4},{1,9},{5,13},{9,1},{13,5},{2,10},{6,14},... | collective-permute-start | bytes 245768 | tf_op jit(solution)/shard_map/ppermute | solution.py:286
  18.2 7.6 %collective-permute-start.12 = (bf16[5,64,128]{2,1,0:T(8,128)(2,1)S(1)}, bf16[5,64,128]{2,1,0:T(8,128)(2,1)S(1)}, u32[]{:S(2)}, u32[]{:S(2)}) collective-permute-start(bf16[5,64,128]{2,1,0:T(8,128)(2,1)S(1)} %get-tuple-element.49), channel_id=1, source_target_pairs={{0,12},{4,0},{8,4},{12,8},{1,13},{5,1},{9,5},{13,9},{2,14},{6,2},{... | collective-permute-start | bytes 245768 | tf_op jit(solution)/shard_map/ppermute | solution.py:286
  28.8 8.4 %collective-permute-start.13 = (bf16[5,64,128]{2,1,0:T(8,128)(2,1)S(1)}, bf16[5,64,128]{2,1,0:T(8,128)(2,1)S(1)}, u32[]{:S(2)}, u32[]{:S(2)}) collective-permute-start(bf16[5,64,128]{2,1,0:T(8,128)(2,1)S(1)} %get-tuple-element.53), channel_id=1, source_target_pairs={{0,12},{4,0},{8,4},{12,8},{1,13},{5,1},{9,5},{13,9},{2,14},{6,2},{... | collective-permute-start | bytes 245768 | tf_op jit(solution)/shard_map/ppermute | solution.py:286
  31.4 9.6 %collective-permute-start.14 = (bf16[5,64,128]{2,1,0:T(8,128)(2,1)S(1)}, bf16[5,64,128]{2,1,0:T(8,128)(2,1)S(1)}, u32[]{:S(2)}, u32[]{:S(2)}) collective-permute-start(bf16[5,64,128]{2,1,0:T(8,128)(2,1)S(1)} %get-tuple-element.54), channel_id=1, source_target_pairs={{0,8},{4,12},{8,0},{12,4},{1,9},{5,13},{9,1},{13,5},{2,10},{6,14},... | collective-permute-start | bytes 245768 | tf_op jit(solution)/shard_map/ppermute | solution.py:286
  31.7 9.3 %collective-permute-start.15 = (bf16[5,64,128]{2,1,0:T(8,128)(2,1)S(1)}, bf16[5,64,128]{2,1,0:T(8,128)(2,1)S(1)}, u32[]{:S(2)}, u32[]{:S(2)}) collective-permute-start(bf16[5,64,128]{2,1,0:T(8,128)(2,1)S(1)} %get-tuple-element.55), channel_id=1, source_target_pairs={{0,4},{4,8},{8,12},{12,0},{1,5},{5,9},{9,13},{13,1},{2,6},{6,10},{... | collective-permute-start | bytes 245768 | tf_op jit(solution)/shard_map/ppermute | solution.py:286
  32.0 11.0 %collective-permute-start.17 = (bf16[3,64,128]{2,1,0:T(8,128)(2,1)S(1)}, bf16[3,64,128]{2,1,0:T(8,128)(2,1)S(1)}, u32[]{:S(2)}, u32[]{:S(2)}) collective-permute-start(bf16[3,64,128]{2,1,0:T(8,128)(2,1)S(1)} %get-tuple-element.58), channel_id=1, source_target_pairs={{0,12},{4,0},{8,4},{12,8},{1,13},{5,1},{9,5},{13,9},{2,14},{6,2},{... | collective-permute-start | bytes 147464 | tf_op jit(solution)/shard_map/ppermute | solution.py:286
  35.5 7.5 %collective-permute-start.18 = (bf16[3,64,128]{2,1,0:T(8,128)(2,1)S(1)}, bf16[3,64,128]{2,1,0:T(8,128)(2,1)S(1)}, u32[]{:S(2)}, u32[]{:S(2)}) collective-permute-start(bf16[3,64,128]{2,1,0:T(8,128)(2,1)S(1)} %get-tuple-element.59), channel_id=1, source_target_pairs={{0,8},{4,12},{8,0},{12,4},{1,9},{5,13},{9,1},{13,5},{2,10},{6,14},... | collective-permute-start | bytes 147464 | tf_op jit(solution)/shard_map/ppermute | solution.py:286
  37.1 5.9 %collective-permute-start.19 = (bf16[3,64,128]{2,1,0:T(8,128)(2,1)S(1)}, bf16[3,64,128]{2,1,0:T(8,128)(2,1)S(1)}, u32[]{:S(2)}, u32[]{:S(2)}) collective-permute-start(bf16[3,64,128]{2,1,0:T(8,128)(2,1)S(1)} %get-tuple-element.60), channel_id=1, source_target_pairs={{0,4},{4,8},{8,12},{12,0},{1,5},{5,9},{9,13},{13,1},{2,6},{6,10},{... | collective-permute-start | bytes 147464 | tf_op jit(solution)/shard_map/ppermute | solution.py:286
  41.7 4.0 %collective-permute-start.16 = (bf16[2,64,128]{2,1,0:T(8,128)(2,1)S(1)}, bf16[2,64,128]{2,1,0:T(8,128)(2,1)S(1)}, u32[]{:S(2)}, u32[]{:S(2)}) collective-permute-start(bf16[2,64,128]{2,1,0:T(8,128)(2,1)S(1)} %get-tuple-element.57), channel_id=1, source_target_pairs={{0,2},{2,0},{1,3},{3,1},{4,6},{6,4},{5,7},{7,5},{8,10},{10,8},{9,1... | collective-permute-start | bytes 98312 | tf_op jit(solution)/shard_map/ppermute | solution.py:251

commit v3 on v2

v3 whole, which is shorter than its diff:
```python
import functools

import jax
import jax.numpy as jnp
from jax import lax
from jax.experimental import pallas as pl
from jax.experimental.pallas import tpu as pltpu
from jax.sharding import PartitionSpec as P

HR = 2
CAP = 11
EVEN = 8
EARLY = 4
STRIDE = 32
TRASH = STRIDE - 2
COUNT = STRIDE - 1
PLACES = 16
BF16 = jnp.bfloat16
F32 = jnp.float32
VMEM = pltpu.VMEM
SMEM = pltpu.SMEM


def whole(space):
    return pl.BlockSpec(memory_space=space)


def wrap(value, size):
    return jnp.where(value < 0, value + size, value)


def regions(d, tiles):
    if d == 0:
        return 0, CAP, 0
    early = EARLY if d == tiles // 2 else 0
    shared = EVEN - early
    return early, shared, CAP - shared


def decode(lists_ref, number_ref, r, a, k, rows):
    used = k < number_ref[0, a, r]
    owner = jnp.where(used, lists_ref[0, a, 0, k, r], -1)
    shift = lists_ref[0, a, 1, k, r]
    return owner, HR + shift * rows + lists_ref[0, a, 2, k, r], shift == 0


def serve(lists_ref, number_ref, send_ref, a, d, early, rows, per_row):
    me = lax.axis_index("lon")
    base = d * STRIDE
    near = jnp.int32(0)
    other = jnp.int32(0)
    for r in range(rows):
        for k in range(per_row):
            owner, row, own_band = decode(lists_ref, number_ref, r, a, k, rows)
            hit = owner == me
            ahead = hit & own_band & (near < early)
            slot = jnp.where(ahead, near, early + other)
            send_ref[base + jnp.where(hit, slot, TRASH)] = row
            near = near + jnp.where(ahead, 1, 0)
            other = other + jnp.where(hit, 1, 0) - jnp.where(ahead, 1, 0)
    send_ref[base + COUNT] = other


def prepare_kernel(tiles, bands, per_row, lists_ref, number_ref, fields_ref, *rest):
    rows_ref, send_ref, *rest = rest
    edges = rest[: 1 if bands == 2 else 2]
    held, wide, sems = rest[len(edges) :]
    rows, channels, _ = rows_ref.shape
    me = lax.axis_index("lon")
    dump = rows + 2 * HR
    chunk = 16
    copies = []
    for i, c in enumerate(range(0, channels, chunk)):
        span = pl.ds(c * rows, chunk * rows)
        copies.append(pltpu.make_async_copy(fields_ref.at[span], held.at[span], sems.at[i]))
        copies[-1].start()
    for d in range(1, tiles):
        for s in range(sum(regions(d, tiles))):
            send_ref[d * STRIDE + s] = dump
    if tiles <= 4:
        for d in range(1, tiles):
            early = regions(d, tiles)[0]
            serve(lists_ref, number_ref, send_ref, wrap(me + d - tiles, tiles), d, early, rows, per_row)
    else:

        @pl.loop(1, tiles)
        def _(d):
            early = jnp.where(d == tiles // 2, EARLY, 0)
            serve(lists_ref, number_ref, send_ref, wrap(me + d - tiles, tiles), d, early, rows, per_row)

    for i, c in enumerate(range(0, channels, chunk)):
        copies[i].wait()
        span = slice(c * rows, (c + chunk) * rows)
        wide[span] = held[span].astype(F32)
        for r in range(rows):
            rows_ref[r, c : c + chunk] = wide[pl.ds(c * rows + r, chunk, stride=rows), :].astype(BF16)
    if bands == 2:
        start = jnp.where(lax.axis_index("lat") == 0, rows - HR, 0)
        edges[0][...] = rows_ref[pl.ds(start, HR)]
    else:
        edges[0][...] = rows_ref[0:HR]
        edges[1][...] = rows_ref[rows - HR : rows]


def pack_kernel(tiles, send_ref, rows_ref, before_ref, after_ref, ext_ref, *rest):
    base, spare = rest[: tiles - 1], rest[tiles - 1 :]
    rows = rows_ref.shape[0]
    ext_ref[0:HR] = before_ref[...]
    ext_ref[HR : HR + rows] = rows_ref[...]
    ext_ref[HR + rows : HR + rows + HR] = after_ref[...]
    for d in range(1, tiles):
        for s in range(EVEN):
            base[d - 1][s] = ext_ref[send_ref[d * STRIDE + s]]
    for d in range(1, tiles):
        _, shared, more = regions(d, tiles)

        @pl.when(send_ref[d * STRIDE + COUNT] > shared)
        def _():
            for s in range(more):
                spare[d - 1][s] = ext_ref[send_ref[d * STRIDE + EVEN + s]]


def arrival_kernel(tiles, per_row, lists_ref, number_ref, cot_ref, taps_ref, *rest):
    cot_rows_ref, mix_ref, place_ref, own_ref, wide, near, other = rest
    rows, channels, cols = cot_rows_ref.shape
    me = lax.axis_index("lon")
    entries = rows * per_row
    ext = rows + 2 * HR
    for s in range(CAP):
        own_ref[s] = ext
    serve(lists_ref, number_ref, own_ref, me, 0, 0, rows, per_row)
    for d in range(tiles + 1):
        near[d] = 0
        other[d] = 0

    def place(r):
        for k in range(per_row):
            owner, ext_row, own_band = decode(lists_ref, number_ref, r, me, k, rows)
            used = owner >= 0
            d = jnp.where(used, wrap(me - owner, tiles), tiles)
            early = jnp.where((d == tiles // 2) & (d > 0), EARLY, 0)
            ahead = own_band & (near[d] < early)
            slot = d * PLACES + jnp.where(ahead, near[d], early + other[d])
            source = jnp.where(owner == me, tiles * PLACES + ext_row, slot)
            place_ref[r * per_row + k] = jnp.where(used, source, tiles * PLACES + ext)
            place_ref[entries + r * per_row + k] = jnp.where(used, slot, tiles * PLACES)
            near[d] = near[d] + jnp.where(ahead, 1, 0)
            other[d] = other[d] + jnp.where(ahead, 0, 1)

    pl.loop(0, rows)(place)
    for d in range(tiles):
        place_ref[2 * entries + d] = other[d]

    wide[...] = cot_ref[...].astype(F32)
    for r in range(rows):
        cot_rows_ref[r] = wide[pl.ds(r, channels, stride=rows), :].astype(BF16)
    w0, w1, w2, w3 = (taps_ref[j] for j in range(4))
    cell = lax.broadcasted_iota(jnp.int32, w0.shape, 1)
    first, last, late = cell == 0, cell == cols - 1, cell == cols - 2
    mix_ref[0] = pltpu.roll(jnp.where(first, 0.0, w0), cols - 1, 1)
    mix_ref[1] = w1 + jnp.where(first, w0, 0.0) + jnp.where(last, w2 + w3, 0.0)
    mix_ref[2] = pltpu.roll(jnp.where(last, 0.0, w2) + jnp.where(late, w3, 0.0), 1, 1)
    mix_ref[3] = pltpu.roll(jnp.where(last | late, 0.0, w3), 2, 1)


def compute_kernel(tiles, per_row, place_ref, mix_ref, cot_ref, ext_ref, *rest):
    n = tiles - 1
    base, spare, rest = rest[:n], rest[n : 2 * n], rest[2 * n :]
    own_out, early_out, rest = rest[0], rest[1], rest[2:]
    shared_out, spare_out, (grad_ref, blocks, terms) = rest[:n], rest[n : 2 * n], rest[2 * n :]
    rows, channels, cols = cot_ref.shape
    entries = rows * per_row
    ext = rows + 2 * HR
    part = min(channels, 32)
    blocks[tiles * PLACES : tiles * PLACES + ext] = ext_ref[0:ext]
    blocks[tiles * PLACES + ext] = jnp.zeros((channels, cols), BF16)
    for d in range(1, tiles):
        _, shared, more = regions(d, tiles)
        at = d * PLACES
        blocks[at : at + EVEN] = base[d - 1][...]

        @pl.when(place_ref[2 * entries + d] > shared)
        def _():
            blocks[at + EVEN : at + EVEN + more] = spare[d - 1][...]

    def row(r, _):
        source = [place_ref[r * per_row + k] for k in range(per_row)]
        target = [place_ref[entries + r * per_row + k] for k in range(per_row)]
        mix = [[mix_ref[j, pl.ds(r * per_row + k, 1), :] for j in range(4)] for k in range(per_row)]
        for lo in range(0, channels, part):
            block = [blocks[source[k], lo : lo + part].astype(F32) for k in range(per_row)]
            tap = [sum(block[k] * mix[k][j] for k in range(per_row)) for j in range(4)]
            interp = (tap[1] + pltpu.roll(tap[0], 1, 1)) + (
                pltpu.roll(tap[2], cols - 1, 1) + pltpu.roll(tap[3], cols - 2, 1)
            )
            bent = jnp.tanh(interp)
            scaled = cot_ref[r, lo : lo + part].astype(F32) * (2.0 - bent * bent)
            scaled = scaled.astype(BF16).astype(F32)
            moved = [
                pltpu.roll(scaled, cols - 1, 1),
                scaled,
                pltpu.roll(scaled, 1, 1),
                pltpu.roll(scaled, 2, 1),
            ]
            for k in range(per_row):
                term = (moved[0] * mix[k][0] + moved[1] * mix[k][1]) + (
                    moved[2] * mix[k][2] + moved[3] * mix[k][3]
                )
                terms[target[k], lo : lo + part] = term.astype(BF16)
                for j in range(4):
                    at = (r * per_row + k) * 4 + j
                    product = jnp.sum((block[k] * moved[j]).reshape(part // 8, 8, cols), axis=0)
                    grad_ref[at] = product if lo == 0 else grad_ref[at] + product
        return 0

    lax.fori_loop(0, rows, row, 0, unroll=4)
    for d in range(1, tiles):
        early, shared, more = regions(d, tiles)
        at = d * PLACES
        shared_out[d - 1][...] = terms[at + early : at + EVEN]
        if early:
            early_out[...] = terms[at : at + early]

        @pl.when(place_ref[2 * entries + d] > shared)
        def _():
            spare_out[d - 1][...] = terms[at + EVEN : at + EVEN + more]

    own_out[...] = terms[0:CAP]


def gradient_kernel(partial_ref, out_ref):
    sums = jnp.sum(partial_ref[...], axis=1)
    count, cols = sums.shape
    tap = lax.broadcasted_iota(jnp.int32, sums.shape, 0) & 3
    cell = lax.broadcasted_iota(jnp.int32, sums.shape, 1)
    grads = jnp.where(tap == 0, pltpu.roll(sums, 1, 1), sums)
    grads = jnp.where(tap == 2, pltpu.roll(sums, cols - 1, 1), grads)
    grads = jnp.where(tap == 3, pltpu.roll(sums, cols - 2, 1), grads)
    following = pltpu.roll(grads, count - 1, 0)
    previous = pltpu.roll(grads, 1, 0)
    second = pltpu.roll(grads, 2, 0)
    fixed = jnp.where((tap == 0) & (cell == 0), following, grads)
    fixed = jnp.where((tap == 2) & (cell == cols - 1), previous, fixed)
    fixed = jnp.where((tap == 3) & (cell == cols - 2), previous, fixed)
    fixed = jnp.where((tap == 3) & (cell == cols - 1), second, fixed)
    out_ref[...] = fixed.astype(BF16)


def add_own_kernel(table_ref, own_ref, total_ref):
    total_ref[...] = jnp.zeros_like(total_ref)
    for s in range(CAP):
        at = table_ref[s]
        total_ref[at] = total_ref[at] + own_ref[s].astype(F32)


def add_shared_kernel(tiles, bands, send_ref, _, *rest):
    shared, spare, (total_ref, *edges) = rest[: tiles - 1], rest[tiles - 1 : 2 * tiles - 2], rest[2 * tiles - 2 :]
    ext = total_ref.shape[0] - 1
    for d in range(1, tiles):
        early, count, more = regions(d, tiles)
        for s in range(count):
            at = send_ref[d * STRIDE + early + s]
            total_ref[at] = total_ref[at] + shared[d - 1][s].astype(F32)

        @pl.when(send_ref[d * STRIDE + COUNT] > count)
        def _():
            for s in range(more):
                at = send_ref[d * STRIDE + EVEN + s]
                total_ref[at] = total_ref[at] + spare[d - 1][s].astype(F32)

    if bands == 2:
        start = jnp.where(lax.axis_index("lat") == 0, ext - HR, 0)
        edges[0][...] = total_ref[pl.ds(start, HR)].astype(BF16)
    else:
        edges[0][...] = total_ref[0:HR].astype(BF16)
        edges[1][...] = total_ref[ext - HR : ext].astype(BF16)


def finish_kernel(tiles, bands, rows, send_ref, _, early_ref, above_ref, below_ref, out_ref, total_ref):
    channels = total_ref.shape[1]
    d = tiles // 2
    for s in range(EARLY):
        at = send_ref[d * STRIDE + s]
        total_ref[at] = total_ref[at] + early_ref[s].astype(F32)
    band = lax.axis_index("lat")
    for r in range(rows):
        value = total_ref[HR + r]
        if r < HR:
            value = value + jnp.where(band > 0, above_ref[r].astype(F32), 0.0)
        if r >= rows - HR:
            value = value + jnp.where(band < bands - 1, below_ref[r - rows + HR].astype(F32), 0.0)
        out_ref[pl.ds(r, channels, stride=rows), :] = value


def swap_lat(edges, bands):
    if bands == 2:
        got = lax.ppermute(edges[0], "lat", [(0, 1), (1, 0)])
        return got, got
    down = [(i, i + 1) for i in range(bands - 1)]
    up = [(i + 1, i) for i in range(bands - 1)]
    return lax.ppermute(edges[1], "lat", down), lax.ppermute(edges[0], "lat", up)


def local(fields, arrival_cot, weights, departures, counts):
    lev_dev, field_count, rows, cols = fields.shape
    channels = lev_dev * field_count
    tiles = lax.axis_size("lon")
    bands = lax.axis_size("lat")
    per_row, taps = weights.shape[3], weights.shape[4]
    entries = rows * per_row
    ext = rows + 2 * HR
    partners = tiles - 1
    middle = tiles // 2
    params = pltpu.CompilerParams(vmem_limit_bytes=48 * 1024 * 1024)

    def call(kernel, out_shape, in_specs, out_specs, scratch=(), name=None, aliases={}):
        return pl.pallas_call(
            kernel,
            out_shape=out_shape,
            in_specs=in_specs,
            out_specs=out_specs,
            scratch_shapes=list(scratch),
            compiler_params=params,
            input_output_aliases=aliases,
            name=name,
        )

    def array(*shape, dtype=BF16):
        return jax.ShapeDtypeStruct(shape, dtype)

    def move(part, d):
        return lax.ppermute(part, "lon", [(i, (i + d) % tiles) for i in range(tiles)])

    def move_all(parts, sign):
        out = [None] * partners
        for d in [middle] + [d for d in range(1, tiles) if d != middle]:
            out[d - 1] = move(parts[d - 1], sign * d)
        return out

    def move_spare(needed, parts, sign):
        return lax.cond(needed, lambda parts: move_all(parts, sign), lambda parts: parts, list(parts))

    lists = jnp.transpose(departures, (0, 2, 4, 3, 1))
    number = jnp.transpose(counts, (0, 2, 1))

    edge = (array(HR, channels, cols),) * (1 if bands == 2 else 2)
    base_slots = (array(EVEN, channels, cols),) * partners
    shared_slots = tuple(array(regions(d, tiles)[1], channels, cols) for d in range(1, tiles))
    spare_slots = tuple(array(regions(d, tiles)[2], channels, cols) for d in range(1, tiles))

    row_blocks, send_rows, *edges = call(
        functools.partial(prepare_kernel, tiles, bands, per_row),
        (array(rows, channels, cols), array(tiles * STRIDE, dtype=jnp.int32)) + edge,
        [whole(SMEM), whole(SMEM), whole(pl.ANY)],
        (whole(VMEM), whole(SMEM)) + (whole(VMEM),) * len(edge),
        [
            VMEM((channels * rows, cols), BF16),
            VMEM((channels * rows, cols), F32),
            pltpu.SemaphoreType.DMA((channels // 16,)),
        ],
        "prepare",
    )(lists, number, fields.reshape(channels * rows, cols))
    before, after = swap_lat(edges, bands)

    ext_blocks, *rest = call(
        functools.partial(pack_kernel, tiles),
        (array(ext + 1, channels, cols),) + base_slots + spare_slots,
        [whole(SMEM)] + [whole(VMEM)] * 3,
        (whole(VMEM),) * (1 + 2 * partners),
        (),
        "pack",
    )(send_rows, row_blocks, before, after)
    base = move_all(rest[:partners], 1)

    tile = jnp.arange(tiles, dtype=jnp.int32)
    entry = jnp.arange(per_row, dtype=jnp.int32)
    named = (entry[:, None] < number[0][:, None, :]) & (lists[0, :, 0] == tile[:, None, None, None])
    own_band = lists[0, :, 1] == 0
    near = jnp.sum(jnp.where(named & own_band, 1, 0), axis=(2, 3))
    far = jnp.sum(jnp.where(named & ~own_band, 1, 0), axis=(2, 3))
    distance = (tile[None, :] - tile[:, None]) % tiles
    early = jnp.where(distance == middle, EARLY, 0)
    needed = jnp.any((far + jnp.maximum(near - early, 0) > EVEN - early) & (distance > 0))
    spare = move_spare(needed, rest[partners:], 1)

    mixing = weights.reshape(rows, per_row, taps, cols).astype(F32)
    mixing = jnp.transpose(mixing, (2, 0, 1, 3)).reshape(taps, entries, cols)
    cot_rows, mix, places, own_table = call(
        functools.partial(arrival_kernel, tiles, per_row),
        (
            array(rows, channels, cols),
            array(taps, entries, cols, dtype=F32),
            array(2 * entries + tiles, dtype=jnp.int32),
            array(STRIDE, dtype=jnp.int32),
        ),
        [whole(SMEM), whole(SMEM), whole(VMEM), whole(VMEM)],
        (whole(VMEM), whole(VMEM), whole(SMEM), whole(SMEM)),
        [VMEM((channels * rows, cols), F32)] + [SMEM((tiles + 1,), jnp.int32)] * 2,
        "arrival",
    )(lists, number, arrival_cot.reshape(channels * rows, cols), mixing)

    own, early, *rest = call(
        functools.partial(compute_kernel, tiles, per_row),
        (array(CAP, channels, cols), array(EARLY, channels, cols))
        + shared_slots
        + spare_slots
        + (array(entries * taps, 8, cols, dtype=F32),),
        [whole(SMEM)] + [whole(VMEM)] * (3 + 2 * partners),
        (whole(VMEM),) * (3 + 2 * partners),
        [
            VMEM((tiles * PLACES + ext + 1, channels, cols), BF16),
            VMEM((tiles * PLACES + 1, channels, cols), BF16),
        ],
        "compute",
    )(places, mix, cot_rows, ext_blocks, *base, *spare)
    grads = rest[-1]
    shared = move_all(rest[:partners], -1)
    early = move(early, -middle)
    spare = move_spare(needed, rest[partners : 2 * partners], -1)

    sums = array(ext + 1, channels, cols, dtype=F32)
    total = call(add_own_kernel, sums, [whole(SMEM), whole(VMEM)], whole(VMEM), (), "add_own")(
        own_table, own
    )
    total, *edges = call(
        functools.partial(add_shared_kernel, tiles, bands),
        (sums,) + edge,
        [whole(SMEM)] + [whole(VMEM)] * (1 + 2 * partners),
        (whole(VMEM),) * (1 + len(edge)),
        (),
        "add_shared",
        {1: 0},
    )(send_rows, total, *shared, *spare)
    from_above, from_below = swap_lat(edges, bands)
    source, _ = call(
        functools.partial(finish_kernel, tiles, bands, rows),
        (array(channels * rows, cols, dtype=F32), sums),
        [whole(SMEM)] + [whole(VMEM)] * 4,
        (whole(VMEM),) * 2,
        (),
        "finish",
        {1: 1},
    )(send_rows, total, early, from_above, from_below)

    grads, _ = lax.optimization_barrier((grads, edges[0]))
    weight_grad = call(
        gradient_kernel,
        array(entries * taps, cols),
        [whole(VMEM)],
        whole(VMEM),
        (),
        "gradient",
    )(grads)
    return source.reshape(fields.shape), weight_grad.reshape(weights.shape)


def solution(mesh):
    return jax.shard_map(
        local,
        mesh=mesh,
        in_specs=(
            P("lev", "ens", "lat", "lon"),
            P("lev", "ens", "lat", "lon"),
            P("lev", "lat", "lon", "ens", None, None),
            P("lev", "lat", None, "ens", None),
            P("lev", "lat", "ens"),
        ),
        out_specs=(P("lev", "ens", "lat", "lon"), P("lev", "lat", "lon", "ens", None, None)),
        check_vma=False,
    )
```

time: 47.6 us -> 47.8 us (level)
  waiting for transfers between devices: 8.26 us -> 13.3 us
  starting transfers between devices: 20.8 us -> 17.8 us
  Pallas kernels: 12 us -> 11.1 us
    ppermute x12 -> x7, waiting for transfers between devices: 5.69 us -> 11.4 us  [move(): lax.ppermute(part, 'lon', [(i, (i + d) % tiles) for i in range(tiles)])]
    ppermute x12 -> x7, starting transfers between devices: 17.2 us -> 13.3 us  [move(): lax.ppermute(part, 'lon', [(i, (i + d) % tiles) for i in range(tiles)])]
    ppermute x2, starting transfers between devices: 3.64 us -> 4.52 us  [swap_lat(): got = lax.ppermute(edges[0], 'lat', [(0, 1), (1, 0)])]
    pallas_call x1, Pallas kernels: 3.42 us -> 2.55 us  [local(): call(functools.partial(prepare_kernel, tiles, bands, per_row), (array(row...]
    pallas_call x3 -> x4, Pallas kernels: 4.37 us -> 5.14 us  [the longest x1 2.07 us: local(): call(functools.partial(compute_kernel, tiles, per_row), (array(CAP, chann...]
    pallas_call x1, Pallas kernels: 2.82 us -> 2.16 us  [local(): call(functools.partial(arrival_kernel, tiles, per_row), (array(rows, chan...]
    ppermute x2, waiting for transfers between devices: 2.57 us -> 1.92 us  [swap_lat(): got = lax.ppermute(edges[0], 'lat', [(0, 1), (1, 0)])]
    unnamed x14 -> x12, local copies, waits for them, and re-layouts: 2.53 us -> 2.99 us
  transfers between devices with their start and end apart: 14 -> 9, of which waited for: 4 -> 5; matrix products, arithmetic and copies ran while one was open for 4% -> 2% of each run, Pallas kernels for 10% -> 9%
where the time goes in v3:
time: 47.8 us; the launch traced here: 47.6 us
  starting transfers between devices  17.8 us (37%)
  waiting for transfers between devices  13.3 us (28%)
  Pallas kernels  11.1 us (23%)
  local copies, waits for them, and re-layouts  3.03 us (6%)
  between operations  1.4 us (3%)
  other arithmetic  0.91 us (2%)
    ppermute x7, starting transfers between devices, move(): lax.ppermute(part, 'lon', [(i, (i + d) % tiles) for i in range(tiles)])  13.3 us
    ppermute x7, waiting for transfers between devices, move(): lax.ppermute(part, 'lon', [(i, (i + d) % tiles) for i in range(tiles)])  11.4 us
    ppermute x2, starting transfers between devices, swap_lat(): got = lax.ppermute(edges[0], 'lat', [(0, 1), (1, 0)])  4.52 us
    unnamed x12, local copies, waits for them, and re-layouts  2.99 us
    pallas_call x1, Pallas kernels, local(): call(functools.partial(prepare_kernel, tiles, bands, per_row), (array(row...  2.55 us
    pallas_call x1, Pallas kernels, local(): call(functools.partial(arrival_kernel, tiles, per_row), (array(rows, chan...  2.16 us
    pallas_call x1, Pallas kernels, local(): call(functools.partial(compute_kernel, tiles, per_row), (array(CAP, chann...  2.07 us
    ppermute x2, waiting for transfers between devices, swap_lat(): got = lax.ppermute(edges[0], 'lat', [(0, 1), (1, 0)])  1.92 us
  transfers between devices with their start and end apart: 9, of which 5 were waited for; matrix products, arithmetic and copies ran while one was open for 2% of the time, Pallas kernels for 9%

profile of v3, /device:TPU:0, one launch (start us, length us, event | category | flops | bytes accessed | tf_op | source)
XLA Modules:
  0.0 47.6 jit_solution(3262984442164831468)
XLA Ops:
  0.6 0.0 copy-start.4
  0.6 0.7 %copy-done.4 = s32[1,16,4]{1,2,0:T(4,128)S(1)} copy-done((s32[1,16,4]{1,2,0:T(4,128)S(1)}, s32[1,16,4]{1,2,0:T(4,128)}, u32[]{:S(2)}) %copy-start.4) | copy-done | bytes 280
  1.3 0.0 copy-start
  1.3 0.9 %copy-done = bf16[16,4,16,128]{3,2,1,0:T(8,128)(2,1)S(1)} copy-done((bf16[16,4,16,128]{3,2,1,0:T(8,128)(2,1)S(1)}, bf16[16,4,16,128]{3,2,1,0:T(8,128)(2,1)}, u32[]{:S(2)}) %copy-start) | copy-done | bytes 262168
  2.3 0.0 copy-start.2
  2.3 0.7 %copy-done.2 = s32[1,16,4,2,3]{1,3,4,2,0:T(2,128)S(1)} copy-done((s32[1,16,4,2,3]{1,3,4,2,0:T(2,128)S(1)}, s32[1,16,4,2,3]{1,3,4,2,0:T(2,128)}, u32[]{:S(2)}) %copy-start.2) | copy-done | bytes 1560
  3.0 2.6 %prepare.1 = (bf16[16,64,128]{2,1,0:T(8,128)(2,1)S(1)}, s32[128]{0:T(128)S(1)}, bf16[2,64,128]{2,1,0:T(8,128)(2,1)S(1)}) custom-call(s32[1,4,3,2,16]{4,3,2,1,0:T(2,128)S(1)} %bitcast.24, s32[1,4,16]{2,1,0:T(4,128)S(1)} %bitcast.28, bf16[1024,128]{1,0:T(8,128)(2,1)S(1)} %bitcast.21), custom_call_target="tpu_custom_call" | custom-call | tf_op jit(solution)/shard_map/prepare/pallas_call | solution.py:351
  5.5 3.0 %collective-permute-start.6 = (bf16[2,64,128]{2,1,0:T(8,128)(2,1)S(1)}, bf16[2,64,128]{2,1,0:T(8,128)(2,1)S(1)}, u32[]{:S(2)}, u32[]{:S(2)}) collective-permute-start(bf16[2,64,128]{2,1,0:T(8,128)(2,1)S(1)} %get-tuple-element.71), channel_id=1, source_target_pairs={{0,2},{2,0},{1,3},{3,1},{4,6},{6,4},{5,7},{7,5},{8,10},{10,8},{9,1... | collective-permute-start | bytes 98312 | tf_op jit(solution)/shard_map/ppermute | solution.py:297
  8.6 0.2 select_reduce_fusion
  8.8 0.7 %and_reduce_fusion = pred[]{:T(512)} fusion(s32[4,4]{1,0:T(4,128)S(1)} %get-tuple-element.105, s32[4,4]{1,0:T(4,128)S(1)} %get-tuple-element.104), kind=kLoop, calls=%fused_computation.18 | loop fusion | flops 351 | bytes 129 | tf_op jit(solution)/shard_map/reduce_or | solution.py:383
  10.1 0.3 collective-permute-done.6.before_ref.after_ref
  10.4 0.6 %pack.1 = (bf16[21,64,128]{2,1,0:T(8,128)(2,1)S(1)}, bf16[8,64,128]{2,1,0:T(8,128)(2,1)S(1)}, bf16[8,64,128]{2,1,0:T(8,128)(2,1)S(1)}, bf16[8,64,128]{2,1,0:T(8,...) custom-call(s32[128]{0:T(128)S(1)} %get-tuple-element.65.send_ref, ...), custom_call_target="tpu_custom_call" | custom-call | tf_op jit(solution)/shard_map/pack/pallas_call | solution.py:365
  11.0 2.2 %collective-permute-start.7 = (bf16[8,64,128]{2,1,0:T(8,128)(2,1)S(1)}, bf16[8,64,128]{2,1,0:T(8,128)(2,1)S(1)}, u32[]{:S(2)}, u32[]{:S(2)}) collective-permute-start(bf16[8,64,128]{2,1,0:T(8,128)(2,1)S(1)} %get-tuple-element.73), channel_id=1, source_target_pairs={{0,4},{4,8},{8,12},{12,0},{1,5},{5,9},{9,13},{13,1},{2,6},{6,10},{... | collective-permute-start | bytes 393224 | tf_op jit(solution)/shard_map/ppermute | solution.py:332
  13.2 2.6 %collective-permute-start.8 = (bf16[8,64,128]{2,1,0:T(8,128)(2,1)S(1)}, bf16[8,64,128]{2,1,0:T(8,128)(2,1)S(1)}, u32[]{:S(2)}, u32[]{:S(2)}) collective-permute-start(bf16[8,64,128]{2,1,0:T(8,128)(2,1)S(1)} %get-tuple-element.74), channel_id=1, source_target_pairs={{0,8},{4,12},{8,0},{12,4},{1,9},{5,13},{9,1},{13,5},{2,10},{6,14},... | collective-permute-start | bytes 393224 | tf_op jit(solution)/shard_map/ppermute | solution.py:332
  15.8 0.0 copy-start.5
  15.8 0.0 copy-start.1
  15.8 1.3 %collective-permute-start.9 = (bf16[8,64,128]{2,1,0:T(8,128)(2,1)S(1)}, bf16[8,64,128]{2,1,0:T(8,128)(2,1)S(1)}, u32[]{:S(2)}, u32[]{:S(2)}) collective-permute-start(bf16[8,64,128]{2,1,0:T(8,128)(2,1)S(1)} %get-tuple-element.75), channel_id=1, source_target_pairs={{0,12},{4,0},{8,4},{12,8},{1,13},{5,1},{9,5},{13,9},{2,14},{6,2},{... | collective-permute-start | bytes 393224 | tf_op jit(solution)/shard_map/ppermute | solution.py:332
  17.1 0.0 copy-done.5
  17.2 0.0 copy-start.3
  17.2 0.0 copy-done.1
  17.2 0.6 %copy-done.3 = s32[1,16,4,2,3]{1,3,4,2,0:T(2,128)S(1)} copy-done((s32[1,16,4,2,3]{1,3,4,2,0:T(2,128)S(1)}, s32[1,16,4,2,3]{1,3,4,2,0:T(2,128)}, u32[]{:S(2)}) %copy-start.3) | copy-done | bytes 1560
  17.9 2.2 %arrival.1 = (bf16[16,64,128]{2,1,0:T(8,128)(2,1)S(1)}, f32[4,32,128]{2,1,0:T(8,128)S(1)}, s32[68]{0:T(128)S(1)}, s32[32]{0:T(128)S(1)}) custom-call(s32[1,4,3,2,16]{4,3,2,1,0:T(2,128)S(1)} %bitcast.27, s32[1,4,16]{2,1,0:T(4,128)S(1)} %bitcast.30, bf16[1024,128]{1,0:T(8,128)(2,1)S(1)} %bitcast.22, f32[4,32,128]{2,1,0:T(8,128)S(1)} %bitcast.23), custom_call_target="tpu_custom_call" | custom-call | tf_op jit(solution)/shard_map/arrival/pallas_call | solution.py:388
  20.0 0.0 collective-permute-done.7.rest_0_
  20.0 3.4 %collective-permute-done.8.rest_1_ = bf16[8,64,128]{2,1,0:T(8,128)(2,1)S(1)} collective-permute-done((bf16[8,64,128]{2,1,0:T(8,128)(2,1)S(1)}, bf16[8,64,128]{2,1,0:T(8,128)(2,1)S(1)}, u32[]{:S(2)}, u32[]{:S(2)}) %collective-permute-start.8) | collective-permute-done | bytes 131104 | tf_op jit(solution)/shard_map/ppermute | solution.py:332
  23.4 0.1 collective-permute-done.9.rest_2_
  23.5 2.1 %compute.1 = (bf16[11,64,128]{2,1,0:T(8,128)(2,1)S(1)}, bf16[4,64,128]{2,1,0:T(8,128)(2,1)S(1)}, bf16[8,64,128]{2,1,0:T(8,128)(2,1)S(1)}, bf16[4,64,128]{2,1,0:T...) custom-call(s32[68]{0:T(128)S(1)} %get-tuple-element.67.place_ref, ...), custom_call_target="tpu_custom_call" | custom-call | tf_op jit(solution)/shard_map/compute/pallas_call | solution.py:402
  25.6 4.2 %collective-permute-start.10 = (bf16[8,64,128]{2,1,0:T(8,128)(2,1)S(1)}, bf16[8,64,128]{2,1,0:T(8,128)(2,1)S(1)}, u32[]{:S(2)}, u32[]{:S(2)}) collective-permute-start(bf16[8,64,128]{2,1,0:T(8,128)(2,1)S(1)} %get-tuple-element.83), channel_id=1, source_target_pairs={{0,12},{4,0},{8,4},{12,8},{1,13},{5,1},{9,5},{13,9},{2,14},{6,2},{... | collective-permute-start | bytes 393224 | tf_op jit(solution)/shard_map/ppermute | solution.py:332
  29.8 0.0 collective-permute-start.12
  29.8 0.6 %collective-permute-start.11 = (bf16[4,64,128]{2,1,0:T(8,128)(2,1)S(1)}, bf16[4,64,128]{2,1,0:T(8,128)(2,1)S(1)}, u32[]{:S(2)}, u32[]{:S(2)}) collective-permute-start(bf16[4,64,128]{2,1,0:T(8,128)(2,1)S(1)} %get-tuple-element.84), channel_id=1, source_target_pairs={{0,8},{4,12},{8,0},{12,4},{1,9},{5,13},{9,1},{13,5},{2,10},{6,14},... | collective-permute-start | bytes 196616 | tf_op jit(solution)/shard_map/ppermute | solution.py:332
  30.4 2.3 %collective-permute-start.13 = (bf16[4,64,128]{2,1,0:T(8,128)(2,1)S(1)}, bf16[4,64,128]{2,1,0:T(8,128)(2,1)S(1)}, u32[]{:S(2)}, u32[]{:S(2)}) collective-permute-start(bf16[4,64,128]{2,1,0:T(8,128)(2,1)S(1)} %get-tuple-element.93), channel_id=1, source_target_pairs={{0,8},{4,12},{8,0},{12,4},{1,9},{5,13},{9,1},{13,5},{2,10},{6,14},... | collective-permute-start | bytes 196616 | tf_op jit(solution)/shard_map/ppermute | solution.py:332
  32.7 0.6 %add_own.1._ = f32[21,64,128]{2,1,0:T(8,128)S(1)} custom-call(s32[32]{0:T(128)S(1)} %get-tuple-element.66.table_ref, bf16[11,64,128]{2,1,0:T(8,128)(2,1)S(1)} %get-tuple-element.82.own_ref), custom_call_target="tpu_custom_call" | custom-call | tf_op jit(solution)/shard_map/add_own/pallas_call | solution.py:422
  33.4 7.9 %collective-permute-done.11.rest_1_ = bf16[4,64,128]{2,1,0:T(8,128)(2,1)S(1)} collective-permute-done((bf16[4,64,128]{2,1,0:T(8,128)(2,1)S(1)}, bf16[4,64,128]{2,1,0:T(8,128)(2,1)S(1)}, u32[]{:S(2)}, u32[]{:S(2)}) %collective-permute-start.11) | collective-permute-done | bytes 65568 | tf_op jit(solution)/shard_map/ppermute | solution.py:332
  41.3 0.0 collective-permute-done.10.rest_0_
  41.3 0.0 collective-permute-done.12.rest_2_
  41.3 0.7 %add_shared.1 = (f32[21,64,128]{2,1,0:T(8,128)S(1)}, bf16[2,64,128]{2,1,0:T(8,128)(2,1)S(1)}) custom-call(s32[128]{0:T(128)S(1)} %get-tuple-element.65.send_ref, f32[21,64,128]{2,1,0:T(8,128)S(1)} %add_own.1._, bf16[8,64,128]{2,1,0:T(8,128)(2,1)S(1)} %collective-permute-done.10.rest_0_, ...), custom_call_target="tpu_custom_call", output_to_operand_aliasing={{0}: (1, {})} | custom-call | tf_op jit(solution)/shard_map/add_shared/pallas_call | solution.py:425
  42.0 1.5 %collective-permute-start.14 = (bf16[2,64,128]{2,1,0:T(8,128)(2,1)S(1)}, bf16[2,64,128]{2,1,0:T(8,128)(2,1)S(1)}, u32[]{:S(2)}, u32[]{:S(2)}) collective-permute-start(bf16[2,64,128]{2,1,0:T(8,128)(2,1)S(1)} %get-tuple-element.94), channel_id=1, source_target_pairs={{0,2},{2,0},{1,3},{3,1},{4,6},{6,4},{5,7},{7,5},{8,10},{10,8},{9,1... | collective-permute-start | bytes 98312 | tf_op jit(solution)/shard_map/ppermute | solution.py:297
  43.5 0.9 %gradient.1 = bf16[128,128]{1,0:T(8,128)(2,1)} custom-call(f32[128,8,128]{2,1,0:T(8,128)S(1)} %get-tuple-element.97.partial_ref), custom_call_target="tpu_custom_call" | custom-call | tf_op jit(solution)/shard_map/gradient/pallas_call | solution.py:446
  44.3 0.0 collective-permute-done.13.early_ref
  44.3 1.6 %collective-permute-done.14.above_ref.below_ref = bf16[2,64,128]{2,1,0:T(8,128)(2,1)S(1)} collective-permute-done((bf16[2,64,128]{2,1,0:T(8,128)(2,1)S(1)}, bf16[2,64,128]{2,1,0:T(8,128)(2,1)S(1)}, u32[]{:S(2)}, u32[]{:S(2)}) %collective-permute-start.14) | collective-permute-done | bytes 32800 | tf_op jit(solution)/shard_map/ppermute | solution.py:297
  45.9 1.6 %finish.1 = (f32[1024,128]{1,0:T(8,128)}, f32[21,64,128]{2,1,0:T(8,128)S(1)}) custom-call(s32[128]{0:T(128)S(1)} %get-tuple-element.65.send_ref, f32[21,64,128]{2,1,0:T(8,128)S(1)} %get-tuple-element.92._, bf16[4,64,128]{2,1,0:T(8,128)(2,1)S(1)} %collective-permute-done.13.early_ref, ...), custom_call_target="tpu_custom_call", output_to_operand_aliasing={{1}: (1, {})} | custom-call | tf_op jit(solution)/shard_map/finish/pallas_call | solution.py:435
  (8 shorter events, 0.1 us)
Async XLA Ops:
  0.6 0.7 %copy-start.4 = (s32[1,16,4]{1,2,0:T(4,128)S(1)}, s32[1,16,4]{1,2,0:T(4,128)}, u32[]{:S(2)}) copy-start(s32[1,16,4]{1,2,0:T(4,128)} %param.13) | copy-start | bytes 772
  1.3 0.9 %copy-start = (bf16[16,4,16,128]{3,2,1,0:T(8,128)(2,1)S(1)}, bf16[16,4,16,128]{3,2,1,0:T(8,128)(2,1)}, u32[]{:S(2)}) copy-start(bf16[16,4,16,128]{3,2,1,0:T(8,128)(2,1)} %param.9) | copy-start | bytes 786436
  2.3 0.7 %copy-start.2 = (s32[1,16,4,2,3]{1,3,4,2,0:T(2,128)S(1)}, s32[1,16,4,2,3]{1,3,4,2,0:T(2,128)}, u32[]{:S(2)}) copy-start(s32[1,16,4,2,3]{1,3,4,2,0:T(2,128)} %param.12) | copy-start | bytes 4612
  5.5 4.9 %collective-permute-start.6 = (bf16[2,64,128]{2,1,0:T(8,128)(2,1)S(1)}, bf16[2,64,128]{2,1,0:T(8,128)(2,1)S(1)}, u32[]{:S(2)}, u32[]{:S(2)}) collective-permute-start(bf16[2,64,128]{2,1,0:T(8,128)(2,1)S(1)} %get-tuple-element.71), channel_id=1, source_target_pairs={{0,2},{2,0},{1,3},{3,1},{4,6},{6,4},{5,7},{7,5},{8,10},{10,8},{9,1... | collective-permute-start | bytes 98312 | tf_op jit(solution)/shard_map/ppermute | solution.py:297
  11.0 9.0 %collective-permute-start.7 = (bf16[8,64,128]{2,1,0:T(8,128)(2,1)S(1)}, bf16[8,64,128]{2,1,0:T(8,128)(2,1)S(1)}, u32[]{:S(2)}, u32[]{:S(2)}) collective-permute-start(bf16[8,64,128]{2,1,0:T(8,128)(2,1)S(1)} %get-tuple-element.73), channel_id=1, source_target_pairs={{0,4},{4,8},{8,12},{12,0},{1,5},{5,9},{9,13},{13,1},{2,6},{6,10},{... | collective-permute-start | bytes 393224 | tf_op jit(solution)/shard_map/ppermute | solution.py:332
  13.2 10.2 %collective-permute-start.8 = (bf16[8,64,128]{2,1,0:T(8,128)(2,1)S(1)}, bf16[8,64,128]{2,1,0:T(8,128)(2,1)S(1)}, u32[]{:S(2)}, u32[]{:S(2)}) collective-permute-start(bf16[8,64,128]{2,1,0:T(8,128)(2,1)S(1)} %get-tuple-element.74), channel_id=1, source_target_pairs={{0,8},{4,12},{8,0},{12,4},{1,9},{5,13},{9,1},{13,5},{2,10},{6,14},... | collective-permute-start | bytes 393224 | tf_op jit(solution)/shard_map/ppermute | solution.py:332
  15.8 1.4 %copy-start.5 = (bf16[1,16,1,2,4,128]{5,4,3,2,1,0:T(4,128)(2,1)S(1)}, bf16[1,16,1,2,4,128]{5,4,3,2,1,0:T(4,128)(2,1)}, u32[]{:S(2)}) copy-start(bf16[1,16,1,2,4,128]{5,4,3,2,1,0:T(4,128)(2,1)} %param.11) | copy-start | bytes 98308
  15.8 1.4 %copy-start.1 = (bf16[16,4,16,128]{3,2,1,0:T(8,128)(2,1)S(1)}, bf16[16,4,16,128]{3,2,1,0:T(8,128)(2,1)}, u32[]{:S(2)}) copy-start(bf16[16,4,16,128]{3,2,1,0:T(8,128)(2,1)} %param.10) | copy-start | bytes 786436
  15.8 7.7 %collective-permute-start.9 = (bf16[8,64,128]{2,1,0:T(8,128)(2,1)S(1)}, bf16[8,64,128]{2,1,0:T(8,128)(2,1)S(1)}, u32[]{:S(2)}, u32[]{:S(2)}) collective-permute-start(bf16[8,64,128]{2,1,0:T(8,128)(2,1)S(1)} %get-tuple-element.75), channel_id=1, source_target_pairs={{0,12},{4,0},{8,4},{12,8},{1,13},{5,1},{9,5},{13,9},{2,14},{6,2},{... | collective-permute-start | bytes 393224 | tf_op jit(solution)/shard_map/ppermute | solution.py:332
  17.2 0.7 %copy-start.3 = (s32[1,16,4,2,3]{1,3,4,2,0:T(2,128)S(1)}, s32[1,16,4,2,3]{1,3,4,2,0:T(2,128)}, u32[]{:S(2)}) copy-start(s32[1,16,4,2,3]{1,3,4,2,0:T(2,128)} %param.12) | copy-start | bytes 4612
  25.6 15.7 %collective-permute-start.10 = (bf16[8,64,128]{2,1,0:T(8,128)(2,1)S(1)}, bf16[8,64,128]{2,1,0:T(8,128)(2,1)S(1)}, u32[]{:S(2)}, u32[]{:S(2)}) collective-permute-start(bf16[8,64,128]{2,1,0:T(8,128)(2,1)S(1)} %get-tuple-element.83), channel_id=1, source_target_pairs={{0,12},{4,0},{8,4},{12,8},{1,13},{5,1},{9,5},{13,9},{2,14},{6,2},{... | collective-permute-start | bytes 393224 | tf_op jit(solution)/shard_map/ppermute | solution.py:332
  29.8 11.5 %collective-permute-start.12 = (bf16[8,64,128]{2,1,0:T(8,128)(2,1)S(1)}, bf16[8,64,128]{2,1,0:T(8,128)(2,1)S(1)}, u32[]{:S(2)}, u32[]{:S(2)}) collective-permute-start(bf16[8,64,128]{2,1,0:T(8,128)(2,1)S(1)} %get-tuple-element.85), channel_id=1, source_target_pairs={{0,4},{4,8},{8,12},{12,0},{1,5},{5,9},{9,13},{13,1},{2,6},{6,10},{... | collective-permute-start | bytes 393224 | tf_op jit(solution)/shard_map/ppermute | solution.py:332
  29.8 11.5 %collective-permute-start.11 = (bf16[4,64,128]{2,1,0:T(8,128)(2,1)S(1)}, bf16[4,64,128]{2,1,0:T(8,128)(2,1)S(1)}, u32[]{:S(2)}, u32[]{:S(2)}) collective-permute-start(bf16[4,64,128]{2,1,0:T(8,128)(2,1)S(1)} %get-tuple-element.84), channel_id=1, source_target_pairs={{0,8},{4,12},{8,0},{12,4},{1,9},{5,13},{9,1},{13,5},{2,10},{6,14},... | collective-permute-start | bytes 196616 | tf_op jit(solution)/shard_map/ppermute | solution.py:332
  30.4 13.9 %collective-permute-start.13 = (bf16[4,64,128]{2,1,0:T(8,128)(2,1)S(1)}, bf16[4,64,128]{2,1,0:T(8,128)(2,1)S(1)}, u32[]{:S(2)}, u32[]{:S(2)}) collective-permute-start(bf16[4,64,128]{2,1,0:T(8,128)(2,1)S(1)} %get-tuple-element.93), channel_id=1, source_target_pairs={{0,8},{4,12},{8,0},{12,4},{1,9},{5,13},{9,1},{13,5},{2,10},{6,14},... | collective-permute-start | bytes 196616 | tf_op jit(solution)/shard_map/ppermute | solution.py:332
  42.0 4.0 %collective-permute-start.14 = (bf16[2,64,128]{2,1,0:T(8,128)(2,1)S(1)}, bf16[2,64,128]{2,1,0:T(8,128)(2,1)S(1)}, u32[]{:S(2)}, u32[]{:S(2)}) collective-permute-start(bf16[2,64,128]{2,1,0:T(8,128)(2,1)S(1)} %get-tuple-element.94), channel_id=1, source_target_pairs={{0,2},{2,0},{1,3},{3,1},{4,6},{6,4},{5,7},{7,5},{8,10},{10,8},{9,1... | collective-permute-start | bytes 98312 | tf_op jit(solution)/shard_map/ppermute | solution.py:297

commit v4 on v3

v4 whole, which is shorter than its diff:
```python
import functools

import jax
import jax.numpy as jnp
from jax import lax
from jax.experimental import pallas as pl
from jax.experimental.pallas import tpu as pltpu
from jax.sharding import PartitionSpec as P

HR = 2
CAP = 11
BASE = 8
SPARE = CAP - BASE
PARTS = 2
STRIDE = 16
TRASH = STRIDE - 2
COUNT = STRIDE - 1
BF16 = jnp.bfloat16
F32 = jnp.float32
VMEM = pltpu.VMEM
SMEM = pltpu.SMEM


def whole(space):
    return pl.BlockSpec(memory_space=space)


def wrap(value, size):
    return jnp.where(value < 0, value + size, value)


def decode(lists_ref, number_ref, r, a, k, rows):
    used = k < number_ref[0, a, r]
    owner = jnp.where(used, lists_ref[0, a, 0, k, r], -1)
    return owner, HR + lists_ref[0, a, 1, k, r] * rows + lists_ref[0, a, 2, k, r]


def serve(lists_ref, number_ref, send_ref, a, d, rows, per_row):
    me = lax.axis_index("lon")
    base = d * STRIDE
    filled = jnp.int32(0)
    for r in range(rows):
        for k in range(per_row):
            owner, row = decode(lists_ref, number_ref, r, a, k, rows)
            send_ref[base + jnp.where(owner == me, filled, TRASH)] = row
            filled = filled + jnp.where(owner == me, 1, 0)
    send_ref[base + COUNT] = filled


def prepare_kernel(tiles, bands, per_row, lists_hbm, number_hbm, fields_hbm, *rest):
    rows_ref, send_ref, *rest = rest
    edges = rest[: 1 if bands == 2 else 2]
    lists_ref, number_ref, held, wide, list_sem, number_sem, sems = rest[len(edges) :]
    rows, channels, _ = rows_ref.shape
    me = lax.axis_index("lon")
    dump = rows + 2 * HR
    chunk = 16
    lists_copy = pltpu.make_async_copy(lists_hbm, lists_ref, list_sem)
    number_copy = pltpu.make_async_copy(number_hbm, number_ref, number_sem)
    lists_copy.start()
    number_copy.start()
    copies = []
    for i, c in enumerate(range(0, channels, chunk)):
        span = pl.ds(c * rows, chunk * rows)
        copies.append(pltpu.make_async_copy(fields_hbm.at[span], held.at[span], sems.at[i]))
        copies[-1].start()
    for d in range(1, tiles):
        for s in range(CAP):
            send_ref[d * STRIDE + s] = dump
    lists_copy.wait()
    number_copy.wait()
    if tiles <= 4:
        for d in range(1, tiles):
            serve(lists_ref, number_ref, send_ref, wrap(me + d - tiles, tiles), d, rows, per_row)
    else:

        @pl.loop(1, tiles)
        def _(d):
            serve(lists_ref, number_ref, send_ref, wrap(me + d - tiles, tiles), d, rows, per_row)

    for i, c in enumerate(range(0, channels, chunk)):
        copies[i].wait()
        span = slice(c * rows, (c + chunk) * rows)
        wide[span] = held[span].astype(F32)
        for r in range(rows):
            rows_ref[r, c : c + chunk] = wide[pl.ds(c * rows + r, chunk, stride=rows), :].astype(BF16)
    if bands == 2:
        start = jnp.where(lax.axis_index("lat") == 0, rows - HR, 0)
        edges[0][...] = rows_ref[pl.ds(start, HR)]
    else:
        edges[0][...] = rows_ref[0:HR]
        edges[1][...] = rows_ref[rows - HR : rows]


def pack_kernel(tiles, start, send_ref, rows_ref, before_ref, after_ref, ext_ref, *rest):
    base, spare = rest[: tiles - 1], rest[tiles - 1 :]
    rows = rows_ref.shape[0]
    part = slice(start, start + ext_ref.shape[1])
    ext_ref[0:HR] = before_ref[:, part]
    ext_ref[HR : HR + rows] = rows_ref[:, part]
    ext_ref[HR + rows : HR + rows + HR] = after_ref[:, part]
    for d in range(1, tiles):
        for s in range(BASE):
            base[d - 1][s] = ext_ref[send_ref[d * STRIDE + s]]
    for d in range(1, tiles):

        @pl.when(send_ref[d * STRIDE + COUNT] > BASE)
        def _():
            for s in range(SPARE):
                spare[d - 1][s] = ext_ref[send_ref[d * STRIDE + BASE + s]]


def arrival_kernel(tiles, per_row, lists_ref, number_ref, cot_ref, taps_ref, *rest):
    cot_rows_ref, mix_ref, place_ref, own_ref, wide, taken = rest
    rows, channels, cols = cot_rows_ref.shape
    me = lax.axis_index("lon")
    entries = rows * per_row
    ext = rows + 2 * HR
    for s in range(CAP):
        own_ref[s] = ext
    serve(lists_ref, number_ref, own_ref, me, 0, rows, per_row)
    for d in range(tiles + 1):
        taken[d] = 0

    def place(r):
        for k in range(per_row):
            owner, ext_row = decode(lists_ref, number_ref, r, me, k, rows)
            used = owner >= 0
            d = jnp.where(used, wrap(me - owner, tiles), tiles)
            slot = d * STRIDE + taken[d]
            source = jnp.where(owner == me, tiles * STRIDE + ext_row, slot)
            place_ref[r * per_row + k] = jnp.where(used, source, tiles * STRIDE + ext)
            place_ref[entries + r * per_row + k] = jnp.where(used, slot, tiles * STRIDE)
            taken[d] = taken[d] + 1

    pl.loop(0, rows)(place)
    for d in range(tiles):
        place_ref[2 * entries + d] = taken[d]

    wide[...] = cot_ref[...].astype(F32)
    for r in range(rows):
        cot_rows_ref[r] = wide[pl.ds(r, channels, stride=rows), :].astype(BF16)
    w0, w1, w2, w3 = (taps_ref[j] for j in range(4))
    cell = lax.broadcasted_iota(jnp.int32, w0.shape, 1)
    first, last, late = cell == 0, cell == cols - 1, cell == cols - 2
    mix_ref[0] = pltpu.roll(jnp.where(first, 0.0, w0), cols - 1, 1)
    mix_ref[1] = w1 + jnp.where(first, w0, 0.0) + jnp.where(last, w2 + w3, 0.0)
    mix_ref[2] = pltpu.roll(jnp.where(last, 0.0, w2) + jnp.where(late, w3, 0.0), 1, 1)
    mix_ref[3] = pltpu.roll(jnp.where(last | late, 0.0, w3), 2, 1)


def compute_kernel(tiles, per_row, start, place_ref, mix_ref, cot_ref, ext_ref, *rest):
    n = tiles - 1
    base, spare, rest = rest[:n], rest[n : 2 * n], rest[2 * n :]
    own_out, base_out, spare_out, rest = rest[0], rest[1 : n + 1], rest[n + 1 : 2 * n + 1], rest[2 * n + 1 :]
    grad_ref, blocks, terms = rest
    rows, _, cols = cot_ref.shape
    channels = ext_ref.shape[1]
    entries = rows * per_row
    ext = rows + 2 * HR
    part = min(channels, 32)
    blocks[tiles * STRIDE : tiles * STRIDE + ext] = ext_ref[0:ext]
    blocks[tiles * STRIDE + ext] = jnp.zeros((channels, cols), BF16)
    for d in range(1, tiles):
        at = d * STRIDE
        blocks[at : at + BASE] = base[d - 1][...]

        @pl.when(place_ref[2 * entries + d] > BASE)
        def _():
            blocks[at + BASE : at + CAP] = spare[d - 1][...]

    def row(r, _):
        source = [place_ref[r * per_row + k] for k in range(per_row)]
        target = [place_ref[entries + r * per_row + k] for k in range(per_row)]
        mix = [[mix_ref[j, pl.ds(r * per_row + k, 1), :] for j in range(4)] for k in range(per_row)]
        for lo in range(0, channels, part):
            block = [blocks[source[k], lo : lo + part].astype(F32) for k in range(per_row)]
            tap = [sum(block[k] * mix[k][j] for k in range(per_row)) for j in range(4)]
            interp = (tap[1] + pltpu.roll(tap[0], 1, 1)) + (
                pltpu.roll(tap[2], cols - 1, 1) + pltpu.roll(tap[3], cols - 2, 1)
            )
            bent = jnp.tanh(interp)
            scaled = cot_ref[r, start + lo : start + lo + part].astype(F32) * (2.0 - bent * bent)
            scaled = scaled.astype(BF16).astype(F32)
            moved = [
                pltpu.roll(scaled, cols - 1, 1),
                scaled,
                pltpu.roll(scaled, 1, 1),
                pltpu.roll(scaled, 2, 1),
            ]
            for k in range(per_row):
                term = (moved[0] * mix[k][0] + moved[1] * mix[k][1]) + (
                    moved[2] * mix[k][2] + moved[3] * mix[k][3]
                )
                terms[target[k], lo : lo + part] = term.astype(BF16)
                for j in range(4):
                    at = (r * per_row + k) * 4 + j
                    product = jnp.sum((block[k] * moved[j]).reshape(part // 8, 8, cols), axis=0)
                    grad_ref[at] = product if lo == 0 else grad_ref[at] + product
        return 0

    lax.fori_loop(0, rows, row, 0, unroll=4)
    for d in range(1, tiles):
        at = d * STRIDE
        base_out[d - 1][...] = terms[at : at + BASE]

        @pl.when(place_ref[2 * entries + d] > BASE)
        def _():
            spare_out[d - 1][...] = terms[at + BASE : at + CAP]

    own_out[...] = terms[0:CAP]


def gradient_kernel(*refs):
    *partial_refs, out_ref = refs
    sums = jnp.sum(sum(ref[...] for ref in partial_refs), axis=1)
    count, cols = sums.shape
    tap = lax.broadcasted_iota(jnp.int32, sums.shape, 0) & 3
    cell = lax.broadcasted_iota(jnp.int32, sums.shape, 1)
    grads = jnp.where(tap == 0, pltpu.roll(sums, 1, 1), sums)
    grads = jnp.where(tap == 2, pltpu.roll(sums, cols - 1, 1), grads)
    grads = jnp.where(tap == 3, pltpu.roll(sums, cols - 2, 1), grads)
    following = pltpu.roll(grads, count - 1, 0)
    previous = pltpu.roll(grads, 1, 0)
    second = pltpu.roll(grads, 2, 0)
    fixed = jnp.where((tap == 0) & (cell == 0), following, grads)
    fixed = jnp.where((tap == 2) & (cell == cols - 1), previous, fixed)
    fixed = jnp.where((tap == 3) & (cell == cols - 2), previous, fixed)
    fixed = jnp.where((tap == 3) & (cell == cols - 1), second, fixed)
    out_ref[...] = fixed.astype(BF16)


def add_own_kernel(table_ref, own_ref, total_ref):
    total_ref[...] = jnp.zeros_like(total_ref)
    for s in range(CAP):
        at = table_ref[s]
        total_ref[at] = total_ref[at] + own_ref[s].astype(F32)


def add_kernel(tiles, bands, send_ref, _, *rest):
    n = tiles - 1
    base, spare, (total_ref, *edges) = rest[:n], rest[n : 2 * n], rest[2 * n :]
    ext = total_ref.shape[0] - 1
    for d in range(1, tiles):
        for s in range(BASE):
            at = send_ref[d * STRIDE + s]
            total_ref[at] = total_ref[at] + base[d - 1][s].astype(F32)

        @pl.when(send_ref[d * STRIDE + COUNT] > BASE)
        def _():
            for s in range(SPARE):
                at = send_ref[d * STRIDE + BASE + s]
                total_ref[at] = total_ref[at] + spare[d - 1][s].astype(F32)

    if bands == 2:
        start = jnp.where(lax.axis_index("lat") == 0, ext - HR, 0)
        edges[0][...] = total_ref[pl.ds(start, HR)].astype(BF16)
    else:
        edges[0][...] = total_ref[0:HR].astype(BF16)
        edges[1][...] = total_ref[ext - HR : ext].astype(BF16)


def finish_kernel(bands, rows, start, total_ref, above_ref, below_ref, *rest):
    out_hbm, held, sems = rest[-3:]
    channels = total_ref.shape[1]
    band = lax.axis_index("lat")
    chunk = 16
    copies = []
    for i, c in enumerate(range(0, channels, chunk)):
        part = slice(c, c + chunk)
        for r in range(rows):
            value = total_ref[HR + r, part]
            if r < HR:
                value = value + jnp.where(band > 0, above_ref[r, part].astype(F32), 0.0)
            if r >= rows - HR:
                below = below_ref[r - rows + HR, part].astype(F32)
                value = value + jnp.where(band < bands - 1, below, 0.0)
            held[pl.ds(c * rows + r, chunk, stride=rows), :] = value
        source = held.at[pl.ds(c * rows, chunk * rows)]
        target = out_hbm.at[pl.ds((start + c) * rows, chunk * rows)]
        copies.append(pltpu.make_async_copy(source, target, sems.at[i]))
        copies[-1].start()
    for copy in copies:
        copy.wait()


def swap_lat(edges, bands):
    if bands == 2:
        got = lax.ppermute(edges[0], "lat", [(0, 1), (1, 0)])
        return got, got
    down = [(i, i + 1) for i in range(bands - 1)]
    up = [(i + 1, i) for i in range(bands - 1)]
    return lax.ppermute(edges[1], "lat", down), lax.ppermute(edges[0], "lat", up)


def local(fields, arrival_cot, weights, departures, counts):
    lev_dev, field_count, rows, cols = fields.shape
    channels = lev_dev * field_count
    tiles = lax.axis_size("lon")
    bands = lax.axis_size("lat")
    per_row, taps = weights.shape[3], weights.shape[4]
    entries = rows * per_row
    ext = rows + 2 * HR
    partners = tiles - 1
    middle = tiles // 2
    width = channels // PARTS
    params = pltpu.CompilerParams(vmem_limit_bytes=48 * 1024 * 1024)

    def call(kernel, out_shape, in_specs, out_specs, scratch=(), name=None, aliases={}):
        return pl.pallas_call(
            kernel,
            out_shape=out_shape,
            in_specs=in_specs,
            out_specs=out_specs,
            scratch_shapes=list(scratch),
            compiler_params=params,
            input_output_aliases=aliases,
            name=name,
        )

    def array(*shape, dtype=BF16):
        return jax.ShapeDtypeStruct(shape, dtype)

    def move(part, d):
        return lax.ppermute(part, "lon", [(i, (i + d) % tiles) for i in range(tiles)])

    def move_all(parts, sign):
        out = [None] * partners
        for d in [middle] + [d for d in range(1, tiles) if d != middle]:
            out[d - 1] = move(parts[d - 1], sign * d)
        return out

    def move_spare(parts, sign):
        return lax.cond(needed, lambda parts: move_all(parts, sign), lambda parts: parts, list(parts))

    lists = jnp.transpose(departures, (0, 2, 4, 3, 1))
    number = jnp.transpose(counts, (0, 2, 1))

    edge_count = 1 if bands == 2 else 2
    edge = (array(HR, channels, cols),) * edge_count
    half_edge = (array(HR, width, cols),) * edge_count
    base_slots = (array(BASE, width, cols),) * partners
    spare_slots = (array(SPARE, width, cols),) * partners

    def hbm(value):
        return pltpu.with_memory_space_constraint(value, pltpu.HBM)

    row_blocks, send_rows, *edges = call(
        functools.partial(prepare_kernel, tiles, bands, per_row),
        (array(rows, channels, cols), array(tiles * STRIDE, dtype=jnp.int32)) + edge,
        [whole(pltpu.HBM)] * 3,
        (whole(VMEM), whole(SMEM)) + (whole(VMEM),) * edge_count,
        [
            SMEM(lists.shape, jnp.int32),
            SMEM(number.shape, jnp.int32),
            VMEM((channels * rows, cols), BF16),
            VMEM((channels * rows, cols), F32),
            pltpu.SemaphoreType.DMA,
            pltpu.SemaphoreType.DMA,
            pltpu.SemaphoreType.DMA((channels // 16,)),
        ],
        "prepare",
    )(hbm(lists), hbm(number), hbm(fields.reshape(channels * rows, cols)))
    before, after = swap_lat(edges, bands)

    tile = jnp.arange(tiles, dtype=jnp.int32)
    entry = jnp.arange(per_row, dtype=jnp.int32)
    named = (entry[:, None] < number[0][:, None, :]) & (lists[0, :, 0] == tile[:, None, None, None])
    filled = jnp.sum(jnp.where(named, 1, 0), axis=(2, 3))
    needed = jnp.any((filled > BASE) & (tile[None, :] != tile[:, None]))

    mixing = weights.reshape(rows, per_row, taps, cols).astype(F32)
    mixing = jnp.transpose(mixing, (2, 0, 1, 3)).reshape(taps, entries, cols)

    sent = []
    for start in range(0, channels, width):
        ext_blocks, *slots = call(
            functools.partial(pack_kernel, tiles, start),
            (array(ext + 1, width, cols),) + base_slots + spare_slots,
            [whole(SMEM)] + [whole(VMEM)] * 3,
            (whole(VMEM),) * (1 + 2 * partners),
            (),
            "pack",
        )(send_rows, row_blocks, before, after)
        sent.append((ext_blocks, move_all(slots[:partners], 1), move_spare(slots[partners:], 1)))

    cot_rows, mix, places, own_table = call(
        functools.partial(arrival_kernel, tiles, per_row),
        (
            array(rows, channels, cols),
            array(taps, entries, cols, dtype=F32),
            array(2 * entries + tiles, dtype=jnp.int32),
            array(STRIDE, dtype=jnp.int32),
        ),
        [whole(SMEM), whole(SMEM), whole(VMEM), whole(VMEM)],
        (whole(VMEM), whole(VMEM), whole(SMEM), whole(SMEM)),
        [VMEM((channels * rows, cols), F32), SMEM((tiles + 1,), jnp.int32)],
        "arrival",
    )(lists, number, arrival_cot.reshape(channels * rows, cols), mixing)

    back, partial = [], []
    for i, (ext_blocks, base, spare) in enumerate(sent):
        own, *slots = call(
            functools.partial(compute_kernel, tiles, per_row, i * width),
            (array(CAP, width, cols),)
            + base_slots
            + spare_slots
            + (array(entries * taps, 8, cols, dtype=F32),),
            [whole(SMEM)] + [whole(VMEM)] * (3 + 2 * partners),
            (whole(VMEM),) * (2 + 2 * partners),
            [
                VMEM((tiles * STRIDE + ext + 1, width, cols), BF16),
                VMEM((tiles * STRIDE + 1, width, cols), BF16),
            ],
            "compute",
        )(places, mix, cot_rows, ext_blocks, *base, *spare)
        back.append((own, move_all(slots[:partners], -1), move_spare(slots[partners : 2 * partners], -1)))
        partial.append(slots[-1])

    sums = array(ext + 1, width, cols, dtype=F32)
    source = None
    for i, (own, base, spare) in enumerate(back):
        total = call(add_own_kernel, sums, [whole(SMEM), whole(VMEM)], whole(VMEM), (), "add_own")(
            own_table, own
        )
        total, *edges = call(
            functools.partial(add_kernel, tiles, bands),
            (sums,) + half_edge,
            [whole(SMEM)] + [whole(VMEM)] * (1 + 2 * partners),
            (whole(VMEM),) * (1 + edge_count),
            (),
            "add",
            {1: 0},
        )(send_rows, total, *base, *spare)
        from_above, from_below = swap_lat(edges, bands)
        earlier = [] if source is None else [source]
        source = call(
            functools.partial(finish_kernel, bands, rows, i * width),
            array(channels * rows, cols, dtype=F32),
            [whole(VMEM)] * 3 + [whole(pltpu.HBM)] * len(earlier),
            whole(pltpu.HBM),
            [VMEM((width * rows, cols), F32), pltpu.SemaphoreType.DMA((width // 16,))],
            "finish",
            {3: 0} if earlier else {},
        )(total, from_above, from_below, *earlier)

    *partial, _ = lax.optimization_barrier((*partial, edges[0]))
    weight_grad = call(
        gradient_kernel,
        array(entries * taps, cols),
        [whole(VMEM)] * PARTS,
        whole(VMEM),
        (),
        "gradient",
    )(*partial)
    return source.reshape(fields.shape), weight_grad.reshape(weights.shape)


def solution(mesh):
    return jax.shard_map(
        local,
        mesh=mesh,
        in_specs=(
            P("lev", "ens", "lat", "lon"),
            P("lev", "ens", "lat", "lon"),
            P("lev", "lat", "lon", "ens", None, None),
            P("lev", "lat", None, "ens", None),
            P("lev", "lat", "ens"),
        ),
        out_specs=(P("lev", "ens", "lat", "lon"), P("lev", "lat", "lon", "ens", None, None)),
        check_vma=False,
    )
```

time: 47.8 us -> 43.8 us (0.916)
  waiting for transfers between devices: 13.3 us -> 3.85 us
  starting transfers between devices: 17.8 us -> 23.3 us
  Pallas kernels: 11.1 us -> 13.5 us
  local copies, waits for them, and re-layouts: 3.03 us -> 0.73 us
    ppermute x7 -> x12, waiting for transfers between devices: 11.4 us -> 2.21 us  [move(): lax.ppermute(part, 'lon', [(i, (i + d) % tiles) for i in range(tiles)])]
    ppermute x7 -> x12, starting transfers between devices: 13.3 us -> 17.1 us  [move(): lax.ppermute(part, 'lon', [(i, (i + d) % tiles) for i in range(tiles)])]
    unnamed x12 -> x8, local copies, waits for them, and re-layouts: 2.99 us -> 0.69 us
    pallas_call x5 -> x9, Pallas kernels: 5.8 us -> 7.89 us  [the longest x2 3.02 us: local(): call(functools.partial(compute_kernel, tiles, per_row, i * width), (array...]
    ppermute x2 -> x3, starting transfers between devices: 4.52 us -> 6.12 us  [swap_lat(): got = lax.ppermute(edges[0], 'lat', [(0, 1), (1, 0)])]
    pallas_call x1 -> x2, Pallas kernels: 0.64 us -> 1.22 us  [local(): call(add_own_kernel, sums, [whole(SMEM), whole(VMEM)], whole(VMEM), (), '...]
    ppermute x2 -> x3, waiting for transfers between devices: 1.92 us -> 1.64 us  [swap_lat(): got = lax.ppermute(edges[0], 'lat', [(0, 1), (1, 0)])]
  transfers between devices with their start and end apart: 9 -> 15, of which waited for: 5 -> 4; matrix products, arithmetic and copies ran while one was open for 2% -> 2% of each run, Pallas kernels for 9% -> 22%
where the time goes in v4:
time: 43.8 us; the launch traced here: 43.6 us
  starting transfers between devices  23.3 us (53%)
  Pallas kernels  13.5 us (31%)
  waiting for transfers between devices  3.85 us (9%)
  between operations  1.46 us (3%)
  other arithmetic  0.8 us (2%)
  local copies, waits for them, and re-layouts  0.73 us (2%)
    ppermute x12, starting transfers between devices, move(): lax.ppermute(part, 'lon', [(i, (i + d) % tiles) for i in range(tiles)])  17.1 us
    ppermute x3, starting transfers between devices, swap_lat(): got = lax.ppermute(edges[0], 'lat', [(0, 1), (1, 0)])  6.12 us
    pallas_call x2, Pallas kernels, local(): call(functools.partial(compute_kernel, tiles, per_row, i * width), (array...  3.02 us
    pallas_call x1, Pallas kernels, local(): call(functools.partial(prepare_kernel, tiles, bands, per_row), (array(row...  2.4 us
    ppermute x12, waiting for transfers between devices, move(): lax.ppermute(part, 'lon', [(i, (i + d) % tiles) for i in range(tiles)])  2.21 us
    pallas_call x1, Pallas kernels, local(): call(functools.partial(arrival_kernel, tiles, per_row), (array(rows, chan...  2 us
    ppermute x3, waiting for transfers between devices, swap_lat(): got = lax.ppermute(edges[0], 'lat', [(0, 1), (1, 0)])  1.64 us
    pallas_call x2, Pallas kernels, local(): call(functools.partial(finish_kernel, bands, rows, i * width), array(chan...  1.53 us
  transfers between devices with their start and end apart: 15, of which 4 were waited for; matrix products, arithmetic and copies ran while one was open for 2% of the time, Pallas kernels for 22%

profile of v4, /device:TPU:0, one launch (start us, length us, event | category | flops | bytes accessed | tf_op | source)
XLA Modules:
  0.0 43.6 jit_solution(8593732287489165722)
XLA Ops:
  0.6 2.4 %prepare.1 = (bf16[16,64,128]{2,1,0:T(8,128)(2,1)S(1)}, s32[64]{0:T(128)S(1)}, bf16[2,64,128]{2,1,0:T(8,128)(2,1)S(1)}) custom-call(s32[1,4,3,2,16]{4,3,2,1,0:T(2,128)} %bitcast.20, s32[1,4,16]{2,1,0:T(4,128)} %bitcast.23, bf16[1024,128]{1,0:T(8,128)(2,1)} %bitcast.27), custom_call_target="tpu_custom_call" | custom-call | tf_op jit(solution)/shard_map/prepare/pallas_call | solution.py:348
  3.0 3.0 %collective-permute-start.12 = (bf16[2,64,128]{2,1,0:T(8,128)(2,1)S(1)}, bf16[2,64,128]{2,1,0:T(8,128)(2,1)S(1)}, u32[]{:S(2)}, u32[]{:S(2)}) collective-permute-start(bf16[2,64,128]{2,1,0:T(8,128)(2,1)S(1)} %get-tuple-element.123), channel_id=1, source_target_pairs={{0,2},{2,0},{1,3},{3,1},{4,6},{6,4},{5,7},{7,5},{8,10},{10,8},{9,1... | collective-permute-start | bytes 98312 | tf_op jit(solution)/shard_map/ppermute | solution.py:289
  6.1 0.7 %copy-done.2 = s32[1,16,4]{1,2,0:T(4,128)S(1)} copy-done((s32[1,16,4]{1,2,0:T(4,128)S(1)}, s32[1,16,4]{1,2,0:T(4,128)}, u32[]{:S(2)}) %copy-start.2) | copy-done | bytes 280
  6.7 0.2 select_reduce_fusion
  6.9 1.0 %collective-permute-done.12.before_ref.after_ref = bf16[2,64,128]{2,1,0:T(8,128)(2,1)S(1)} collective-permute-done((bf16[2,64,128]{2,1,0:T(8,128)(2,1)S(1)}, bf16[2,64,128]{2,1,0:T(8,128)(2,1)S(1)}, u32[]{:S(2)}, u32[]{:S(2)}) %collective-permute-start.12) | collective-permute-done | bytes 32800 | tf_op jit(solution)/shard_map/ppermute | solution.py:289
  7.9 0.6 %pack.3 = (bf16[21,32,128]{2,1,0:T(8,128)(2,1)S(1)}, bf16[8,32,128]{2,1,0:T(8,128)(2,1)S(1)}, bf16[8,32,128]{2,1,0:T(8,128)(2,1)S(1)}, bf16[8,32,128]{2,1,0:T(8,...) custom-call(s32[64]{0:T(128)S(1)} %get-tuple-element.117.send_ref, ...), custom_call_target="tpu_custom_call" | custom-call | tf_op jit(solution)/shard_map/pack/pallas_call | solution.py:377
  8.5 2.2 %collective-permute-start.20 = (bf16[8,32,128]{2,1,0:T(8,128)(2,1)S(1)}, bf16[8,32,128]{2,1,0:T(8,128)(2,1)S(1)}, u32[]{:S(2)}, u32[]{:S(2)}) collective-permute-start(bf16[8,32,128]{2,1,0:T(8,128)(2,1)S(1)} %get-tuple-element.147), channel_id=1, source_target_pairs={{0,4},{4,8},{8,12},{12,0},{1,5},{5,9},{9,13},{13,1},{2,6},{6,10},{... | collective-permute-start | bytes 196616 | tf_op jit(solution)/shard_map/ppermute | solution.py:325
  10.7 0.6 %fusion.2 = pred[]{:T(512)} fusion(s32[4,4]{1,0:T(4,128)S(1)} %select_reduce_fusion), kind=kLoop, calls=%fused_computation.8 | loop fusion | flops 63 | bytes 65 | tf_op jit(solution)/shard_map/reduce_or | solution.py:370
  12.0 2.7 %collective-permute-start.21 = (bf16[8,32,128]{2,1,0:T(8,128)(2,1)S(1)}, bf16[8,32,128]{2,1,0:T(8,128)(2,1)S(1)}, u32[]{:S(2)}, u32[]{:S(2)}) collective-permute-start(bf16[8,32,128]{2,1,0:T(8,128)(2,1)S(1)} %get-tuple-element.148), channel_id=1, source_target_pairs={{0,8},{4,12},{8,0},{12,4},{1,9},{5,13},{9,1},{13,5},{2,10},{6,14},... | collective-permute-start | bytes 196616 | tf_op jit(solution)/shard_map/ppermute | solution.py:325
  14.6 0.6 %pack.2 = (bf16[21,32,128]{2,1,0:T(8,128)(2,1)S(1)}, bf16[8,32,128]{2,1,0:T(8,128)(2,1)S(1)}, bf16[8,32,128]{2,1,0:T(8,128)(2,1)S(1)}, bf16[8,32,128]{2,1,0:T(8,...) custom-call(s32[64]{0:T(128)S(1)} %get-tuple-element.117.send_ref, ...), custom_call_target="tpu_custom_call" | custom-call | tf_op jit(solution)/shard_map/pack/pallas_call | solution.py:377
  15.2 0.0 copy-start
  15.3 1.4 %collective-permute-start.22 = (bf16[8,32,128]{2,1,0:T(8,128)(2,1)S(1)}, bf16[8,32,128]{2,1,0:T(8,128)(2,1)S(1)}, u32[]{:S(2)}, u32[]{:S(2)}) collective-permute-start(bf16[8,32,128]{2,1,0:T(8,128)(2,1)S(1)} %get-tuple-element.149), channel_id=1, source_target_pairs={{0,12},{4,0},{8,4},{12,8},{1,13},{5,1},{9,5},{13,9},{2,14},{6,2},{... | collective-permute-start | bytes 196616 | tf_op jit(solution)/shard_map/ppermute | solution.py:325
  16.7 0.7 %collective-permute-start.13 = (bf16[8,32,128]{2,1,0:T(8,128)(2,1)S(1)}, bf16[8,32,128]{2,1,0:T(8,128)(2,1)S(1)}, u32[]{:S(2)}, u32[]{:S(2)}) collective-permute-start(bf16[8,32,128]{2,1,0:T(8,128)(2,1)S(1)} %get-tuple-element.125), channel_id=1, source_target_pairs={{0,4},{4,8},{8,12},{12,0},{1,5},{5,9},{9,13},{13,1},{2,6},{6,10},{... | collective-permute-start | bytes 196616 | tf_op jit(solution)/shard_map/ppermute | solution.py:325
  17.3 0.3 collective-permute-start.14
  17.7 0.0 collective-permute-done.20.rest_0_
  17.7 2.8 %collective-permute-start.15 = (bf16[8,32,128]{2,1,0:T(8,128)(2,1)S(1)}, bf16[8,32,128]{2,1,0:T(8,128)(2,1)S(1)}, u32[]{:S(2)}, u32[]{:S(2)}) collective-permute-start(bf16[8,32,128]{2,1,0:T(8,128)(2,1)S(1)} %get-tuple-element.127), channel_id=1, source_target_pairs={{0,12},{4,0},{8,4},{12,8},{1,13},{5,1},{9,5},{13,9},{2,14},{6,2},{... | collective-permute-start | bytes 196616 | tf_op jit(solution)/shard_map/ppermute | solution.py:325
  20.5 0.0 copy-done.3
  20.6 2.0 %arrival.1 = (bf16[16,64,128]{2,1,0:T(8,128)(2,1)S(1)}, f32[4,32,128]{2,1,0:T(8,128)S(1)}, s32[68]{0:T(128)S(1)}, s32[16]{0:T(128)S(1)}) custom-call(s32[1,4,3,2,16]{4,3,2,1,0:T(2,128)S(1)} %bitcast.22, s32[1,4,16]{2,1,0:T(4,128)S(1)} %bitcast.25, bf16[1024,128]{1,0:T(8,128)(2,1)S(1)} %bitcast.18, f32[4,32,128]{2,1,0:T(8,128)S(1)} %bitcast.19), custom_call_target="tpu_custom_call" | custom-call | tf_op jit(solution)/shard_map/arrival/pallas_call | solution.py:387
  22.6 0.0 collective-permute-done.21.rest_1_
  22.6 0.0 collective-permute-done.22.rest_2_
  22.6 1.5 %compute.3 = (bf16[11,32,128]{2,1,0:T(8,128)(2,1)S(1)}, bf16[8,32,128]{2,1,0:T(8,128)(2,1)S(1)}, bf16[8,32,128]{2,1,0:T(8,128)(2,1)S(1)}, bf16[8,32,128]{2,1,0:T...) custom-call(s32[68]{0:T(128)S(1)} %get-tuple-element.119.place_ref, ...), custom_call_target="tpu_custom_call" | custom-call | tf_op jit(solution)/shard_map/compute/pallas_call | solution.py:403
  24.1 1.3 %collective-permute-start.23 = (bf16[8,32,128]{2,1,0:T(8,128)(2,1)S(1)}, bf16[8,32,128]{2,1,0:T(8,128)(2,1)S(1)}, u32[]{:S(2)}, u32[]{:S(2)}) collective-permute-start(bf16[8,32,128]{2,1,0:T(8,128)(2,1)S(1)} %get-tuple-element.157), channel_id=1, source_target_pairs={{0,12},{4,0},{8,4},{12,8},{1,13},{5,1},{9,5},{13,9},{2,14},{6,2},{... | collective-permute-start | bytes 196616 | tf_op jit(solution)/shard_map/ppermute | solution.py:325
  25.4 0.0 collective-permute-done.13.rest_0_
  25.4 0.0 collective-permute-done.14.rest_1_
  25.4 0.0 collective-permute-done.15.rest_2_
  25.4 1.5 %compute.2 = (bf16[11,32,128]{2,1,0:T(8,128)(2,1)S(1)}, bf16[8,32,128]{2,1,0:T(8,128)(2,1)S(1)}, bf16[8,32,128]{2,1,0:T(8,128)(2,1)S(1)}, bf16[8,32,128]{2,1,0:T...) custom-call(s32[68]{0:T(128)S(1)} %get-tuple-element.119.place_ref, ...), custom_call_target="tpu_custom_call" | custom-call | tf_op jit(solution)/shard_map/compute/pallas_call | solution.py:403
  27.0 0.9 %collective-permute-start.24 = (bf16[8,32,128]{2,1,0:T(8,128)(2,1)S(1)}, bf16[8,32,128]{2,1,0:T(8,128)(2,1)S(1)}, u32[]{:S(2)}, u32[]{:S(2)}) collective-permute-start(bf16[8,32,128]{2,1,0:T(8,128)(2,1)S(1)} %get-tuple-element.158), channel_id=1, source_target_pairs={{0,8},{4,12},{8,0},{12,4},{1,9},{5,13},{9,1},{13,5},{2,10},{6,14},... | collective-permute-start | bytes 196616 | tf_op jit(solution)/shard_map/ppermute | solution.py:325
  27.9 2.0 %collective-permute-start.25 = (bf16[8,32,128]{2,1,0:T(8,128)(2,1)S(1)}, bf16[8,32,128]{2,1,0:T(8,128)(2,1)S(1)}, u32[]{:S(2)}, u32[]{:S(2)}) collective-permute-start(bf16[8,32,128]{2,1,0:T(8,128)(2,1)S(1)} %get-tuple-element.159), channel_id=1, source_target_pairs={{0,4},{4,8},{8,12},{12,0},{1,5},{5,9},{9,13},{13,1},{2,6},{6,10},{... | collective-permute-start | bytes 196616 | tf_op jit(solution)/shard_map/ppermute | solution.py:325
  29.8 1.8 %collective-permute-start.16 = (bf16[8,32,128]{2,1,0:T(8,128)(2,1)S(1)}, bf16[8,32,128]{2,1,0:T(8,128)(2,1)S(1)}, u32[]{:S(2)}, u32[]{:S(2)}) collective-permute-start(bf16[8,32,128]{2,1,0:T(8,128)(2,1)S(1)} %get-tuple-element.135), channel_id=1, source_target_pairs={{0,12},{4,0},{8,4},{12,8},{1,13},{5,1},{9,5},{13,9},{2,14},{6,2},{... | collective-permute-start | bytes 196616 | tf_op jit(solution)/shard_map/ppermute | solution.py:325
  31.7 0.3 collective-permute-start.17
  32.0 0.0 collective-permute-done.23.rest_0_
  32.0 0.8 %collective-permute-start.18 = (bf16[8,32,128]{2,1,0:T(8,128)(2,1)S(1)}, bf16[8,32,128]{2,1,0:T(8,128)(2,1)S(1)}, u32[]{:S(2)}, u32[]{:S(2)}) collective-permute-start(bf16[8,32,128]{2,1,0:T(8,128)(2,1)S(1)} %get-tuple-element.137), channel_id=1, source_target_pairs={{0,4},{4,8},{8,12},{12,0},{1,5},{5,9},{9,13},{13,1},{2,6},{6,10},{... | collective-permute-start | bytes 196616 | tf_op jit(solution)/shard_map/ppermute | solution.py:325
  32.8 0.6 %add_own.2._ = f32[21,32,128]{2,1,0:T(8,128)S(1)} custom-call(s32[16]{0:T(128)S(1)} %get-tuple-element.118.table_ref, bf16[11,32,128]{2,1,0:T(8,128)(2,1)S(1)} %get-tuple-element.134.own_ref), custom_call_target="tpu_custom_call" | custom-call | tf_op jit(solution)/shard_map/add_own/pallas_call | solution.py:423
  33.4 0.6 %add_own.3._ = f32[21,32,128]{2,1,0:T(8,128)S(1)} custom-call(s32[16]{0:T(128)S(1)} %get-tuple-element.118.table_ref, bf16[11,32,128]{2,1,0:T(8,128)(2,1)S(1)} %get-tuple-element.156.own_ref), custom_call_target="tpu_custom_call" | custom-call | tf_op jit(solution)/shard_map/add_own/pallas_call | solution.py:423
  34.0 1.7 %collective-permute-done.24.rest_1_ = bf16[8,32,128]{2,1,0:T(8,128)(2,1)S(1)} collective-permute-done((bf16[8,32,128]{2,1,0:T(8,128)(2,1)S(1)}, bf16[8,32,128]{2,1,0:T(8,128)(2,1)S(1)}, u32[]{:S(2)}, u32[]{:S(2)}) %collective-permute-start.24) | collective-permute-done | bytes 65568 | tf_op jit(solution)/shard_map/ppermute | solution.py:325
  35.7 0.0 collective-permute-done.25.rest_2_
  35.7 0.7 %add.3 = (f32[21,32,128]{2,1,0:T(8,128)S(1)}, bf16[2,32,128]{2,1,0:T(8,128)(2,1)S(1)}) custom-call(s32[64]{0:T(128)S(1)} %get-tuple-element.117.send_ref, f32[21,32,128]{2,1,0:T(8,128)S(1)} %add_own.3._, bf16[8,32,128]{2,1,0:T(8,128)(2,1)S(1)} %collective-permute-done.23.rest_0_, ...), custom_call_target="tpu_custom_call", output_to_operand_aliasing={{0}: (1, {})} | custom-call | tf_op jit(solution)/shard_map/add/pallas_call | solution.py:426
  36.3 1.6 %collective-permute-start.26 = (bf16[2,32,128]{2,1,0:T(8,128)(2,1)S(1)}, bf16[2,32,128]{2,1,0:T(8,128)(2,1)S(1)}, u32[]{:S(2)}, u32[]{:S(2)}) collective-permute-start(bf16[2,32,128]{2,1,0:T(8,128)(2,1)S(1)} %get-tuple-element.167), channel_id=1, source_target_pairs={{0,2},{2,0},{1,3},{3,1},{4,6},{6,4},{5,7},{7,5},{8,10},{10,8},{9,1... | collective-permute-start | bytes 49160 | tf_op jit(solution)/shard_map/ppermute | solution.py:289
  37.9 0.0 collective-permute-done.16.rest_0_
  37.9 0.5 %collective-permute-done.17.rest_1_ = bf16[8,32,128]{2,1,0:T(8,128)(2,1)S(1)} collective-permute-done((bf16[8,32,128]{2,1,0:T(8,128)(2,1)S(1)}, bf16[8,32,128]{2,1,0:T(8,128)(2,1)S(1)}, u32[]{:S(2)}, u32[]{:S(2)}) %collective-permute-start.17) | collective-permute-done | bytes 65568 | tf_op jit(solution)/shard_map/ppermute | solution.py:325
  38.4 0.0 collective-permute-done.18.rest_2_
  38.4 0.7 %add.2 = (f32[21,32,128]{2,1,0:T(8,128)S(1)}, bf16[2,32,128]{2,1,0:T(8,128)(2,1)S(1)}) custom-call(s32[64]{0:T(128)S(1)} %get-tuple-element.117.send_ref, f32[21,32,128]{2,1,0:T(8,128)S(1)} %add_own.2._, bf16[8,32,128]{2,1,0:T(8,128)(2,1)S(1)} %collective-permute-done.16.rest_0_, ...), custom_call_target="tpu_custom_call", output_to_operand_aliasing={{0}: (1, {})} | custom-call | tf_op jit(solution)/shard_map/add/pallas_call | solution.py:426
  39.1 1.6 %collective-permute-start.19 = (bf16[2,32,128]{2,1,0:T(8,128)(2,1)S(1)}, bf16[2,32,128]{2,1,0:T(8,128)(2,1)S(1)}, u32[]{:S(2)}, u32[]{:S(2)}) collective-permute-start(bf16[2,32,128]{2,1,0:T(8,128)(2,1)S(1)} %get-tuple-element.145), channel_id=1, source_target_pairs={{0,2},{2,0},{1,3},{3,1},{4,6},{6,4},{5,7},{7,5},{8,10},{10,8},{9,1... | collective-permute-start | bytes 49160 | tf_op jit(solution)/shard_map/ppermute | solution.py:289
  40.6 0.9 %gradient.1 = bf16[128,128]{1,0:T(8,128)(2,1)} custom-call(f32[128,8,128]{2,1,0:T(8,128)S(1)} %get-tuple-element.170.refs_0_, f32[128,8,128]{2,1,0:T(8,128)S(1)} %get-tuple-element.171.refs_1_), custom_call_target="tpu_custom_call" | custom-call | tf_op jit(solution)/shard_map/gradient/pallas_call | solution.py:448
  41.5 0.0 collective-permute-done.26.above_ref.below_ref
  41.5 0.8 %finish.2.rest_0_ = f32[1024,128]{1,0:T(8,128)} custom-call(f32[21,32,128]{2,1,0:T(8,128)S(1)} %get-tuple-element.166.total_ref, bf16[2,32,128]{2,1,0:T(8,128)(2,1)S(1)} %collective-permute-done.26.above_ref.below_ref, bf16[2,32,128]{2,1,0:T(8,128)(2,1)S(1)} %collective-permute-done.26.above_ref.below_ref), custom_call_target="tpu_custom_call" | custom-call | tf_op jit(solution)/shard_map/finish/pallas_call | solution.py:437
  42.3 0.6 %collective-permute-done.19.above_ref.below_ref = bf16[2,32,128]{2,1,0:T(8,128)(2,1)S(1)} collective-permute-done((bf16[2,32,128]{2,1,0:T(8,128)(2,1)S(1)}, bf16[2,32,128]{2,1,0:T(8,128)(2,1)S(1)}, u32[]{:S(2)}, u32[]{:S(2)}) %collective-permute-start.19) | collective-permute-done | bytes 16416 | tf_op jit(solution)/shard_map/ppermute | solution.py:289
  42.9 0.8 %finish.3 = f32[1024,128]{1,0:T(8,128)} custom-call(f32[21,32,128]{2,1,0:T(8,128)S(1)} %get-tuple-element.144.total_ref, bf16[2,32,128]{2,1,0:T(8,128)(2,1)S(1)} %collective-permute-done.19.above_ref.below_ref, bf16[2,32,128]{2,1,0:T(8,128)(2,1)S(1)} %collective-permute-done.19.above_ref.below_ref, ...), custom_call_target="tpu_custom_call", output_to_operand_aliasing={{}: (3, {})} | custom-call | tf_op jit(solution)/shard_map/finish/pallas_call | solution.py:437
  (14 shorter events, 0.1 us)
Async XLA Ops:
  0.6 5.4 %copy-start.1 = (s32[1,16,4,2,3]{1,3,4,2,0:T(2,128)S(1)}, s32[1,16,4,2,3]{1,3,4,2,0:T(2,128)}, u32[]{:S(2)}) copy-start(s32[1,16,4,2,3]{1,3,4,2,0:T(2,128)} %param.16) | copy-start | bytes 4612
  3.0 4.9 %collective-permute-start.12 = (bf16[2,64,128]{2,1,0:T(8,128)(2,1)S(1)}, bf16[2,64,128]{2,1,0:T(8,128)(2,1)S(1)}, u32[]{:S(2)}, u32[]{:S(2)}) collective-permute-start(bf16[2,64,128]{2,1,0:T(8,128)(2,1)S(1)} %get-tuple-element.123), channel_id=1, source_target_pairs={{0,2},{2,0},{1,3},{3,1},{4,6},{6,4},{5,7},{7,5},{8,10},{10,8},{9,1... | collective-permute-start | bytes 98312 | tf_op jit(solution)/shard_map/ppermute | solution.py:289
  6.1 0.7 %copy-start.2 = (s32[1,16,4]{1,2,0:T(4,128)S(1)}, s32[1,16,4]{1,2,0:T(4,128)}, u32[]{:S(2)}) copy-start(s32[1,16,4]{1,2,0:T(4,128)} %param.17) | copy-start | bytes 772
  8.5 9.1 %collective-permute-start.20 = (bf16[8,32,128]{2,1,0:T(8,128)(2,1)S(1)}, bf16[8,32,128]{2,1,0:T(8,128)(2,1)S(1)}, u32[]{:S(2)}, u32[]{:S(2)}) collective-permute-start(bf16[8,32,128]{2,1,0:T(8,128)(2,1)S(1)} %get-tuple-element.147), channel_id=1, source_target_pairs={{0,4},{4,8},{8,12},{12,0},{1,5},{5,9},{9,13},{13,1},{2,6},{6,10},{... | collective-permute-start | bytes 196616 | tf_op jit(solution)/shard_map/ppermute | solution.py:325
  12.0 10.6 %collective-permute-start.21 = (bf16[8,32,128]{2,1,0:T(8,128)(2,1)S(1)}, bf16[8,32,128]{2,1,0:T(8,128)(2,1)S(1)}, u32[]{:S(2)}, u32[]{:S(2)}) collective-permute-start(bf16[8,32,128]{2,1,0:T(8,128)(2,1)S(1)} %get-tuple-element.148), channel_id=1, source_target_pairs={{0,8},{4,12},{8,0},{12,4},{1,9},{5,13},{9,1},{13,5},{2,10},{6,14},... | collective-permute-start | bytes 196616 | tf_op jit(solution)/shard_map/ppermute | solution.py:325
  14.6 5.9 %copy-start.3 = (bf16[1,16,1,2,4,128]{5,4,3,2,1,0:T(4,128)(2,1)S(1)}, bf16[1,16,1,2,4,128]{5,4,3,2,1,0:T(4,128)(2,1)}, u32[]{:S(2)}) copy-start(bf16[1,16,1,2,4,128]{5,4,3,2,1,0:T(4,128)(2,1)} %param.15) | copy-start | bytes 98308
  15.2 5.3 %copy-start = (bf16[16,4,16,128]{3,2,1,0:T(8,128)(2,1)S(1)}, bf16[16,4,16,128]{3,2,1,0:T(8,128)(2,1)}, u32[]{:S(2)}) copy-start(bf16[16,4,16,128]{3,2,1,0:T(8,128)(2,1)} %param.14) | copy-start | bytes 786436
  15.3 7.3 %collective-permute-start.22 = (bf16[8,32,128]{2,1,0:T(8,128)(2,1)S(1)}, bf16[8,32,128]{2,1,0:T(8,128)(2,1)S(1)}, u32[]{:S(2)}, u32[]{:S(2)}) collective-permute-start(bf16[8,32,128]{2,1,0:T(8,128)(2,1)S(1)} %get-tuple-element.149), channel_id=1, source_target_pairs={{0,12},{4,0},{8,4},{12,8},{1,13},{5,1},{9,5},{13,9},{2,14},{6,2},{... | collective-permute-start | bytes 196616 | tf_op jit(solution)/shard_map/ppermute | solution.py:325
  16.7 8.7 %collective-permute-start.13 = (bf16[8,32,128]{2,1,0:T(8,128)(2,1)S(1)}, bf16[8,32,128]{2,1,0:T(8,128)(2,1)S(1)}, u32[]{:S(2)}, u32[]{:S(2)}) collective-permute-start(bf16[8,32,128]{2,1,0:T(8,128)(2,1)S(1)} %get-tuple-element.125), channel_id=1, source_target_pairs={{0,4},{4,8},{8,12},{12,0},{1,5},{5,9},{9,13},{13,1},{2,6},{6,10},{... | collective-permute-start | bytes 196616 | tf_op jit(solution)/shard_map/ppermute | solution.py:325
  17.3 8.1 %collective-permute-start.14 = (bf16[8,32,128]{2,1,0:T(8,128)(2,1)S(1)}, bf16[8,32,128]{2,1,0:T(8,128)(2,1)S(1)}, u32[]{:S(2)}, u32[]{:S(2)}) collective-permute-start(bf16[8,32,128]{2,1,0:T(8,128)(2,1)S(1)} %get-tuple-element.126), channel_id=1, source_target_pairs={{0,8},{4,12},{8,0},{12,4},{1,9},{5,13},{9,1},{13,5},{2,10},{6,14},... | collective-permute-start | bytes 196616 | tf_op jit(solution)/shard_map/ppermute | solution.py:325
  17.7 7.7 %collective-permute-start.15 = (bf16[8,32,128]{2,1,0:T(8,128)(2,1)S(1)}, bf16[8,32,128]{2,1,0:T(8,128)(2,1)S(1)}, u32[]{:S(2)}, u32[]{:S(2)}) collective-permute-start(bf16[8,32,128]{2,1,0:T(8,128)(2,1)S(1)} %get-tuple-element.127), channel_id=1, source_target_pairs={{0,12},{4,0},{8,4},{12,8},{1,13},{5,1},{9,5},{13,9},{2,14},{6,2},{... | collective-permute-start | bytes 196616 | tf_op jit(solution)/shard_map/ppermute | solution.py:325
  24.1 7.9 %collective-permute-start.23 = (bf16[8,32,128]{2,1,0:T(8,128)(2,1)S(1)}, bf16[8,32,128]{2,1,0:T(8,128)(2,1)S(1)}, u32[]{:S(2)}, u32[]{:S(2)}) collective-permute-start(bf16[8,32,128]{2,1,0:T(8,128)(2,1)S(1)} %get-tuple-element.157), channel_id=1, source_target_pairs={{0,12},{4,0},{8,4},{12,8},{1,13},{5,1},{9,5},{13,9},{2,14},{6,2},{... | collective-permute-start | bytes 196616 | tf_op jit(solution)/shard_map/ppermute | solution.py:325
  27.0 8.7 %collective-permute-start.24 = (bf16[8,32,128]{2,1,0:T(8,128)(2,1)S(1)}, bf16[8,32,128]{2,1,0:T(8,128)(2,1)S(1)}, u32[]{:S(2)}, u32[]{:S(2)}) collective-permute-start(bf16[8,32,128]{2,1,0:T(8,128)(2,1)S(1)} %get-tuple-element.158), channel_id=1, source_target_pairs={{0,8},{4,12},{8,0},{12,4},{1,9},{5,13},{9,1},{13,5},{2,10},{6,14},... | collective-permute-start | bytes 196616 | tf_op jit(solution)/shard_map/ppermute | solution.py:325
  27.9 7.8 %collective-permute-start.25 = (bf16[8,32,128]{2,1,0:T(8,128)(2,1)S(1)}, bf16[8,32,128]{2,1,0:T(8,128)(2,1)S(1)}, u32[]{:S(2)}, u32[]{:S(2)}) collective-permute-start(bf16[8,32,128]{2,1,0:T(8,128)(2,1)S(1)} %get-tuple-element.159), channel_id=1, source_target_pairs={{0,4},{4,8},{8,12},{12,0},{1,5},{5,9},{9,13},{13,1},{2,6},{6,10},{... | collective-permute-start | bytes 196616 | tf_op jit(solution)/shard_map/ppermute | solution.py:325
  29.8 8.0 %collective-permute-start.16 = (bf16[8,32,128]{2,1,0:T(8,128)(2,1)S(1)}, bf16[8,32,128]{2,1,0:T(8,128)(2,1)S(1)}, u32[]{:S(2)}, u32[]{:S(2)}) collective-permute-start(bf16[8,32,128]{2,1,0:T(8,128)(2,1)S(1)} %get-tuple-element.135), channel_id=1, source_target_pairs={{0,12},{4,0},{8,4},{12,8},{1,13},{5,1},{9,5},{13,9},{2,14},{6,2},{... | collective-permute-start | bytes 196616 | tf_op jit(solution)/shard_map/ppermute | solution.py:325
  31.7 6.7 %collective-permute-start.17 = (bf16[8,32,128]{2,1,0:T(8,128)(2,1)S(1)}, bf16[8,32,128]{2,1,0:T(8,128)(2,1)S(1)}, u32[]{:S(2)}, u32[]{:S(2)}) collective-permute-start(bf16[8,32,128]{2,1,0:T(8,128)(2,1)S(1)} %get-tuple-element.136), channel_id=1, source_target_pairs={{0,8},{4,12},{8,0},{12,4},{1,9},{5,13},{9,1},{13,5},{2,10},{6,14},... | collective-permute-start | bytes 196616 | tf_op jit(solution)/shard_map/ppermute | solution.py:325
  32.0 6.4 %collective-permute-start.18 = (bf16[8,32,128]{2,1,0:T(8,128)(2,1)S(1)}, bf16[8,32,128]{2,1,0:T(8,128)(2,1)S(1)}, u32[]{:S(2)}, u32[]{:S(2)}) collective-permute-start(bf16[8,32,128]{2,1,0:T(8,128)(2,1)S(1)} %get-tuple-element.137), channel_id=1, source_target_pairs={{0,4},{4,8},{8,12},{12,0},{1,5},{5,9},{9,13},{13,1},{2,6},{6,10},{... | collective-permute-start | bytes 196616 | tf_op jit(solution)/shard_map/ppermute | solution.py:325
  36.3 5.2 %collective-permute-start.26 = (bf16[2,32,128]{2,1,0:T(8,128)(2,1)S(1)}, bf16[2,32,128]{2,1,0:T(8,128)(2,1)S(1)}, u32[]{:S(2)}, u32[]{:S(2)}) collective-permute-start(bf16[2,32,128]{2,1,0:T(8,128)(2,1)S(1)} %get-tuple-element.167), channel_id=1, source_target_pairs={{0,2},{2,0},{1,3},{3,1},{4,6},{6,4},{5,7},{7,5},{8,10},{10,8},{9,1... | collective-permute-start | bytes 49160 | tf_op jit(solution)/shard_map/ppermute | solution.py:289
  39.1 3.8 %collective-permute-start.19 = (bf16[2,32,128]{2,1,0:T(8,128)(2,1)S(1)}, bf16[2,32,128]{2,1,0:T(8,128)(2,1)S(1)}, u32[]{:S(2)}, u32[]{:S(2)}) collective-permute-start(bf16[2,32,128]{2,1,0:T(8,128)(2,1)S(1)} %get-tuple-element.145), channel_id=1, source_target_pairs={{0,2},{2,0},{1,3},{3,1},{4,6},{6,4},{5,7},{7,5},{8,10},{10,8},{9,1... | collective-permute-start | bytes 49160 | tf_op jit(solution)/shard_map/ppermute | solution.py:289

commit v5 on v4

v5 whole, which is shorter than its diff:
```python
import functools

import jax
import jax.numpy as jnp
from jax import lax
from jax.experimental import pallas as pl
from jax.experimental.pallas import tpu as pltpu
from jax.sharding import PartitionSpec as P

HR = 2
CAP = 11
BASE = 8
SPARE = CAP - BASE
PARTS = 2
STRIDE = 16
TRASH = STRIDE - 2
COUNT = STRIDE - 1
BF16 = jnp.bfloat16
F32 = jnp.float32
VMEM = pltpu.VMEM
SMEM = pltpu.SMEM


def whole(space):
    return pl.BlockSpec(memory_space=space)


def wrap(value, size):
    return jnp.where(value < 0, value + size, value)


def prepare_kernel(bands, fields_hbm, rows_ref, *rest):
    *edges, held, wide, sems = rest
    rows, channels, _ = rows_ref.shape
    chunk = 16
    copies = []
    for i, c in enumerate(range(0, channels, chunk)):
        span = pl.ds(c * rows, chunk * rows)
        copies.append(pltpu.make_async_copy(fields_hbm.at[span], held.at[span], sems.at[i]))
        copies[-1].start()
    for i, c in enumerate(range(0, channels, chunk)):
        copies[i].wait()
        span = slice(c * rows, (c + chunk) * rows)
        wide[span] = held[span].astype(F32)
        for r in range(rows):
            rows_ref[r, c : c + chunk] = wide[pl.ds(c * rows + r, chunk, stride=rows), :].astype(BF16)
    if bands == 2:
        start = jnp.where(lax.axis_index("lat") == 0, rows - HR, 0)
        edges[0][...] = rows_ref[pl.ds(start, HR)]
    else:
        edges[0][...] = rows_ref[0:HR]
        edges[1][...] = rows_ref[rows - HR : rows]


def entry_of(lists_ref, number_ref, a, r, k, rows):
    used = k < number_ref[0, a, r]
    owner = jnp.where(used, lists_ref[0, a, 0, k, r], -1)
    return owner, HR + lists_ref[0, a, 1, k, r] * rows + lists_ref[0, a, 2, k, r]


def send_kernel(tiles, rows, per_row, lists_ref, number_ref, send_ref):
    me = lax.axis_index("lon")

    def scan(d):
        a = wrap(me + d - tiles, tiles)
        for s in range(CAP):
            send_ref[d * STRIDE + s] = rows + 2 * HR
        filled = jnp.int32(0)
        for r in range(rows):
            for k in range(per_row):
                owner, row = entry_of(lists_ref, number_ref, a, r, k, rows)
                send_ref[d * STRIDE + jnp.where(owner == me, filled, TRASH)] = row
                filled = filled + jnp.where(owner == me, 1, 0)
        send_ref[d * STRIDE + COUNT] = filled

    if tiles <= 4:
        for d in range(1, tiles):
            scan(d)
    else:
        pl.loop(1, tiles)(scan)


def pack_kernel(tiles, width, send_ref, rows_ref, before_ref, after_ref, ext_ref, *rest):
    n = tiles - 1
    middle = tiles // 2
    base, halves, spare = rest[: n - 1], rest[n - 1 : n - 1 + PARTS], rest[n - 1 + PARTS :]
    rows = rows_ref.shape[0]
    ext_ref[0:HR] = before_ref[...]
    ext_ref[HR : HR + rows] = rows_ref[...]
    ext_ref[HR + rows : HR + rows + HR] = after_ref[...]
    whole_distances = [d for d in range(1, tiles) if d != middle]
    for s in range(BASE):
        block = ext_ref[send_ref[middle * STRIDE + s]]
        for i in range(PARTS):
            halves[i][s] = block[i * width : (i + 1) * width]
    for d, out in zip(whole_distances, base):
        for s in range(BASE):
            out[s] = ext_ref[send_ref[d * STRIDE + s]]
    for d in range(1, tiles):

        @pl.when(send_ref[d * STRIDE + COUNT] > BASE)
        def _():
            for s in range(SPARE):
                spare[d - 1][s] = ext_ref[send_ref[d * STRIDE + BASE + s]]


def arrival_kernel(tiles, per_row, lists_ref, number_ref, cot_ref, taps_ref, *rest):
    cot_rows_ref, mix_ref, place_ref, own_ref, needed_ref, wide, taken = rest
    rows, channels, cols = cot_rows_ref.shape
    me = lax.axis_index("lon")
    entries = rows * per_row
    dump = rows + 2 * HR
    for s in range(CAP):
        own_ref[s] = dump

    def place(r, k, owner, row, d, count):
        used = owner >= 0
        own = owner == me
        slot = d * STRIDE + count
        source = jnp.where(own, tiles * STRIDE + row, slot)
        place_ref[r * per_row + k] = jnp.where(used, source, tiles * STRIDE + dump)
        place_ref[entries + r * per_row + k] = jnp.where(used, slot, tiles * STRIDE)
        own_ref[jnp.where(own, count, TRASH)] = row

    if tiles <= 4:

        def add_up(owner, counts):
            return [count + jnp.where(owner == o, 1, 0) for o, count in enumerate(counts)]

        most = jnp.int32(0)
        for d in range(1, tiles):
            a = wrap(me + d - tiles, tiles)
            counts = [jnp.int32(0)] * tiles
            for r in range(rows):
                for k in range(per_row):
                    counts = add_up(entry_of(lists_ref, number_ref, a, r, k, rows)[0], counts)
            for o in range(tiles):
                most = jnp.maximum(most, jnp.where(a == o, 0, counts[o]))
        counts = [jnp.int32(0)] * tiles
        for r in range(rows):
            for k in range(per_row):
                owner, row = entry_of(lists_ref, number_ref, me, r, k, rows)
                count = sum(jnp.where(owner == o, counts[o], 0) for o in range(tiles))
                place(r, k, owner, row, wrap(me - owner, tiles), count)
                counts = add_up(owner, counts)
        for o in range(tiles):
            place_ref[2 * entries + wrap(me - o, tiles)] = counts[o]
            most = jnp.maximum(most, jnp.where(me == o, 0, counts[o]))
        needed_ref[0] = jnp.where(most > BASE, 1, 0)
    else:
        for d in range(tiles + 1):
            taken[d] = 0

        @pl.loop(0, rows)
        def _(r):
            for k in range(per_row):
                owner, row = entry_of(lists_ref, number_ref, me, r, k, rows)
                d = jnp.where(owner >= 0, wrap(me - owner, tiles), tiles)
                place(r, k, owner, row, d, taken[d])
                taken[d] = taken[d] + 1

        for d in range(tiles):
            place_ref[2 * entries + d] = taken[d]
        needed_ref[0] = 0

    wide[...] = cot_ref[...].astype(F32)
    for r in range(rows):
        cot_rows_ref[r] = wide[pl.ds(r, channels, stride=rows), :].astype(BF16)
    w0, w1, w2, w3 = (taps_ref[j] for j in range(4))
    cell = lax.broadcasted_iota(jnp.int32, w0.shape, 1)
    first, last, late = cell == 0, cell == cols - 1, cell == cols - 2
    mix_ref[0] = pltpu.roll(jnp.where(first, 0.0, w0), cols - 1, 1)
    mix_ref[1] = w1 + jnp.where(first, w0, 0.0) + jnp.where(last, w2 + w3, 0.0)
    mix_ref[2] = pltpu.roll(jnp.where(last, 0.0, w2) + jnp.where(late, w3, 0.0), 1, 1)
    mix_ref[3] = pltpu.roll(jnp.where(last | late, 0.0, w3), 2, 1)


def compute_kernel(tiles, per_row, start, width, place_ref, mix_ref, cot_ref, ext_ref, *rest):
    n = tiles - 1
    middle = tiles // 2
    whole_distances = [d for d in range(1, tiles) if d != middle]
    base, half, spare, rest = rest[: n - 1], rest[n - 1], rest[n : 2 * n], rest[2 * n :]
    if start > 0:
        rest = rest[2 * n :]
    own_out, base_out, spare_out, rest = rest[0], rest[1:n], rest[n : 2 * n], rest[2 * n :]
    half_out, grad_ref, blocks, terms = rest
    rows, _, cols = cot_ref.shape
    entries = rows * per_row
    ext = rows + 2 * HR
    part = min(width, 32)
    mine = slice(start, start + width)
    blocks[tiles * STRIDE : tiles * STRIDE + ext] = ext_ref[0:ext, mine]
    blocks[tiles * STRIDE + ext] = jnp.zeros((width, cols), BF16)
    blocks[middle * STRIDE : middle * STRIDE + BASE] = half[...]
    for d, arrived in zip(whole_distances, base):
        blocks[d * STRIDE : d * STRIDE + BASE] = arrived[:, mine]
    for d in range(1, tiles):

        @pl.when(place_ref[2 * entries + d] > BASE)
        def _():
            blocks[d * STRIDE + BASE : d * STRIDE + CAP] = spare[d - 1][:, mine]

    def row(r, _):
        source = [place_ref[r * per_row + k] for k in range(per_row)]
        target = [place_ref[entries + r * per_row + k] for k in range(per_row)]
        mix = [[mix_ref[j, pl.ds(r * per_row + k, 1), :] for j in range(4)] for k in range(per_row)]
        for lo in range(0, width, part):
            block = [blocks[source[k], lo : lo + part].astype(F32) for k in range(per_row)]
            tap = [sum(block[k] * mix[k][j] for k in range(per_row)) for j in range(4)]
            interp = (tap[1] + pltpu.roll(tap[0], 1, 1)) + (
                pltpu.roll(tap[2], cols - 1, 1) + pltpu.roll(tap[3], cols - 2, 1)
            )
            bent = jnp.tanh(interp)
            scaled = cot_ref[r, start + lo : start + lo + part].astype(F32) * (2.0 - bent * bent)
            scaled = scaled.astype(BF16).astype(F32)
            moved = [
                pltpu.roll(scaled, cols - 1, 1),
                scaled,
                pltpu.roll(scaled, 1, 1),
                pltpu.roll(scaled, 2, 1),
            ]
            for k in range(per_row):
                term = (moved[0] * mix[k][0] + moved[1] * mix[k][1]) + (
                    moved[2] * mix[k][2] + moved[3] * mix[k][3]
                )
                terms[target[k], lo : lo + part] = term.astype(BF16)
                for j in range(4):
                    at = (r * per_row + k) * 4 + j
                    product = jnp.sum((block[k] * moved[j]).reshape(part // 8, 8, cols), axis=0)
                    grad_ref[at] = product if lo == 0 else grad_ref[at] + product
        return 0

    lax.fori_loop(0, rows, row, 0, unroll=4)
    half_out[...] = terms[middle * STRIDE : middle * STRIDE + BASE]
    for d, out in zip(whole_distances, base_out):
        out[:, mine] = terms[d * STRIDE : d * STRIDE + BASE]
    for d in range(1, tiles):

        @pl.when(place_ref[2 * entries + d] > BASE)
        def _():
            spare_out[d - 1][:, mine] = terms[d * STRIDE + BASE : d * STRIDE + CAP]

    own_out[:, mine] = terms[0:CAP]


def gradient_kernel(*refs):
    *partial_refs, out_ref = refs
    sums = jnp.sum(sum(ref[...] for ref in partial_refs), axis=1)
    count, cols = sums.shape
    tap = lax.broadcasted_iota(jnp.int32, sums.shape, 0) & 3
    cell = lax.broadcasted_iota(jnp.int32, sums.shape, 1)
    grads = jnp.where(tap == 0, pltpu.roll(sums, 1, 1), sums)
    grads = jnp.where(tap == 2, pltpu.roll(sums, cols - 1, 1), grads)
    grads = jnp.where(tap == 3, pltpu.roll(sums, cols - 2, 1), grads)
    following = pltpu.roll(grads, count - 1, 0)
    previous = pltpu.roll(grads, 1, 0)
    second = pltpu.roll(grads, 2, 0)
    fixed = jnp.where((tap == 0) & (cell == 0), following, grads)
    fixed = jnp.where((tap == 2) & (cell == cols - 1), previous, fixed)
    fixed = jnp.where((tap == 3) & (cell == cols - 2), previous, fixed)
    fixed = jnp.where((tap == 3) & (cell == cols - 1), second, fixed)
    out_ref[...] = fixed.astype(BF16)


def add_own_kernel(table_ref, own_ref, total_ref):
    total_ref[...] = jnp.zeros_like(total_ref)
    for s in range(CAP):
        at = table_ref[s]
        total_ref[at] = total_ref[at] + own_ref[s].astype(F32)


def slot_refs(tiles, base, halves, spare):
    middle = tiles // 2
    whole_distances = [d for d in range(1, tiles) if d != middle]
    out = [(d, 0, BASE, 0, ref) for d, ref in zip(whole_distances, base)]
    width = halves[0].shape[1]
    out += [(middle, 0, BASE, i * width, ref) for i, ref in enumerate(halves)]
    return out, [(d, BASE, SPARE, 0, ref) for d, ref in enumerate(spare, 1)]


def edge_kernel(tiles, bands, send_ref, total_ref, *rest):
    n = tiles - 1
    base, halves, spare, edges = rest[: n - 1], rest[n - 1 : n - 1 + PARTS], rest[n - 1 + PARTS : 2 * n - 1 + PARTS], rest[2 * n - 1 + PARTS :]
    *edges, sums = edges
    ext = total_ref.shape[0] - 1
    if bands == 2:
        starts = [jnp.where(lax.axis_index("lat") == 0, ext - HR, 0)]
    else:
        starts = [0, ext - HR]
    always, seldom = slot_refs(tiles, base, halves, spare)
    wanted = [(e, h) for e in range(len(starts)) for h in range(HR)]
    for e, h in wanted:
        sums[e, h] = total_ref[starts[e] + h]

    def gather(refs):
        for d, first, slots, channel, ref in refs:
            part = slice(channel, channel + ref.shape[1])
            for c in range(part.start, part.stop, 16):
                found = [sums[e, h, c : c + 16] for e, h in wanted]
                for s in range(slots):
                    at = send_ref[d * STRIDE + first + s]
                    value = ref[s, c - channel : c - channel + 16].astype(F32)
                    found = [
                        jnp.where(at == starts[e] + h, total + value, total)
                        for (e, h), total in zip(wanted, found)
                    ]
                for (e, h), total in zip(wanted, found):
                    sums[e, h, c : c + 16] = total

    gather(always)
    for item in seldom:

        @pl.when(send_ref[item[0] * STRIDE + COUNT] > BASE)
        def _():
            gather([item])

    for e, edge in enumerate(edges):
        edge[...] = sums[e].astype(BF16)


def add_kernel(tiles, send_ref, _, *rest):
    n = tiles - 1
    base, halves, spare, (total_ref,) = rest[: n - 1], rest[n - 1 : n - 1 + PARTS], rest[n - 1 + PARTS : 2 * n - 1 + PARTS], rest[2 * n - 1 + PARTS :]
    always, seldom = slot_refs(tiles, base, halves, spare)

    def gather(d, first, slots, channel, ref):
        part = slice(channel, channel + ref.shape[1])
        for s in range(slots):
            at = send_ref[d * STRIDE + first + s]
            total_ref[at, part] = total_ref[at, part] + ref[s].astype(F32)

    for item in always:
        gather(*item)
    for item in seldom:
        pl.when(send_ref[item[0] * STRIDE + COUNT] > BASE)(functools.partial(gather, *item))


def finish_kernel(bands, rows, total_ref, above_ref, below_ref, out_hbm, held, sems):
    channels = total_ref.shape[1]
    band = lax.axis_index("lat")
    chunk = 16
    copies = []
    for i, c in enumerate(range(0, channels, chunk)):
        part = slice(c, c + chunk)
        for r in range(rows):
            value = total_ref[HR + r, part]
            if r < HR:
                value = value + jnp.where(band > 0, above_ref[r, part].astype(F32), 0.0)
            if r >= rows - HR:
                below = below_ref[r - rows + HR, part].astype(F32)
                value = value + jnp.where(band < bands - 1, below, 0.0)
            held[pl.ds(c * rows + r, chunk, stride=rows), :] = value
        source = held.at[pl.ds(c * rows, chunk * rows)]
        target = out_hbm.at[pl.ds(c * rows, chunk * rows)]
        copies.append(pltpu.make_async_copy(source, target, sems.at[i]))
        copies[-1].start()
    for copy in copies:
        copy.wait()


def swap_lat(edges, bands):
    if bands == 2:
        got = lax.ppermute(edges[0], "lat", [(0, 1), (1, 0)])
        return got, got
    down = [(i, i + 1) for i in range(bands - 1)]
    up = [(i + 1, i) for i in range(bands - 1)]
    return lax.ppermute(edges[1], "lat", down), lax.ppermute(edges[0], "lat", up)


def local(fields, arrival_cot, weights, departures, counts):
    lev_dev, field_count, rows, cols = fields.shape
    channels = lev_dev * field_count
    tiles = lax.axis_size("lon")
    bands = lax.axis_size("lat")
    per_row, taps = weights.shape[3], weights.shape[4]
    entries = rows * per_row
    ext = rows + 2 * HR
    partners = tiles - 1
    middle = tiles // 2
    whole_distances = [d for d in range(1, tiles) if d != middle]
    width = channels // PARTS
    params = pltpu.CompilerParams(vmem_limit_bytes=48 * 1024 * 1024)

    def call(kernel, out_shape, in_specs, out_specs, scratch=(), name=None, aliases={}):
        return pl.pallas_call(
            kernel,
            out_shape=out_shape,
            in_specs=in_specs,
            out_specs=out_specs,
            scratch_shapes=list(scratch),
            compiler_params=params,
            input_output_aliases=aliases,
            name=name,
        )

    def array(*shape, dtype=BF16):
        return jax.ShapeDtypeStruct(shape, dtype)

    def move(part, d):
        return lax.ppermute(part, "lon", [(i, (i + d) % tiles) for i in range(tiles)])

    def move_all(parts, sign):
        return [move(part, sign * d) for d, part in enumerate(parts, 1)]

    def move_spare(parts, sign):
        return lax.cond(needed, lambda parts: move_all(parts, sign), lambda parts: parts, list(parts))

    def move_whole(parts, sign):
        return [move(part, sign * d) for d, part in zip(whole_distances, parts)]

    lists = jnp.transpose(departures, (0, 2, 4, 3, 1))
    number = jnp.transpose(counts, (0, 2, 1))

    edge_count = 1 if bands == 2 else 2
    edge = (array(HR, channels, cols),) * edge_count
    base_slots = (array(BASE, channels, cols),) * (partners - 1)
    half_slots = array(BASE, width, cols)
    spare_slots = (array(SPARE, channels, cols),) * partners

    def hbm(value):
        return pltpu.with_memory_space_constraint(value, pltpu.HBM)

    row_blocks, *edges = call(
        functools.partial(prepare_kernel, bands),
        (array(rows, channels, cols),) + edge,
        [whole(pltpu.HBM)],
        (whole(VMEM),) * (1 + edge_count),
        [
            VMEM((channels * rows, cols), BF16),
            VMEM((channels * rows, cols), F32),
            pltpu.SemaphoreType.DMA((channels // 16,)),
        ],
        "prepare",
    )(hbm(fields.reshape(channels * rows, cols)))
    before, after = swap_lat(edges, bands)

    send_rows = call(
        functools.partial(send_kernel, tiles, rows, per_row),
        array(tiles * STRIDE, dtype=jnp.int32),
        [whole(SMEM)] * 2,
        whole(SMEM),
        (),
        "send",
    )(lists, number)
    ext_blocks, *rest = call(
        functools.partial(pack_kernel, tiles, width),
        (array(ext + 1, channels, cols),) + base_slots + (half_slots,) * PARTS + spare_slots,
        [whole(SMEM)] + [whole(VMEM)] * 3,
        (whole(VMEM),) * (2 * partners + PARTS),
        (),
        "pack",
    )(send_rows, row_blocks, before, after)
    base, halves, spare = (
        rest[: partners - 1],
        rest[partners - 1 : partners - 1 + PARTS],
        rest[partners - 1 + PARTS :],
    )
    halves = [move(half, middle) for half in halves]
    base = move_whole(base, 1)

    mixing = weights.reshape(rows, per_row, taps, cols).astype(F32)
    mixing = jnp.transpose(mixing, (2, 0, 1, 3)).reshape(taps, entries, cols)
    cot_rows, mix, places, own_table, needed = call(
        functools.partial(arrival_kernel, tiles, per_row),
        (
            array(rows, channels, cols),
            array(taps, entries, cols, dtype=F32),
            array(2 * entries + tiles, dtype=jnp.int32),
            array(STRIDE, dtype=jnp.int32),
            array(1, dtype=jnp.int32),
        ),
        [whole(SMEM), whole(SMEM), whole(VMEM), whole(VMEM)],
        (whole(VMEM), whole(VMEM), whole(SMEM), whole(SMEM), whole(SMEM)),
        [VMEM((channels * rows, cols), F32), SMEM((tiles + 1,), jnp.int32)],
        "arrival",
    )(lists, number, arrival_cot.reshape(channels * rows, cols), mixing)
    if tiles <= 4:
        needed = needed[0] > 0
    else:
        tile = jnp.arange(tiles, dtype=jnp.int32)
        entry = jnp.arange(per_row, dtype=jnp.int32)
        named = (entry[:, None] < number[0][:, None, :]) & (lists[0, :, 0] == tile[:, None, None, None])
        filled = jnp.sum(jnp.where(named, 1, 0), axis=(2, 3))
        needed = jnp.any((filled > BASE) & (tile[None, :] != tile[:, None]))
    spare = move_spare(spare, 1)

    filling = (array(CAP, channels, cols),) + base_slots + spare_slots
    began, back, partial = [], [], []
    for i in range(PARTS):
        inputs = 4 + 2 * partners
        *began, half, sums = call(
            functools.partial(compute_kernel, tiles, per_row, i * width, width),
            filling + (half_slots, array(entries * taps, 8, cols, dtype=F32)),
            [whole(SMEM)] + [whole(VMEM)] * (inputs - 1 + len(began)),
            (whole(VMEM),) * (len(filling) + 2),
            [
                VMEM((tiles * STRIDE + ext + 1, width, cols), BF16),
                VMEM((tiles * STRIDE + 1, width, cols), BF16),
            ],
            "compute",
            {inputs + j: j for j in range(len(began))},
        )(places, mix, cot_rows, ext_blocks, *base, halves[i], *spare, *began)
        back.append(move(half, -middle))
        partial.append(sums)
    own, base, spare = began[0], move_whole(began[1:partners], -1), move_spare(began[partners:], -1)

    sums = array(ext + 1, channels, cols, dtype=F32)
    total = call(add_own_kernel, sums, [whole(SMEM), whole(VMEM)], whole(VMEM), (), "add_own")(
        own_table, own
    )
    returned = [*base, *back, *spare]
    edges = call(
        functools.partial(edge_kernel, tiles, bands),
        edge,
        [whole(SMEM)] + [whole(VMEM)] * (1 + len(returned)),
        (whole(VMEM),) * edge_count,
        [VMEM((edge_count, HR, channels, cols), F32)],
        "edges",
    )(send_rows, total, *returned)
    from_above, from_below = swap_lat(edges, bands)
    total = call(
        functools.partial(add_kernel, tiles),
        sums,
        [whole(SMEM)] + [whole(VMEM)] * (1 + len(returned)),
        whole(VMEM),
        (),
        "add",
        {1: 0},
    )(send_rows, lax.optimization_barrier((total, edges[0]))[0], *returned)
    source = call(
        functools.partial(finish_kernel, bands, rows),
        array(channels * rows, cols, dtype=F32),
        [whole(VMEM)] * 3,
        whole(pltpu.HBM),
        [VMEM((channels * rows, cols), F32), pltpu.SemaphoreType.DMA((channels // 16,))],
        "finish",
    )(total, from_above, from_below)

    *partial, _ = lax.optimization_barrier((*partial, edges[0]))
    weight_grad = call(
        gradient_kernel,
        array(entries * taps, cols),
        [whole(VMEM)] * PARTS,
        whole(VMEM),
        (),
        "gradient",
    )(*partial)
    return source.reshape(fields.shape), weight_grad.reshape(weights.shape)


def solution(mesh):
    return jax.shard_map(
        local,
        mesh=mesh,
        in_specs=(
            P("lev", "ens", "lat", "lon"),
            P("lev", "ens", "lat", "lon"),
            P("lev", "lat", "lon", "ens", None, None),
            P("lev", "lat", None, "ens", None),
            P("lev", "lat", "ens"),
        ),
        out_specs=(P("lev", "ens", "lat", "lon"), P("lev", "lat", "lon", "ens", None, None)),
        check_vma=False,
    )
```

time: 43.8 us -> 42.9 us (0.979)
  waiting for transfers between devices: 3.85 us -> 10.9 us
  starting transfers between devices: 23.3 us -> 17.4 us
  other arithmetic: 0.8 us -> 0.01 us
  local copies, waits for them, and re-layouts: 0.73 us -> 0.06 us
  Pallas kernels: 13.5 us -> 13 us
    ppermute x12 -> x8, waiting for transfers between devices: 2.21 us -> 9.89 us  [move(): lax.ppermute(part, 'lon', [(i, (i + d) % tiles) for i in range(tiles)])]
    ppermute x12 -> x8, starting transfers between devices: 17.1 us -> 12.9 us  [move(): lax.ppermute(part, 'lon', [(i, (i + d) % tiles) for i in range(tiles)])]
    ppermute x3 -> x2, starting transfers between devices: 6.12 us -> 4.44 us  [swap_lat(): got = lax.ppermute(edges[0], 'lat', [(0, 1), (1, 0)])]
    ppermute x3 -> x2, waiting for transfers between devices: 1.64 us -> 0.96 us  [swap_lat(): got = lax.ppermute(edges[0], 'lat', [(0, 1), (1, 0)])]
    unnamed x8, local copies, waits for them, and re-layouts: 0.69 us -> 0.02 us
    reduce_or x1 -> x0, other arithmetic: 0.63 us -> none  [local(): needed = jnp.any((filled > BASE) & (tile[None, :] != tile[:, None]))]
    pallas_call x2 -> x1, Pallas kernels: 1.22 us -> 0.64 us  [local(): call(add_own_kernel, sums, [whole(SMEM), whole(VMEM)], whole(VMEM), (), '...]
    pallas_call x1, Pallas kernels: 2 us -> 2.5 us  [local(): call(functools.partial(arrival_kernel, tiles, per_row), (array(rows, chan...]
  transfers between devices with their start and end apart: 15 -> 10, of which waited for: 4 -> 4; matrix products, arithmetic and copies ran while one was open for 2% -> 0% of each run, Pallas kernels for 22% -> 15%
where the time goes in v5:
time: 42.9 us; the launch traced here: 42.7 us
  starting transfers between devices  17.4 us (41%)
  Pallas kernels  13 us (30%)
  waiting for transfers between devices  10.9 us (25%)
  between operations  1.43 us (3%)
    ppermute x8, starting transfers between devices, move(): lax.ppermute(part, 'lon', [(i, (i + d) % tiles) for i in range(tiles)])  12.9 us
    ppermute x8, waiting for transfers between devices, move(): lax.ppermute(part, 'lon', [(i, (i + d) % tiles) for i in range(tiles)])  9.89 us
    ppermute x2, starting transfers between devices, swap_lat(): got = lax.ppermute(edges[0], 'lat', [(0, 1), (1, 0)])  4.44 us
    pallas_call x2, Pallas kernels, local(): call(functools.partial(compute_kernel, tiles, per_row, i * width, width),...  3.05 us
    pallas_call x1, Pallas kernels, local(): call(functools.partial(arrival_kernel, tiles, per_row), (array(rows, chan...  2.5 us
    pallas_call x1, Pallas kernels, local(): call(functools.partial(send_kernel, tiles, rows, per_row), array(tiles *...  1.92 us
    pallas_call x1, Pallas kernels, local(): call(functools.partial(prepare_kernel, bands), (array(rows, channels, col...  1.1 us
    ppermute x2, waiting for transfers between devices, swap_lat(): got = lax.ppermute(edges[0], 'lat', [(0, 1), (1, 0)])  0.96 us
  transfers between devices with their start and end apart: 10, of which 4 were waited for; matrix products, arithmetic and copies ran while one was open for 0% of the time, Pallas kernels for 15%

profile of v5, /device:TPU:0, one launch (start us, length us, event | category | flops | bytes accessed | tf_op | source)
XLA Modules:
  0.0 42.7 jit_solution(13453674124345435457)
XLA Ops:
  0.6 0.0 copy-start.1
  0.6 1.1 %prepare.1 = (bf16[16,64,128]{2,1,0:T(8,128)(2,1)S(1)}, bf16[2,64,128]{2,1,0:T(8,128)(2,1)S(1)}) custom-call(bf16[1024,128]{1,0:T(8,128)(2,1)} %bitcast.22), custom_call_target="tpu_custom_call" | custom-call | tf_op jit(solution)/shard_map/prepare/pallas_call | solution.py:423
  1.7 0.0 copy-start.2
  1.8 3.0 %collective-permute-start.6 = (bf16[2,64,128]{2,1,0:T(8,128)(2,1)S(1)}, bf16[2,64,128]{2,1,0:T(8,128)(2,1)S(1)}, u32[]{:S(2)}, u32[]{:S(2)}) collective-permute-start(bf16[2,64,128]{2,1,0:T(8,128)(2,1)S(1)} %get-tuple-element.77), channel_id=1, source_target_pairs={{0,2},{2,0},{1,3},{3,1},{4,6},{6,4},{5,7},{7,5},{8,10},{10,8},{9,1... | collective-permute-start | bytes 98312 | tf_op jit(solution)/shard_map/ppermute | solution.py:363
  4.8 0.0 copy-done.1
  4.8 0.0 copy-done.2
  4.8 1.9 %send.1.send_ref = s32[64]{0:T(128)S(1)} custom-call(s32[1,4,3,2,16]{4,3,2,1,0:T(2,128)S(1)} %bitcast.17, s32[1,4,16]{2,1,0:T(4,128)S(1)} %bitcast.19), custom_call_target="tpu_custom_call" | custom-call | tf_op jit(solution)/shard_map/send/pallas_call | solution.py:437
  6.7 0.0 collective-permute-done.6.before_ref.after_ref
  6.7 0.0 copy-start.3
  6.7 0.0 copy-start
  6.7 0.6 %pack.1 = (bf16[21,64,128]{2,1,0:T(8,128)(2,1)S(1)}, bf16[8,64,128]{2,1,0:T(8,128)(2,1)S(1)}, bf16[8,64,128]{2,1,0:T(8,128)(2,1)S(1)}, bf16[8,32,128]{2,1,0:T(8,...) custom-call(s32[64]{0:T(128)S(1)} %send.1.send_ref, ...), custom_call_target="tpu_custom_call" | custom-call | tf_op jit(solution)/shard_map/pack/pallas_call | solution.py:445
  7.3 2.1 %collective-permute-start.7 = (bf16[8,64,128]{2,1,0:T(8,128)(2,1)S(1)}, bf16[8,64,128]{2,1,0:T(8,128)(2,1)S(1)}, u32[]{:S(2)}, u32[]{:S(2)}) collective-permute-start(bf16[8,64,128]{2,1,0:T(8,128)(2,1)S(1)} %get-tuple-element.79), channel_id=1, source_target_pairs={{0,4},{4,8},{8,12},{12,0},{1,5},{5,9},{9,13},{13,1},{2,6},{6,10},{... | collective-permute-start | bytes 393224 | tf_op jit(solution)/shard_map/ppermute | solution.py:400
  9.4 2.1 %collective-permute-start.8 = (bf16[8,64,128]{2,1,0:T(8,128)(2,1)S(1)}, bf16[8,64,128]{2,1,0:T(8,128)(2,1)S(1)}, u32[]{:S(2)}, u32[]{:S(2)}) collective-permute-start(bf16[8,64,128]{2,1,0:T(8,128)(2,1)S(1)} %get-tuple-element.80), channel_id=1, source_target_pairs={{0,12},{4,0},{8,4},{12,8},{1,13},{5,1},{9,5},{13,9},{2,14},{6,2},{... | collective-permute-start | bytes 393224 | tf_op jit(solution)/shard_map/ppermute | solution.py:400
  11.5 0.0 copy-done.3
  11.6 0.0 copy-done
  11.6 2.5 %arrival.1 = (bf16[16,64,128]{2,1,0:T(8,128)(2,1)S(1)}, f32[4,32,128]{2,1,0:T(8,128)S(1)}, s32[68]{0:T(128)S(1)}, s32[16]{0:T(128)S(1)}, s32[1]{0:T(128)}) custom-call(s32[1,4,3,2,16]{4,3,2,1,0:T(2,128)S(1)} %bitcast.18, s32[1,4,16]{2,1,0:T(4,128)S(1)} %bitcast.20, bf16[1024,128]{1,0:T(8,128)(2,1)S(1)} %bitcast.15, f32[4,32,128]{2,1,0:T(8,128)S(1)} %bitcast.16), custom_call_target="tpu_custom_call" | custom-call | tf_op jit(solution)/shard_map/arrival/pallas_call | solution.py:463
  14.8 1.0 %collective-permute-start.10 = (bf16[8,32,128]{2,1,0:T(8,128)(2,1)S(1)}, bf16[8,32,128]{2,1,0:T(8,128)(2,1)S(1)}, u32[]{:S(2)}, u32[]{:S(2)}) collective-permute-start(bf16[8,32,128]{2,1,0:T(8,128)(2,1)S(1)} %get-tuple-element.89), channel_id=1, source_target_pairs={{0,8},{4,12},{8,0},{12,4},{1,9},{5,13},{9,1},{13,5},{2,10},{6,14},... | collective-permute-start | bytes 196616 | tf_op jit(solution)/shard_map/ppermute | solution.py:400
  15.8 2.0 %collective-permute-start.9 = (bf16[8,32,128]{2,1,0:T(8,128)(2,1)S(1)}, bf16[8,32,128]{2,1,0:T(8,128)(2,1)S(1)}, u32[]{:S(2)}, u32[]{:S(2)}) collective-permute-start(bf16[8,32,128]{2,1,0:T(8,128)(2,1)S(1)} %get-tuple-element.81), channel_id=1, source_target_pairs={{0,8},{4,12},{8,0},{12,4},{1,9},{5,13},{9,1},{13,5},{2,10},{6,14},... | collective-permute-start | bytes 196616 | tf_op jit(solution)/shard_map/ppermute | solution.py:400
  17.8 3.5 %collective-permute-done.10.rest_2_ = bf16[8,32,128]{2,1,0:T(8,128)(2,1)S(1)} collective-permute-done((bf16[8,32,128]{2,1,0:T(8,128)(2,1)S(1)}, bf16[8,32,128]{2,1,0:T(8,128)(2,1)S(1)}, u32[]{:S(2)}, u32[]{:S(2)}) %collective-permute-start.10) | collective-permute-done | bytes 65568 | tf_op jit(solution)/shard_map/ppermute | solution.py:400
  21.2 0.0 collective-permute-done.7.rest_0_
  21.2 0.0 collective-permute-done.8.rest_1_
  21.2 1.5 %compute.2 = (bf16[11,64,128]{2,1,0:T(8,128)(2,1)S(1)}, bf16[8,64,128]{2,1,0:T(8,128)(2,1)S(1)}, bf16[8,64,128]{2,1,0:T(8,128)(2,1)S(1)}, bf16[3,64,128]{2,1,0:T...) custom-call(s32[68]{0:T(128)S(1)} %get-tuple-element.73.place_ref, ...), custom_call_target="tpu_custom_call" | custom-call | tf_op jit(solution)/shard_map/compute/pallas_call | solution.py:491
  22.8 0.0 collective-permute-done.9.rest_2_
  22.8 1.5 %compute.3 = (bf16[11,64,128]{2,1,0:T(8,128)(2,1)S(1)}, bf16[8,64,128]{2,1,0:T(8,128)(2,1)S(1)}, bf16[8,64,128]{2,1,0:T(8,128)(2,1)S(1)}, bf16[3,64,128]{2,1,0:T...) custom-call(s32[68]{0:T(128)S(1)} %get-tuple-element.73.place_ref, ...), custom_call_target="tpu_custom_call", output_to_operand_aliasing={{0}: (10, {}), {1}: (11, {}), {2}: (12, {}), {3}: (13, {}),... | custom-call | tf_op jit(solution)/shard_map/compute/pallas_call | solution.py:491
  24.3 2.8 %collective-permute-start.11 = (bf16[8,64,128]{2,1,0:T(8,128)(2,1)S(1)}, bf16[8,64,128]{2,1,0:T(8,128)(2,1)S(1)}, u32[]{:S(2)}, u32[]{:S(2)}) collective-permute-start(bf16[8,64,128]{2,1,0:T(8,128)(2,1)S(1)} %get-tuple-element.97), channel_id=1, source_target_pairs={{0,12},{4,0},{8,4},{12,8},{1,13},{5,1},{9,5},{13,9},{2,14},{6,2},{... | collective-permute-start | bytes 393224 | tf_op jit(solution)/shard_map/ppermute | solution.py:400
  27.2 0.0 collective-permute-start.12
  27.2 0.6 %collective-permute-start.14 = (bf16[8,32,128]{2,1,0:T(8,128)(2,1)S(1)}, bf16[8,32,128]{2,1,0:T(8,128)(2,1)S(1)}, u32[]{:S(2)}, u32[]{:S(2)}) collective-permute-start(bf16[8,32,128]{2,1,0:T(8,128)(2,1)S(1)} %get-tuple-element.100), channel_id=1, source_target_pairs={{0,8},{4,12},{8,0},{12,4},{1,9},{5,13},{9,1},{13,5},{2,10},{6,14},... | collective-permute-start | bytes 196616 | tf_op jit(solution)/shard_map/ppermute | solution.py:400
  27.8 2.3 %collective-permute-start.13 = (bf16[8,32,128]{2,1,0:T(8,128)(2,1)S(1)}, bf16[8,32,128]{2,1,0:T(8,128)(2,1)S(1)}, u32[]{:S(2)}, u32[]{:S(2)}) collective-permute-start(bf16[8,32,128]{2,1,0:T(8,128)(2,1)S(1)} %get-tuple-element.99), channel_id=1, source_target_pairs={{0,8},{4,12},{8,0},{12,4},{1,9},{5,13},{9,1},{13,5},{2,10},{6,14},... | collective-permute-start | bytes 196616 | tf_op jit(solution)/shard_map/ppermute | solution.py:400
  30.1 0.6 %add_own.1.total_ref._ = f32[21,64,128]{2,1,0:T(8,128)S(1)} custom-call(s32[16]{0:T(128)S(1)} %get-tuple-element.72.table_ref, bf16[11,64,128]{2,1,0:T(8,128)(2,1)S(1)} %get-tuple-element.96.own_ref), custom_call_target="tpu_custom_call" | custom-call | tf_op jit(solution)/shard_map/add_own/pallas_call | solution.py:508
  30.7 5.7 %collective-permute-done.14.rest_3_ = bf16[8,32,128]{2,1,0:T(8,128)(2,1)S(1)} collective-permute-done((bf16[8,32,128]{2,1,0:T(8,128)(2,1)S(1)}, bf16[8,32,128]{2,1,0:T(8,128)(2,1)S(1)}, u32[]{:S(2)}, u32[]{:S(2)}) %collective-permute-start.14) | collective-permute-done | bytes 65568 | tf_op jit(solution)/shard_map/ppermute | solution.py:400
  36.4 0.7 %collective-permute-done.13.rest_2_ = bf16[8,32,128]{2,1,0:T(8,128)(2,1)S(1)} collective-permute-done((bf16[8,32,128]{2,1,0:T(8,128)(2,1)S(1)}, bf16[8,32,128]{2,1,0:T(8,128)(2,1)S(1)}, u32[]{:S(2)}, u32[]{:S(2)}) %collective-permute-start.13) | collective-permute-done | bytes 65568 | tf_op jit(solution)/shard_map/ppermute | solution.py:400
  37.1 0.0 collective-permute-done.11.rest_0_
  37.1 0.0 collective-permute-done.12.rest_1_
  37.2 0.7 %edges.1 = bf16[2,64,128]{2,1,0:T(8,128)(2,1)S(1)} custom-call(s32[64]{0:T(128)S(1)} %send.1.send_ref, f32[21,64,128]{2,1,0:T(8,128)S(1)} %add_own.1.total_ref._, bf16[8,64,128]{2,1,0:T(8,128)(2,1)S(1)} %collective-permute-done.11.rest_0_, bf16[8,64,128]{2,1,0:T(8,128)(2,1)S(1)} %collective-permute-done.12.rest_1_, ...), custom_call_target="tpu_custom_call" | custom-call | tf_op jit(solution)/shard_map/edges/pallas_call | solution.py:512
  37.9 1.4 %collective-permute-start.15 = (bf16[2,64,128]{2,1,0:T(8,128)(2,1)S(1)}, bf16[2,64,128]{2,1,0:T(8,128)(2,1)S(1)}, u32[]{:S(2)}, u32[]{:S(2)}) collective-permute-start(bf16[2,64,128]{2,1,0:T(8,128)(2,1)S(1)} %edges.1), channel_id=1, source_target_pairs={{0,2},{2,0},{1,3},{3,1},{4,6},{6,4},{5,7},{7,5},{8,10},{10,8},{9,1... | collective-permute-start | bytes 98312 | tf_op jit(solution)/shard_map/ppermute | solution.py:363
  39.3 0.9 %gradient.1 = bf16[128,128]{1,0:T(8,128)(2,1)} custom-call(f32[128,8,128]{2,1,0:T(8,128)S(1)} %get-tuple-element.110.refs_0_, f32[128,8,128]{2,1,0:T(8,128)S(1)} %get-tuple-element.111.refs_1_), custom_call_target="tpu_custom_call" | custom-call | tf_op jit(solution)/shard_map/gradient/pallas_call | solution.py:540
  40.2 0.7 %add.1.total_ref = f32[21,64,128]{2,1,0:T(8,128)S(1)} custom-call(s32[64]{0:T(128)S(1)} %send.1.send_ref, f32[21,64,128]{2,1,0:T(8,128)S(1)} %add_own.1.total_ref._, bf16[8,64,128]{2,1,0:T(8,128)(2,1)S(1)} %collective-permute-done.11.rest_0_, bf16[8,64,128]{2,1,0:T(8,128)(2,1)S(1)} %collective-permute-done.12.rest_1_, ...), custom_call_target="tpu_custom_call", output_to_operand_aliasing={{}: (1, {})} | custom-call | tf_op jit(solution)/shard_map/add/pallas_call | solution.py:521
  40.9 1.0 %collective-permute-done.15.above_ref.below_ref = bf16[2,64,128]{2,1,0:T(8,128)(2,1)S(1)} collective-permute-done((bf16[2,64,128]{2,1,0:T(8,128)(2,1)S(1)}, bf16[2,64,128]{2,1,0:T(8,128)(2,1)S(1)}, u32[]{:S(2)}, u32[]{:S(2)}) %collective-permute-start.15) | collective-permute-done | bytes 32800 | tf_op jit(solution)/shard_map/ppermute | solution.py:363
  41.9 0.9 %finish.1 = f32[1024,128]{1,0:T(8,128)} custom-call(f32[21,64,128]{2,1,0:T(8,128)S(1)} %add.1.total_ref, bf16[2,64,128]{2,1,0:T(8,128)(2,1)S(1)} %collective-permute-done.15.above_ref.below_ref, bf16[2,64,128]{2,1,0:T(8,128)(2,1)S(1)} %collective-permute-done.15.above_ref.below_ref), custom_call_target="tpu_custom_call" | custom-call | tf_op jit(solution)/shard_map/finish/pallas_call | solution.py:530
  (4 shorter events, 0.0 us)
Async XLA Ops:
  0.6 4.1 %copy-start.1 = (s32[1,16,4,2,3]{1,3,4,2,0:T(2,128)S(1)}, s32[1,16,4,2,3]{1,3,4,2,0:T(2,128)}, u32[]{:S(2)}) copy-start(s32[1,16,4,2,3]{1,3,4,2,0:T(2,128)} %param.12) | copy-start | bytes 4612
  1.7 3.0 %copy-start.2 = (s32[1,16,4]{1,2,0:T(4,128)S(1)}, s32[1,16,4]{1,2,0:T(4,128)}, u32[]{:S(2)}) copy-start(s32[1,16,4]{1,2,0:T(4,128)} %param.13) | copy-start | bytes 772
  1.8 4.9 %collective-permute-start.6 = (bf16[2,64,128]{2,1,0:T(8,128)(2,1)S(1)}, bf16[2,64,128]{2,1,0:T(8,128)(2,1)S(1)}, u32[]{:S(2)}, u32[]{:S(2)}) collective-permute-start(bf16[2,64,128]{2,1,0:T(8,128)(2,1)S(1)} %get-tuple-element.77), channel_id=1, source_target_pairs={{0,2},{2,0},{1,3},{3,1},{4,6},{6,4},{5,7},{7,5},{8,10},{10,8},{9,1... | collective-permute-start | bytes 98312 | tf_op jit(solution)/shard_map/ppermute | solution.py:363
  6.7 4.8 %copy-start.3 = (bf16[1,16,1,2,4,128]{5,4,3,2,1,0:T(4,128)(2,1)S(1)}, bf16[1,16,1,2,4,128]{5,4,3,2,1,0:T(4,128)(2,1)}, u32[]{:S(2)}) copy-start(bf16[1,16,1,2,4,128]{5,4,3,2,1,0:T(4,128)(2,1)} %param.11) | copy-start | bytes 98308
  6.7 4.9 %copy-start = (bf16[16,4,16,128]{3,2,1,0:T(8,128)(2,1)S(1)}, bf16[16,4,16,128]{3,2,1,0:T(8,128)(2,1)}, u32[]{:S(2)}) copy-start(bf16[16,4,16,128]{3,2,1,0:T(8,128)(2,1)} %param.10) | copy-start | bytes 786436
  7.3 13.9 %collective-permute-start.7 = (bf16[8,64,128]{2,1,0:T(8,128)(2,1)S(1)}, bf16[8,64,128]{2,1,0:T(8,128)(2,1)S(1)}, u32[]{:S(2)}, u32[]{:S(2)}) collective-permute-start(bf16[8,64,128]{2,1,0:T(8,128)(2,1)S(1)} %get-tuple-element.79), channel_id=1, source_target_pairs={{0,4},{4,8},{8,12},{12,0},{1,5},{5,9},{9,13},{13,1},{2,6},{6,10},{... | collective-permute-start | bytes 393224 | tf_op jit(solution)/shard_map/ppermute | solution.py:400
  9.4 11.8 %collective-permute-start.8 = (bf16[8,64,128]{2,1,0:T(8,128)(2,1)S(1)}, bf16[8,64,128]{2,1,0:T(8,128)(2,1)S(1)}, u32[]{:S(2)}, u32[]{:S(2)}) collective-permute-start(bf16[8,64,128]{2,1,0:T(8,128)(2,1)S(1)} %get-tuple-element.80), channel_id=1, source_target_pairs={{0,12},{4,0},{8,4},{12,8},{1,13},{5,1},{9,5},{13,9},{2,14},{6,2},{... | collective-permute-start | bytes 393224 | tf_op jit(solution)/shard_map/ppermute | solution.py:400
  14.8 6.5 %collective-permute-start.10 = (bf16[8,32,128]{2,1,0:T(8,128)(2,1)S(1)}, bf16[8,32,128]{2,1,0:T(8,128)(2,1)S(1)}, u32[]{:S(2)}, u32[]{:S(2)}) collective-permute-start(bf16[8,32,128]{2,1,0:T(8,128)(2,1)S(1)} %get-tuple-element.89), channel_id=1, source_target_pairs={{0,8},{4,12},{8,0},{12,4},{1,9},{5,13},{9,1},{13,5},{2,10},{6,14},... | collective-permute-start | bytes 196616 | tf_op jit(solution)/shard_map/ppermute | solution.py:400
  15.8 7.0 %collective-permute-start.9 = (bf16[8,32,128]{2,1,0:T(8,128)(2,1)S(1)}, bf16[8,32,128]{2,1,0:T(8,128)(2,1)S(1)}, u32[]{:S(2)}, u32[]{:S(2)}) collective-permute-start(bf16[8,32,128]{2,1,0:T(8,128)(2,1)S(1)} %get-tuple-element.81), channel_id=1, source_target_pairs={{0,8},{4,12},{8,0},{12,4},{1,9},{5,13},{9,1},{13,5},{2,10},{6,14},... | collective-permute-start | bytes 196616 | tf_op jit(solution)/shard_map/ppermute | solution.py:400
  24.3 12.8 %collective-permute-start.11 = (bf16[8,64,128]{2,1,0:T(8,128)(2,1)S(1)}, bf16[8,64,128]{2,1,0:T(8,128)(2,1)S(1)}, u32[]{:S(2)}, u32[]{:S(2)}) collective-permute-start(bf16[8,64,128]{2,1,0:T(8,128)(2,1)S(1)} %get-tuple-element.97), channel_id=1, source_target_pairs={{0,12},{4,0},{8,4},{12,8},{1,13},{5,1},{9,5},{13,9},{2,14},{6,2},{... | collective-permute-start | bytes 393224 | tf_op jit(solution)/shard_map/ppermute | solution.py:400
  27.2 10.0 %collective-permute-start.12 = (bf16[8,64,128]{2,1,0:T(8,128)(2,1)S(1)}, bf16[8,64,128]{2,1,0:T(8,128)(2,1)S(1)}, u32[]{:S(2)}, u32[]{:S(2)}) collective-permute-start(bf16[8,64,128]{2,1,0:T(8,128)(2,1)S(1)} %get-tuple-element.98), channel_id=1, source_target_pairs={{0,4},{4,8},{8,12},{12,0},{1,5},{5,9},{9,13},{13,1},{2,6},{6,10},{... | collective-permute-start | bytes 393224 | tf_op jit(solution)/shard_map/ppermute | solution.py:400
  27.2 9.3 %collective-permute-start.14 = (bf16[8,32,128]{2,1,0:T(8,128)(2,1)S(1)}, bf16[8,32,128]{2,1,0:T(8,128)(2,1)S(1)}, u32[]{:S(2)}, u32[]{:S(2)}) collective-permute-start(bf16[8,32,128]{2,1,0:T(8,128)(2,1)S(1)} %get-tuple-element.100), channel_id=1, source_target_pairs={{0,8},{4,12},{8,0},{12,4},{1,9},{5,13},{9,1},{13,5},{2,10},{6,14},... | collective-permute-start | bytes 196616 | tf_op jit(solution)/shard_map/ppermute | solution.py:400
  27.8 9.3 %collective-permute-start.13 = (bf16[8,32,128]{2,1,0:T(8,128)(2,1)S(1)}, bf16[8,32,128]{2,1,0:T(8,128)(2,1)S(1)}, u32[]{:S(2)}, u32[]{:S(2)}) collective-permute-start(bf16[8,32,128]{2,1,0:T(8,128)(2,1)S(1)} %get-tuple-element.99), channel_id=1, source_target_pairs={{0,8},{4,12},{8,0},{12,4},{1,9},{5,13},{9,1},{13,5},{2,10},{6,14},... | collective-permute-start | bytes 196616 | tf_op jit(solution)/shard_map/ppermute | solution.py:400
  37.9 4.0 %collective-permute-start.15 = (bf16[2,64,128]{2,1,0:T(8,128)(2,1)S(1)}, bf16[2,64,128]{2,1,0:T(8,128)(2,1)S(1)}, u32[]{:S(2)}, u32[]{:S(2)}) collective-permute-start(bf16[2,64,128]{2,1,0:T(8,128)(2,1)S(1)} %edges.1), channel_id=1, source_target_pairs={{0,2},{2,0},{1,3},{3,1},{4,6},{6,4},{5,7},{7,5},{8,10},{10,8},{9,1... | collective-permute-start | bytes 98312 | tf_op jit(solution)/shard_map/ppermute | solution.py:363

commit v6 on v5

--- a/solution.py
+++ b/solution.py
@@ -11,7 +11,7 @@
 CAP = 11
 BASE = 8
 SPARE = CAP - BASE
-PARTS = 2
+PARTS = 1
 STRIDE = 16
 TRASH = STRIDE - 2
 COUNT = STRIDE - 1
@@ -58,26 +58,43 @@
     return owner, HR + lists_ref[0, a, 1, k, r] * rows + lists_ref[0, a, 2, k, r]
 
 
+def add_up(owner, counts):
+    return [count + jnp.where(owner == o, 1, 0) for o, count in enumerate(counts)]
+
+
 def send_kernel(tiles, rows, per_row, lists_ref, number_ref, send_ref):
     me = lax.axis_index("lon")
 
-    def scan(d):
+    def scan(d, most):
         a = wrap(me + d - tiles, tiles)
         for s in range(CAP):
             send_ref[d * STRIDE + s] = rows + 2 * HR
         filled = jnp.int32(0)
+        others = [o for o in range(1, tiles) if o != d] if tiles <= 4 else []
+        owners = [wrap(me + o - tiles, tiles) for o in others]
+        counts = [jnp.int32(0)] * len(others)
         for r in range(rows):
             for k in range(per_row):
                 owner, row = entry_of(lists_ref, number_ref, a, r, k, rows)
-                send_ref[d * STRIDE + jnp.where(owner == me, filled, TRASH)] = row
-                filled = filled + jnp.where(owner == me, 1, 0)
+                hit = owner == me
+                send_ref[d * STRIDE + jnp.where(hit, filled, TRASH)] = row
+                filled = filled + jnp.where(hit, 1, 0)
+                counts = [count + jnp.where(owner == o, 1, 0) for o, count in zip(owners, counts)]
         send_ref[d * STRIDE + COUNT] = filled
+        for count in [filled] + counts:
+            most = jnp.maximum(most, count)
+        return most
 
     if tiles <= 4:
+        most = jnp.int32(0)
         for d in range(1, tiles):
-            scan(d)
+            most = scan(d, most)
+        send_ref[COUNT] = most
     else:
-        pl.loop(1, tiles)(scan)
+
+        @pl.loop(1, tiles)
+        def _(d):
+            scan(d, jnp.int32(0))
 
 
 def pack_kernel(tiles, width, send_ref, rows_ref, before_ref, after_ref, ext_ref, *rest):
@@ -104,7 +121,7 @@
                 spare[d - 1][s] = ext_ref[send_ref[d * STRIDE + BASE + s]]
 
 
-def arrival_kernel(tiles, per_row, lists_ref, number_ref, cot_ref, taps_ref, *rest):
+def arrival_kernel(tiles, per_row, send_ref, lists_ref, number_ref, cot_ref, taps_ref, *rest):
     cot_rows_ref, mix_ref, place_ref, own_ref, needed_ref, wide, taken = rest
     rows, channels, cols = cot_rows_ref.shape
     me = lax.axis_index("lon")
@@ -123,19 +140,7 @@
         own_ref[jnp.where(own, count, TRASH)] = row
 
     if tiles <= 4:
-
-        def add_up(owner, counts):
-            return [count + jnp.where(owner == o, 1, 0) for o, count in enumerate(counts)]
-
-        most = jnp.int32(0)
-        for d in range(1, tiles):
-            a = wrap(me + d - tiles, tiles)
-            counts = [jnp.int32(0)] * tiles
-            for r in range(rows):
-                for k in range(per_row):
-                    counts = add_up(entry_of(lists_ref, number_ref, a, r, k, rows)[0], counts)
-            for o in range(tiles):
-                most = jnp.maximum(most, jnp.where(a == o, 0, counts[o]))
+        most = send_ref[COUNT]
         counts = [jnp.int32(0)] * tiles
         for r in range(rows):
             for k in range(per_row):
@@ -469,11 +474,11 @@
             array(STRIDE, dtype=jnp.int32),
             array(1, dtype=jnp.int32),
         ),
-        [whole(SMEM), whole(SMEM), whole(VMEM), whole(VMEM)],
+        [whole(SMEM)] * 3 + [whole(VMEM)] * 2,
         (whole(VMEM), whole(VMEM), whole(SMEM), whole(SMEM), whole(SMEM)),
         [VMEM((channels * rows, cols), F32), SMEM((tiles + 1,), jnp.int32)],
         "arrival",
-    )(lists, number, arrival_cot.reshape(channels * rows, cols), mixing)
+    )(send_rows, lists, number, arrival_cot.reshape(channels * rows, cols), mixing)
     if tiles <= 4:
         needed = needed[0] > 0
     else:
@@ -482,7 +487,7 @@
         named = (entry[:, None] < number[0][:, None, :]) & (lists[0, :, 0] == tile[:, None, None, None])
         filled = jnp.sum(jnp.where(named, 1, 0), axis=(2, 3))
         needed = jnp.any((filled > BASE) & (tile[None, :] != tile[:, None]))
-    spare = move_spare(spare, 1)
+    spare = move_spare(list(lax.optimization_barrier((*spare, halves[0], base[0]))[:partners]), 1)
 
     filling = (array(CAP, channels, cols),) + base_slots + spare_slots
     began, back, partial = [], [], []
@@ -502,7 +507,7 @@
         )(places, mix, cot_rows, ext_blocks, *base, halves[i], *spare, *began)
         back.append(move(half, -middle))
         partial.append(sums)
-    own, base, spare = began[0], move_whole(began[1:partners], -1), move_spare(began[partners:], -1)
+    own, base, spare = began[0], move_whole(began[1:partners], -1), move_spare(list(lax.optimization_barrier((*began[partners:], back[0], back[-1]))[:partners]), -1)
 
     sums = array(ext + 1, channels, cols, dtype=F32)
     total = call(add_own_kernel, sums, [whole(SMEM), whole(VMEM)], whole(VMEM), (), "add_own")(

time: 42.9 us -> 41.7 us (0.972)
  waiting for transfers between devices: 10.9 us -> 16.7 us
  starting transfers between devices: 17.4 us -> 11.7 us
  Pallas kernels: 13 us -> 11.7 us
    ppermute x8 -> x6, waiting for transfers between devices: 9.89 us -> 15.5 us  [move(): lax.ppermute(part, 'lon', [(i, (i + d) % tiles) for i in range(tiles)])]
    ppermute x8 -> x6, starting transfers between devices: 12.9 us -> 7.38 us  [move(): lax.ppermute(part, 'lon', [(i, (i + d) % tiles) for i in range(tiles)])]
    pallas_call x2 -> x1, Pallas kernels: 3.05 us -> 2.1 us  [local(): call(functools.partial(compute_kernel, tiles, per_row, i * width, width),...]
    pallas_call x1, Pallas kernels: 2.5 us -> 1.97 us  [local(): call(functools.partial(arrival_kernel, tiles, per_row), (array(rows, chan...]
  transfers between devices with their start and end apart: 10 -> 8, of which waited for: 4 -> 5; matrix products, arithmetic and copies ran while one was open for 0% -> 0% of each run, Pallas kernels for 15% -> 10%
where the time goes in v6:
time: 41.7 us; the launch traced here: 41.5 us
  waiting for transfers between devices  16.7 us (40%)
  Pallas kernels  11.7 us (28%)
  starting transfers between devices  11.7 us (28%)
  between operations  1.41 us (3%)
    ppermute x6, waiting for transfers between devices, move(): lax.ppermute(part, 'lon', [(i, (i + d) % tiles) for i in range(tiles)])  15.5 us
    ppermute x6, starting transfers between devices, move(): lax.ppermute(part, 'lon', [(i, (i + d) % tiles) for i in range(tiles)])  7.38 us
    ppermute x2, starting transfers between devices, swap_lat(): got = lax.ppermute(edges[0], 'lat', [(0, 1), (1, 0)])  4.28 us
    pallas_call x1, Pallas kernels, local(): call(functools.partial(send_kernel, tiles, rows, per_row), array(tiles *...  2.15 us
    pallas_call x1, Pallas kernels, local(): call(functools.partial(compute_kernel, tiles, per_row, i * width, width),...  2.1 us
    pallas_call x1, Pallas kernels, local(): call(functools.partial(arrival_kernel, tiles, per_row), (array(rows, chan...  1.97 us
    ppermute x2, waiting for transfers between devices, swap_lat(): got = lax.ppermute(edges[0], 'lat', [(0, 1), (1, 0)])  1.17 us
    pallas_call x1, Pallas kernels, local(): call(functools.partial(prepare_kernel, bands), (array(rows, channels, col...  1.1 us
  transfers between devices with their start and end apart: 8, of which 5 were waited for; matrix products, arithmetic and copies ran while one was open for 0% of the time, Pallas kernels for 10%

profile of v6, /device:TPU:0, one launch (start us, length us, event | category | flops | bytes accessed | tf_op | source)
XLA Modules:
  0.0 41.5 jit_solution(654244120414774381)
XLA Ops:
  0.6 0.0 copy-start.1
  0.6 1.1 %prepare.1 = (bf16[16,64,128]{2,1,0:T(8,128)(2,1)S(1)}, bf16[2,64,128]{2,1,0:T(8,128)(2,1)S(1)}) custom-call(bf16[1024,128]{1,0:T(8,128)(2,1)} %bitcast.22), custom_call_target="tpu_custom_call" | custom-call | tf_op jit(solution)/shard_map/prepare/pallas_call | solution.py:428
  1.7 0.0 copy-start.2
  1.8 3.0 %collective-permute-start.6 = (bf16[2,64,128]{2,1,0:T(8,128)(2,1)S(1)}, bf16[2,64,128]{2,1,0:T(8,128)(2,1)S(1)}, u32[]{:S(2)}, u32[]{:S(2)}) collective-permute-start(bf16[2,64,128]{2,1,0:T(8,128)(2,1)S(1)} %get-tuple-element.73), channel_id=1, source_target_pairs={{0,2},{2,0},{1,3},{3,1},{4,6},{6,4},{5,7},{7,5},{8,10},{10,8},{9,1... | collective-permute-start | bytes 98312 | tf_op jit(solution)/shard_map/ppermute | solution.py:368
  4.8 0.0 copy-done.1
  4.8 0.0 copy-done.2
  4.8 2.2 %send.1.send_ref = s32[64]{0:T(128)S(1)} custom-call(s32[1,4,3,2,16]{4,3,2,1,0:T(2,128)S(1)} %bitcast.17, s32[1,4,16]{2,1,0:T(4,128)S(1)} %bitcast.19), custom_call_target="tpu_custom_call" | custom-call | tf_op jit(solution)/shard_map/send/pallas_call | solution.py:442
  6.9 0.0 collective-permute-done.6.before_ref.after_ref
  6.9 0.0 copy-start.3
  7.0 0.0 copy-start
  7.0 0.6 %pack.1 = (bf16[21,64,128]{2,1,0:T(8,128)(2,1)S(1)}, bf16[8,64,128]{2,1,0:T(8,128)(2,1)S(1)}, bf16[8,64,128]{2,1,0:T(8,128)(2,1)S(1)}, bf16[8,64,128]{2,1,0:T(8,...) custom-call(s32[64]{0:T(128)S(1)} %send.1.send_ref, ...), custom_call_target="tpu_custom_call" | custom-call | tf_op jit(solution)/shard_map/pack/pallas_call | solution.py:450
  7.6 1.9 %collective-permute-start.7 = (bf16[8,64,128]{2,1,0:T(8,128)(2,1)S(1)}, bf16[8,64,128]{2,1,0:T(8,128)(2,1)S(1)}, u32[]{:S(2)}, u32[]{:S(2)}) collective-permute-start(bf16[8,64,128]{2,1,0:T(8,128)(2,1)S(1)} %get-tuple-element.75), channel_id=1, source_target_pairs={{0,4},{4,8},{8,12},{12,0},{1,5},{5,9},{9,13},{13,1},{2,6},{6,10},{... | collective-permute-start | bytes 393224 | tf_op jit(solution)/shard_map/ppermute | solution.py:405
  9.4 2.1 %collective-permute-start.8 = (bf16[8,64,128]{2,1,0:T(8,128)(2,1)S(1)}, bf16[8,64,128]{2,1,0:T(8,128)(2,1)S(1)}, u32[]{:S(2)}, u32[]{:S(2)}) collective-permute-start(bf16[8,64,128]{2,1,0:T(8,128)(2,1)S(1)} %get-tuple-element.76), channel_id=1, source_target_pairs={{0,12},{4,0},{8,4},{12,8},{1,13},{5,1},{9,5},{13,9},{2,14},{6,2},{... | collective-permute-start | bytes 393224 | tf_op jit(solution)/shard_map/ppermute | solution.py:405
  11.5 0.9 %collective-permute-start.9 = (bf16[8,64,128]{2,1,0:T(8,128)(2,1)S(1)}, bf16[8,64,128]{2,1,0:T(8,128)(2,1)S(1)}, u32[]{:S(2)}, u32[]{:S(2)}) collective-permute-start(bf16[8,64,128]{2,1,0:T(8,128)(2,1)S(1)} %get-tuple-element.77), channel_id=1, source_target_pairs={{0,8},{4,12},{8,0},{12,4},{1,9},{5,13},{9,1},{13,5},{2,10},{6,14},... | collective-permute-start | bytes 393224 | tf_op jit(solution)/shard_map/ppermute | solution.py:405
  12.5 0.0 copy-done.3
  12.5 0.0 copy-done
  12.5 2.0 %arrival.1 = (bf16[16,64,128]{2,1,0:T(8,128)(2,1)S(1)}, f32[4,32,128]{2,1,0:T(8,128)S(1)}, s32[68]{0:T(128)S(1)}, s32[16]{0:T(128)S(1)}, s32[1]{0:T(128)}) custom-call(s32[64]{0:T(128)S(1)} %send.1.send_ref, s32[1,4,3,2,16]{4,3,2,1,0:T(2,128)S(1)} %bitcast.18, s32[1,4,16]{2,1,0:T(4,128)S(1)} %bitcast.20, bf16[1024,128]{1,0:T(8,128)(2,1)S(1)} %bitcast.15, ...), custom_call_target="tpu_custom_call" | custom-call | tf_op jit(solution)/shard_map/arrival/pallas_call | solution.py:468
  15.2 0.6 %collective-permute-done.7.rest_0_ = bf16[8,64,128]{2,1,0:T(8,128)(2,1)S(1)} collective-permute-done((bf16[8,64,128]{2,1,0:T(8,128)(2,1)S(1)}, bf16[8,64,128]{2,1,0:T(8,128)(2,1)S(1)}, u32[]{:S(2)}, u32[]{:S(2)}) %collective-permute-start.7) | collective-permute-done | bytes 131104 | tf_op jit(solution)/shard_map/ppermute | solution.py:405
  15.8 7.1 %collective-permute-done.9.rest_2_ = bf16[8,64,128]{2,1,0:T(8,128)(2,1)S(1)} collective-permute-done((bf16[8,64,128]{2,1,0:T(8,128)(2,1)S(1)}, bf16[8,64,128]{2,1,0:T(8,128)(2,1)S(1)}, u32[]{:S(2)}, u32[]{:S(2)}) %collective-permute-start.9) | collective-permute-done | bytes 131104 | tf_op jit(solution)/shard_map/ppermute | solution.py:405
  22.9 0.0 collective-permute-done.8.rest_1_
  22.9 2.1 %compute.1 = (bf16[11,64,128]{2,1,0:T(8,128)(2,1)S(1)}, bf16[8,64,128]{2,1,0:T(8,128)(2,1)S(1)}, bf16[8,64,128]{2,1,0:T(8,128)(2,1)S(1)}, bf16[3,64,128]{2,1,0:T...) custom-call(s32[68]{0:T(128)S(1)} %get-tuple-element.69.place_ref, ...), custom_call_target="tpu_custom_call" | custom-call | tf_op jit(solution)/shard_map/compute/pallas_call | solution.py:496
  25.0 0.1 collective-permute-start.12
  25.1 1.9 %collective-permute-start.10 = (bf16[8,64,128]{2,1,0:T(8,128)(2,1)S(1)}, bf16[8,64,128]{2,1,0:T(8,128)(2,1)S(1)}, u32[]{:S(2)}, u32[]{:S(2)}) collective-permute-start(bf16[8,64,128]{2,1,0:T(8,128)(2,1)S(1)} %get-tuple-element.89), channel_id=1, source_target_pairs={{0,12},{4,0},{8,4},{12,8},{1,13},{5,1},{9,5},{13,9},{2,14},{6,2},{... | collective-permute-start | bytes 393224 | tf_op jit(solution)/shard_map/ppermute | solution.py:405
  27.0 0.5 %collective-permute-start.11 = (bf16[8,64,128]{2,1,0:T(8,128)(2,1)S(1)}, bf16[8,64,128]{2,1,0:T(8,128)(2,1)S(1)}, u32[]{:S(2)}, u32[]{:S(2)}) collective-permute-start(bf16[8,64,128]{2,1,0:T(8,128)(2,1)S(1)} %get-tuple-element.90), channel_id=1, source_target_pairs={{0,4},{4,8},{8,12},{12,0},{1,5},{5,9},{9,13},{13,1},{2,6},{6,10},{... | collective-permute-start | bytes 393224 | tf_op jit(solution)/shard_map/ppermute | solution.py:405
  27.5 0.6 %add_own.1.total_ref._ = f32[21,64,128]{2,1,0:T(8,128)S(1)} custom-call(s32[16]{0:T(128)S(1)} %get-tuple-element.68.table_ref, bf16[11,64,128]{2,1,0:T(8,128)(2,1)S(1)} %get-tuple-element.88.own_ref), custom_call_target="tpu_custom_call" | custom-call | tf_op jit(solution)/shard_map/add_own/pallas_call | solution.py:513
  28.1 7.5 %collective-permute-done.12.rest_2_ = bf16[8,64,128]{2,1,0:T(8,128)(2,1)S(1)} collective-permute-done((bf16[8,64,128]{2,1,0:T(8,128)(2,1)S(1)}, bf16[8,64,128]{2,1,0:T(8,128)(2,1)S(1)}, u32[]{:S(2)}, u32[]{:S(2)}) %collective-permute-start.12) | collective-permute-done | bytes 131104 | tf_op jit(solution)/shard_map/ppermute | solution.py:405
  35.7 0.3 collective-permute-done.10.rest_0_
  35.9 0.0 collective-permute-done.11.rest_1_
  36.0 0.7 %edges.1 = bf16[2,64,128]{2,1,0:T(8,128)(2,1)S(1)} custom-call(s32[64]{0:T(128)S(1)} %send.1.send_ref, f32[21,64,128]{2,1,0:T(8,128)S(1)} %add_own.1.total_ref._, bf16[8,64,128]{2,1,0:T(8,128)(2,1)S(1)} %collective-permute-done.10.rest_0_, bf16[8,64,128]{2,1,0:T(8,128)(2,1)S(1)} %collective-permute-done.11.rest_1_, ...), custom_call_target="tpu_custom_call" | custom-call | tf_op jit(solution)/shard_map/edges/pallas_call | solution.py:517
  36.7 1.3 %collective-permute-start.13 = (bf16[2,64,128]{2,1,0:T(8,128)(2,1)S(1)}, bf16[2,64,128]{2,1,0:T(8,128)(2,1)S(1)}, u32[]{:S(2)}, u32[]{:S(2)}) collective-permute-start(bf16[2,64,128]{2,1,0:T(8,128)(2,1)S(1)} %edges.1), channel_id=1, source_target_pairs={{0,2},{2,0},{1,3},{3,1},{4,6},{6,4},{5,7},{7,5},{8,10},{10,8},{9,1... | collective-permute-start | bytes 98312 | tf_op jit(solution)/shard_map/ppermute | solution.py:368
  38.0 0.9 %gradient.1 = bf16[128,128]{1,0:T(8,128)(2,1)} custom-call(f32[128,8,128]{2,1,0:T(8,128)S(1)} %get-tuple-element.103.refs_0_), custom_call_target="tpu_custom_call" | custom-call | tf_op jit(solution)/shard_map/gradient/pallas_call | solution.py:545
  38.8 0.7 %add.1.total_ref = f32[21,64,128]{2,1,0:T(8,128)S(1)} custom-call(s32[64]{0:T(128)S(1)} %send.1.send_ref, f32[21,64,128]{2,1,0:T(8,128)S(1)} %add_own.1.total_ref._, bf16[8,64,128]{2,1,0:T(8,128)(2,1)S(1)} %collective-permute-done.10.rest_0_, bf16[8,64,128]{2,1,0:T(8,128)(2,1)S(1)} %collective-permute-done.11.rest_1_, ...), custom_call_target="tpu_custom_call", output_to_operand_aliasing={{}: (1, {})} | custom-call | tf_op jit(solution)/shard_map/add/pallas_call | solution.py:526
  39.5 1.2 %collective-permute-done.13.above_ref.below_ref = bf16[2,64,128]{2,1,0:T(8,128)(2,1)S(1)} collective-permute-done((bf16[2,64,128]{2,1,0:T(8,128)(2,1)S(1)}, bf16[2,64,128]{2,1,0:T(8,128)(2,1)S(1)}, u32[]{:S(2)}, u32[]{:S(2)}) %collective-permute-start.13) | collective-permute-done | bytes 32800 | tf_op jit(solution)/shard_map/ppermute | solution.py:368
  40.7 0.9 %finish.1 = f32[1024,128]{1,0:T(8,128)} custom-call(f32[21,64,128]{2,1,0:T(8,128)S(1)} %add.1.total_ref, bf16[2,64,128]{2,1,0:T(8,128)(2,1)S(1)} %collective-permute-done.13.above_ref.below_ref, bf16[2,64,128]{2,1,0:T(8,128)(2,1)S(1)} %collective-permute-done.13.above_ref.below_ref), custom_call_target="tpu_custom_call" | custom-call | tf_op jit(solution)/shard_map/finish/pallas_call | solution.py:535
  (4 shorter events, 0.0 us)
Async XLA Ops:
  0.6 4.1 %copy-start.1 = (s32[1,16,4,2,3]{1,3,4,2,0:T(2,128)S(1)}, s32[1,16,4,2,3]{1,3,4,2,0:T(2,128)}, u32[]{:S(2)}) copy-start(s32[1,16,4,2,3]{1,3,4,2,0:T(2,128)} %param.12) | copy-start | bytes 4612
  1.7 3.0 %copy-start.2 = (s32[1,16,4]{1,2,0:T(4,128)S(1)}, s32[1,16,4]{1,2,0:T(4,128)}, u32[]{:S(2)}) copy-start(s32[1,16,4]{1,2,0:T(4,128)} %param.13) | copy-start | bytes 772
  1.8 5.2 %collective-permute-start.6 = (bf16[2,64,128]{2,1,0:T(8,128)(2,1)S(1)}, bf16[2,64,128]{2,1,0:T(8,128)(2,1)S(1)}, u32[]{:S(2)}, u32[]{:S(2)}) collective-permute-start(bf16[2,64,128]{2,1,0:T(8,128)(2,1)S(1)} %get-tuple-element.73), channel_id=1, source_target_pairs={{0,2},{2,0},{1,3},{3,1},{4,6},{6,4},{5,7},{7,5},{8,10},{10,8},{9,1... | collective-permute-start | bytes 98312 | tf_op jit(solution)/shard_map/ppermute | solution.py:368
  6.9 5.5 %copy-start.3 = (bf16[1,16,1,2,4,128]{5,4,3,2,1,0:T(4,128)(2,1)S(1)}, bf16[1,16,1,2,4,128]{5,4,3,2,1,0:T(4,128)(2,1)}, u32[]{:S(2)}) copy-start(bf16[1,16,1,2,4,128]{5,4,3,2,1,0:T(4,128)(2,1)} %param.11) | copy-start | bytes 98308
  7.0 5.6 %copy-start = (bf16[16,4,16,128]{3,2,1,0:T(8,128)(2,1)S(1)}, bf16[16,4,16,128]{3,2,1,0:T(8,128)(2,1)}, u32[]{:S(2)}) copy-start(bf16[16,4,16,128]{3,2,1,0:T(8,128)(2,1)} %param.10) | copy-start | bytes 786436
  7.6 8.2 %collective-permute-start.7 = (bf16[8,64,128]{2,1,0:T(8,128)(2,1)S(1)}, bf16[8,64,128]{2,1,0:T(8,128)(2,1)S(1)}, u32[]{:S(2)}, u32[]{:S(2)}) collective-permute-start(bf16[8,64,128]{2,1,0:T(8,128)(2,1)S(1)} %get-tuple-element.75), channel_id=1, source_target_pairs={{0,4},{4,8},{8,12},{12,0},{1,5},{5,9},{9,13},{13,1},{2,6},{6,10},{... | collective-permute-start | bytes 393224 | tf_op jit(solution)/shard_map/ppermute | solution.py:405
  9.4 13.4 %collective-permute-start.8 = (bf16[8,64,128]{2,1,0:T(8,128)(2,1)S(1)}, bf16[8,64,128]{2,1,0:T(8,128)(2,1)S(1)}, u32[]{:S(2)}, u32[]{:S(2)}) collective-permute-start(bf16[8,64,128]{2,1,0:T(8,128)(2,1)S(1)} %get-tuple-element.76), channel_id=1, source_target_pairs={{0,12},{4,0},{8,4},{12,8},{1,13},{5,1},{9,5},{13,9},{2,14},{6,2},{... | collective-permute-start | bytes 393224 | tf_op jit(solution)/shard_map/ppermute | solution.py:405
  11.5 11.4 %collective-permute-start.9 = (bf16[8,64,128]{2,1,0:T(8,128)(2,1)S(1)}, bf16[8,64,128]{2,1,0:T(8,128)(2,1)S(1)}, u32[]{:S(2)}, u32[]{:S(2)}) collective-permute-start(bf16[8,64,128]{2,1,0:T(8,128)(2,1)S(1)} %get-tuple-element.77), channel_id=1, source_target_pairs={{0,8},{4,12},{8,0},{12,4},{1,9},{5,13},{9,1},{13,5},{2,10},{6,14},... | collective-permute-start | bytes 393224 | tf_op jit(solution)/shard_map/ppermute | solution.py:405
  25.0 10.7 %collective-permute-start.12 = (bf16[8,64,128]{2,1,0:T(8,128)(2,1)S(1)}, bf16[8,64,128]{2,1,0:T(8,128)(2,1)S(1)}, u32[]{:S(2)}, u32[]{:S(2)}) collective-permute-start(bf16[8,64,128]{2,1,0:T(8,128)(2,1)S(1)} %get-tuple-element.91), channel_id=1, source_target_pairs={{0,8},{4,12},{8,0},{12,4},{1,9},{5,13},{9,1},{13,5},{2,10},{6,14},... | collective-permute-start | bytes 393224 | tf_op jit(solution)/shard_map/ppermute | solution.py:405
  25.1 10.9 %collective-permute-start.10 = (bf16[8,64,128]{2,1,0:T(8,128)(2,1)S(1)}, bf16[8,64,128]{2,1,0:T(8,128)(2,1)S(1)}, u32[]{:S(2)}, u32[]{:S(2)}) collective-permute-start(bf16[8,64,128]{2,1,0:T(8,128)(2,1)S(1)} %get-tuple-element.89), channel_id=1, source_target_pairs={{0,12},{4,0},{8,4},{12,8},{1,13},{5,1},{9,5},{13,9},{2,14},{6,2},{... | collective-permute-start | bytes 393224 | tf_op jit(solution)/shard_map/ppermute | solution.py:405
  27.0 9.0 %collective-permute-start.11 = (bf16[8,64,128]{2,1,0:T(8,128)(2,1)S(1)}, bf16[8,64,128]{2,1,0:T(8,128)(2,1)S(1)}, u32[]{:S(2)}, u32[]{:S(2)}) collective-permute-start(bf16[8,64,128]{2,1,0:T(8,128)(2,1)S(1)} %get-tuple-element.90), channel_id=1, source_target_pairs={{0,4},{4,8},{8,12},{12,0},{1,5},{5,9},{9,13},{13,1},{2,6},{6,10},{... | collective-permute-start | bytes 393224 | tf_op jit(solution)/shard_map/ppermute | solution.py:405
  36.7 4.0 %collective-permute-start.13 = (bf16[2,64,128]{2,1,0:T(8,128)(2,1)S(1)}, bf16[2,64,128]{2,1,0:T(8,128)(2,1)S(1)}, u32[]{:S(2)}, u32[]{:S(2)}) collective-permute-start(bf16[2,64,128]{2,1,0:T(8,128)(2,1)S(1)} %edges.1), channel_id=1, source_target_pairs={{0,2},{2,0},{1,3},{3,1},{4,6},{6,4},{5,7},{7,5},{8,10},{10,8},{9,1... | collective-permute-start | bytes 98312 | tf_op jit(solution)/shard_map/ppermute | solution.py:368

commit v7 on v6

--- a/solution.py
+++ b/solution.py
@@ -209,6 +209,7 @@
         source = [place_ref[r * per_row + k] for k in range(per_row)]
         target = [place_ref[entries + r * per_row + k] for k in range(per_row)]
         mix = [[mix_ref[j, pl.ds(r * per_row + k, 1), :] for j in range(4)] for k in range(per_row)]
+        grads = [None] * (per_row * 4)
         for lo in range(0, width, part):
             block = [blocks[source[k], lo : lo + part].astype(F32) for k in range(per_row)]
             tap = [sum(block[k] * mix[k][j] for k in range(per_row)) for j in range(4)]
@@ -230,9 +231,10 @@
                 )
                 terms[target[k], lo : lo + part] = term.astype(BF16)
                 for j in range(4):
-                    at = (r * per_row + k) * 4 + j
                     product = jnp.sum((block[k] * moved[j]).reshape(part // 8, 8, cols), axis=0)
-                    grad_ref[at] = product if lo == 0 else grad_ref[at] + product
+                    grads[k * 4 + j] = product if lo == 0 else grads[k * 4 + j] + product
+        for i in range(per_row * 4):
+            grad_ref[r * per_row * 4 + i] = grads[i]
         return 0
 
     lax.fori_loop(0, rows, row, 0, unroll=4)
@@ -267,11 +269,24 @@
     out_ref[...] = fixed.astype(BF16)
 
 
-def add_own_kernel(table_ref, own_ref, total_ref):
+def edge_starts(bands, ext):
+    if bands == 2:
+        return [jnp.where(lax.axis_index("lat") == 0, ext - HR, 0)]
+    return [0, ext - HR]
+
+
+def add_own_kernel(tiles, bands, table_ref, send_ref, own_ref, total_ref, mask_ref):
     total_ref[...] = jnp.zeros_like(total_ref)
     for s in range(CAP):
         at = table_ref[s]
         total_ref[at] = total_ref[at] + own_ref[s].astype(F32)
+    for e, start in enumerate(edge_starts(bands, total_ref.shape[0] - 1)):
+        for d in range(1, tiles):
+            for s in range(CAP):
+                row = send_ref[d * STRIDE + s] - start
+                for h in range(HR):
+                    hit = jnp.where(row == h, 1.0, 0.0)
+                    mask_ref[e * HR + h, (d - 1) * CAP + s] = jnp.full(mask_ref.shape[2:], hit, F32)
 
 
 def slot_refs(tiles, base, halves, spare):
@@ -283,44 +298,32 @@
     return out, [(d, BASE, SPARE, 0, ref) for d, ref in enumerate(spare, 1)]
 
 
-def edge_kernel(tiles, bands, send_ref, total_ref, *rest):
+def edge_kernel(tiles, bands, mask_ref, total_ref, *rest):
     n = tiles - 1
-    base, halves, spare, edges = rest[: n - 1], rest[n - 1 : n - 1 + PARTS], rest[n - 1 + PARTS : 2 * n - 1 + PARTS], rest[2 * n - 1 + PARTS :]
-    *edges, sums = edges
-    ext = total_ref.shape[0] - 1
-    if bands == 2:
-        starts = [jnp.where(lax.axis_index("lat") == 0, ext - HR, 0)]
-    else:
-        starts = [0, ext - HR]
+    base, halves, rest = rest[: n - 1], rest[n - 1 : n - 1 + PARTS], rest[n - 1 + PARTS :]
+    spare, edges = rest[:n], rest[n:]
+    starts = edge_starts(bands, total_ref.shape[0] - 1)
     always, seldom = slot_refs(tiles, base, halves, spare)
-    wanted = [(e, h) for e in range(len(starts)) for h in range(HR)]
-    for e, h in wanted:
-        sums[e, h] = total_ref[starts[e] + h]
-
-    def gather(refs):
-        for d, first, slots, channel, ref in refs:
-            part = slice(channel, channel + ref.shape[1])
-            for c in range(part.start, part.stop, 16):
-                found = [sums[e, h, c : c + 16] for e, h in wanted]
-                for s in range(slots):
-                    at = send_ref[d * STRIDE + first + s]
-                    value = ref[s, c - channel : c - channel + 16].astype(F32)
-                    found = [
-                        jnp.where(at == starts[e] + h, total + value, total)
-                        for (e, h), total in zip(wanted, found)
+    _, channels, cols = edges[0].shape
+    chunk = 16
+    for c in range(0, channels, chunk):
+        found = [
+            [total_ref[start + h, c + g : c + g + 8] for g in range(0, chunk, 8)]
+            for start in starts
+            for h in range(HR)
+        ]
+        for d, first, slots, channel, ref in always + seldom:
+            if not channel <= c < channel + ref.shape[1]:
+                continue
+            for s in range(slots):
+                value = ref[s, c - channel : c - channel + chunk].astype(F32)
+                for i in range(len(found)):
+                    hit = mask_ref[i, (d - 1) * CAP + first + s] > 0.5
+                    found[i] = [
+                        group + jnp.where(hit, value[8 * g : 8 * g + 8], 0.0) for g, group in enumerate(found[i])
                     ]
-                for (e, h), total in zip(wanted, found):
-                    sums[e, h, c : c + 16] = total
-
-    gather(always)
-    for item in seldom:
-
-        @pl.when(send_ref[item[0] * STRIDE + COUNT] > BASE)
-        def _():
-            gather([item])
-
-    for e, edge in enumerate(edges):
-        edge[...] = sums[e].astype(BF16)
+        for i, groups in enumerate(found):
+            edges[i // HR][i % HR, c : c + chunk] = jnp.concatenate(groups, axis=0).astype(BF16)
 
 
 def add_kernel(tiles, send_ref, _, *rest):
@@ -510,18 +513,23 @@
     own, base, spare = began[0], move_whole(began[1:partners], -1), move_spare(list(lax.optimization_barrier((*began[partners:], back[0], back[-1]))[:partners]), -1)
 
     sums = array(ext + 1, channels, cols, dtype=F32)
-    total = call(add_own_kernel, sums, [whole(SMEM), whole(VMEM)], whole(VMEM), (), "add_own")(
-        own_table, own
-    )
+    total, masks = call(
+        functools.partial(add_own_kernel, tiles, bands),
+        (sums, array(edge_count * HR, partners * CAP, 8, cols, dtype=F32)),
+        [whole(SMEM), whole(SMEM), whole(VMEM)],
+        (whole(VMEM),) * 2,
+        (),
+        "add_own",
+    )(own_table, send_rows, own)
     returned = [*base, *back, *spare]
     edges = call(
         functools.partial(edge_kernel, tiles, bands),
         edge,
-        [whole(SMEM)] + [whole(VMEM)] * (1 + len(returned)),
+        [whole(VMEM)] * (2 + len(returned)),
         (whole(VMEM),) * edge_count,
-        [VMEM((edge_count, HR, channels, cols), F32)],
+        (),
         "edges",
-    )(send_rows, total, *returned)
+    )(masks, total, *returned)
     from_above, from_below = swap_lat(edges, bands)
     total = call(
         functools.partial(add_kernel, tiles),

time: 41.7 us -> 41.2 us (0.988)
  Pallas kernels: 11.7 us -> 11.2 us
    pallas_call x2, Pallas kernels: 1.37 us -> 0.93 us  [the longest x1 0.68 us: local(): call(functools.partial(add_own_kernel, tiles, bands), (sums, array(edge_c...]
where the time goes in v7:
time: 41.2 us; the launch traced here: 41 us
  waiting for transfers between devices  16.7 us (41%)
  starting transfers between devices  11.7 us (28%)
  Pallas kernels  11.2 us (27%)
  between operations  1.41 us (3%)
    ppermute x6, waiting for transfers between devices, move(): lax.ppermute(part, 'lon', [(i, (i + d) % tiles) for i in range(tiles)])  15.5 us
    ppermute x6, starting transfers between devices, move(): lax.ppermute(part, 'lon', [(i, (i + d) % tiles) for i in range(tiles)])  7.38 us
    ppermute x2, starting transfers between devices, swap_lat(): got = lax.ppermute(edges[0], 'lat', [(0, 1), (1, 0)])  4.28 us
    pallas_call x1, Pallas kernels, local(): call(functools.partial(send_kernel, tiles, rows, per_row), array(tiles *...  2.15 us
    pallas_call x1, Pallas kernels, local(): call(functools.partial(compute_kernel, tiles, per_row, i * width, width),...  2.07 us
    pallas_call x1, Pallas kernels, local(): call(functools.partial(arrival_kernel, tiles, per_row), (array(rows, chan...  1.97 us
    ppermute x2, waiting for transfers between devices, swap_lat(): got = lax.ppermute(edges[0], 'lat', [(0, 1), (1, 0)])  1.17 us
    pallas_call x1, Pallas kernels, local(): call(functools.partial(prepare_kernel, bands), (array(rows, channels, col...  1.1 us
  transfers between devices with their start and end apart: 8, of which 5 were waited for; matrix products, arithmetic and copies ran while one was open for 0% of the time, Pallas kernels for 10%

profile of v7, /device:TPU:0, one launch (start us, length us, event | category | flops | bytes accessed | tf_op | source)
XLA Modules:
  0.0 41.0 jit_solution(13686160761184017023)
XLA Ops:
  0.6 0.0 copy-start.1
  0.6 1.1 %prepare.1 = (bf16[16,64,128]{2,1,0:T(8,128)(2,1)S(1)}, bf16[2,64,128]{2,1,0:T(8,128)(2,1)S(1)}) custom-call(bf16[1024,128]{1,0:T(8,128)(2,1)} %bitcast.22), custom_call_target="tpu_custom_call" | custom-call | tf_op jit(solution)/shard_map/prepare/pallas_call | solution.py:431
  1.7 0.0 copy-start.2
  1.8 3.0 %collective-permute-start.6 = (bf16[2,64,128]{2,1,0:T(8,128)(2,1)S(1)}, bf16[2,64,128]{2,1,0:T(8,128)(2,1)S(1)}, u32[]{:S(2)}, u32[]{:S(2)}) collective-permute-start(bf16[2,64,128]{2,1,0:T(8,128)(2,1)S(1)} %get-tuple-element.75), channel_id=1, source_target_pairs={{0,2},{2,0},{1,3},{3,1},{4,6},{6,4},{5,7},{7,5},{8,10},{10,8},{9,1... | collective-permute-start | bytes 98312 | tf_op jit(solution)/shard_map/ppermute | solution.py:371
  4.8 0.0 copy-done.1
  4.8 0.0 copy-done.2
  4.8 2.2 %send.1.send_ref = s32[64]{0:T(128)S(1)} custom-call(s32[1,4,3,2,16]{4,3,2,1,0:T(2,128)S(1)} %bitcast.17, s32[1,4,16]{2,1,0:T(4,128)S(1)} %bitcast.19), custom_call_target="tpu_custom_call" | custom-call | tf_op jit(solution)/shard_map/send/pallas_call | solution.py:445
  6.9 0.0 collective-permute-done.6.before_ref.after_ref
  6.9 0.0 copy-start.3
  7.0 0.0 copy-start
  7.0 0.6 %pack.1 = (bf16[21,64,128]{2,1,0:T(8,128)(2,1)S(1)}, bf16[8,64,128]{2,1,0:T(8,128)(2,1)S(1)}, bf16[8,64,128]{2,1,0:T(8,128)(2,1)S(1)}, bf16[8,64,128]{2,1,0:T(8,...) custom-call(s32[64]{0:T(128)S(1)} %send.1.send_ref, ...), custom_call_target="tpu_custom_call" | custom-call | tf_op jit(solution)/shard_map/pack/pallas_call | solution.py:453
  7.6 1.9 %collective-permute-start.7 = (bf16[8,64,128]{2,1,0:T(8,128)(2,1)S(1)}, bf16[8,64,128]{2,1,0:T(8,128)(2,1)S(1)}, u32[]{:S(2)}, u32[]{:S(2)}) collective-permute-start(bf16[8,64,128]{2,1,0:T(8,128)(2,1)S(1)} %get-tuple-element.77), channel_id=1, source_target_pairs={{0,4},{4,8},{8,12},{12,0},{1,5},{5,9},{9,13},{13,1},{2,6},{6,10},{... | collective-permute-start | bytes 393224 | tf_op jit(solution)/shard_map/ppermute | solution.py:408
  9.4 2.1 %collective-permute-start.8 = (bf16[8,64,128]{2,1,0:T(8,128)(2,1)S(1)}, bf16[8,64,128]{2,1,0:T(8,128)(2,1)S(1)}, u32[]{:S(2)}, u32[]{:S(2)}) collective-permute-start(bf16[8,64,128]{2,1,0:T(8,128)(2,1)S(1)} %get-tuple-element.78), channel_id=1, source_target_pairs={{0,12},{4,0},{8,4},{12,8},{1,13},{5,1},{9,5},{13,9},{2,14},{6,2},{... | collective-permute-start | bytes 393224 | tf_op jit(solution)/shard_map/ppermute | solution.py:408
  11.5 0.9 %collective-permute-start.9 = (bf16[8,64,128]{2,1,0:T(8,128)(2,1)S(1)}, bf16[8,64,128]{2,1,0:T(8,128)(2,1)S(1)}, u32[]{:S(2)}, u32[]{:S(2)}) collective-permute-start(bf16[8,64,128]{2,1,0:T(8,128)(2,1)S(1)} %get-tuple-element.79), channel_id=1, source_target_pairs={{0,8},{4,12},{8,0},{12,4},{1,9},{5,13},{9,1},{13,5},{2,10},{6,14},... | collective-permute-start | bytes 393224 | tf_op jit(solution)/shard_map/ppermute | solution.py:408
  12.5 0.0 copy-done.3
  12.5 0.0 copy-done
  12.5 2.0 %arrival.1 = (bf16[16,64,128]{2,1,0:T(8,128)(2,1)S(1)}, f32[4,32,128]{2,1,0:T(8,128)S(1)}, s32[68]{0:T(128)S(1)}, s32[16]{0:T(128)S(1)}, s32[1]{0:T(128)}) custom-call(s32[64]{0:T(128)S(1)} %send.1.send_ref, s32[1,4,3,2,16]{4,3,2,1,0:T(2,128)S(1)} %bitcast.18, s32[1,4,16]{2,1,0:T(4,128)S(1)} %bitcast.20, bf16[1024,128]{1,0:T(8,128)(2,1)S(1)} %bitcast.15, ...), custom_call_target="tpu_custom_call" | custom-call | tf_op jit(solution)/shard_map/arrival/pallas_call | solution.py:471
  15.2 0.6 %collective-permute-done.7.rest_0_ = bf16[8,64,128]{2,1,0:T(8,128)(2,1)S(1)} collective-permute-done((bf16[8,64,128]{2,1,0:T(8,128)(2,1)S(1)}, bf16[8,64,128]{2,1,0:T(8,128)(2,1)S(1)}, u32[]{:S(2)}, u32[]{:S(2)}) %collective-permute-start.7) | collective-permute-done | bytes 131104 | tf_op jit(solution)/shard_map/ppermute | solution.py:408
  15.8 7.1 %collective-permute-done.9.rest_2_ = bf16[8,64,128]{2,1,0:T(8,128)(2,1)S(1)} collective-permute-done((bf16[8,64,128]{2,1,0:T(8,128)(2,1)S(1)}, bf16[8,64,128]{2,1,0:T(8,128)(2,1)S(1)}, u32[]{:S(2)}, u32[]{:S(2)}) %collective-permute-start.9) | collective-permute-done | bytes 131104 | tf_op jit(solution)/shard_map/ppermute | solution.py:408
  22.9 0.0 collective-permute-done.8.rest_1_
  22.9 2.1 %compute.1 = (bf16[11,64,128]{2,1,0:T(8,128)(2,1)S(1)}, bf16[8,64,128]{2,1,0:T(8,128)(2,1)S(1)}, bf16[8,64,128]{2,1,0:T(8,128)(2,1)S(1)}, bf16[3,64,128]{2,1,0:T...) custom-call(s32[68]{0:T(128)S(1)} %get-tuple-element.71.place_ref, ...), custom_call_target="tpu_custom_call" | custom-call | tf_op jit(solution)/shard_map/compute/pallas_call | solution.py:499
  25.0 0.1 collective-permute-start.12
  25.0 1.9 %collective-permute-start.10 = (bf16[8,64,128]{2,1,0:T(8,128)(2,1)S(1)}, bf16[8,64,128]{2,1,0:T(8,128)(2,1)S(1)}, u32[]{:S(2)}, u32[]{:S(2)}) collective-permute-start(bf16[8,64,128]{2,1,0:T(8,128)(2,1)S(1)} %get-tuple-element.93), channel_id=1, source_target_pairs={{0,12},{4,0},{8,4},{12,8},{1,13},{5,1},{9,5},{13,9},{2,14},{6,2},{... | collective-permute-start | bytes 393224 | tf_op jit(solution)/shard_map/ppermute | solution.py:408
  27.0 0.5 %collective-permute-start.11 = (bf16[8,64,128]{2,1,0:T(8,128)(2,1)S(1)}, bf16[8,64,128]{2,1,0:T(8,128)(2,1)S(1)}, u32[]{:S(2)}, u32[]{:S(2)}) collective-permute-start(bf16[8,64,128]{2,1,0:T(8,128)(2,1)S(1)} %get-tuple-element.94), channel_id=1, source_target_pairs={{0,4},{4,8},{8,12},{12,0},{1,5},{5,9},{9,13},{13,1},{2,6},{6,10},{... | collective-permute-start | bytes 393224 | tf_op jit(solution)/shard_map/ppermute | solution.py:408
  27.5 0.7 %add_own.1 = (f32[21,64,128]{2,1,0:T(8,128)S(1)}, f32[2,33,8,128]{3,2,1,0:T(8,128)S(1)}) custom-call(s32[16]{0:T(128)S(1)} %get-tuple-element.70.table_ref, s32[64]{0:T(128)S(1)} %send.1.send_ref, bf16[11,64,128]{2,1,0:T(8,128)(2,1)S(1)} %get-tuple-element.90.own_ref), custom_call_target="tpu_custom_call" | custom-call | tf_op jit(solution)/shard_map/add_own/pallas_call | solution.py:516
  28.1 7.5 %collective-permute-done.12.rest_2_ = bf16[8,64,128]{2,1,0:T(8,128)(2,1)S(1)} collective-permute-done((bf16[8,64,128]{2,1,0:T(8,128)(2,1)S(1)}, bf16[8,64,128]{2,1,0:T(8,128)(2,1)S(1)}, u32[]{:S(2)}, u32[]{:S(2)}) %collective-permute-start.12) | collective-permute-done | bytes 131104 | tf_op jit(solution)/shard_map/ppermute | solution.py:408
  35.6 0.3 collective-permute-done.10.rest_0_
  35.9 0.0 collective-permute-done.11.rest_1_
  35.9 0.3 edges.1
  36.2 1.3 %collective-permute-start.13 = (bf16[2,64,128]{2,1,0:T(8,128)(2,1)S(1)}, bf16[2,64,128]{2,1,0:T(8,128)(2,1)S(1)}, u32[]{:S(2)}, u32[]{:S(2)}) collective-permute-start(bf16[2,64,128]{2,1,0:T(8,128)(2,1)S(1)} %edges.1), channel_id=1, source_target_pairs={{0,2},{2,0},{1,3},{3,1},{4,6},{6,4},{5,7},{7,5},{8,10},{10,8},{9,1... | collective-permute-start | bytes 98312 | tf_op jit(solution)/shard_map/ppermute | solution.py:371
  37.5 0.9 %gradient.1 = bf16[128,128]{1,0:T(8,128)(2,1)} custom-call(f32[128,8,128]{2,1,0:T(8,128)S(1)} %get-tuple-element.107.refs_0_), custom_call_target="tpu_custom_call" | custom-call | tf_op jit(solution)/shard_map/gradient/pallas_call | solution.py:553
  38.3 0.7 %add.1.total_ref = f32[21,64,128]{2,1,0:T(8,128)S(1)} custom-call(s32[64]{0:T(128)S(1)} %send.1.send_ref, f32[21,64,128]{2,1,0:T(8,128)S(1)} %get-tuple-element.105.total_ref._, bf16[8,64,128]{2,1,0:T(8,128)(2,1)S(1)} %collective-permute-done.10.rest_0_, bf16[8,64,128]{2,1,0:T(8,128)(2,1)S(1)} %collective-permute-done.11.rest_1_, ...), custom_call_target="tpu_custom_call", output_to_operand_aliasing={{}: (1, {})} | custom-call | tf_op jit(solution)/shard_map/add/pallas_call | solution.py:534
  39.0 1.2 %collective-permute-done.13.above_ref.below_ref = bf16[2,64,128]{2,1,0:T(8,128)(2,1)S(1)} collective-permute-done((bf16[2,64,128]{2,1,0:T(8,128)(2,1)S(1)}, bf16[2,64,128]{2,1,0:T(8,128)(2,1)S(1)}, u32[]{:S(2)}, u32[]{:S(2)}) %collective-permute-start.13) | collective-permute-done | bytes 32800 | tf_op jit(solution)/shard_map/ppermute | solution.py:371
  40.2 0.9 %finish.1 = f32[1024,128]{1,0:T(8,128)} custom-call(f32[21,64,128]{2,1,0:T(8,128)S(1)} %add.1.total_ref, bf16[2,64,128]{2,1,0:T(8,128)(2,1)S(1)} %collective-permute-done.13.above_ref.below_ref, bf16[2,64,128]{2,1,0:T(8,128)(2,1)S(1)} %collective-permute-done.13.above_ref.below_ref), custom_call_target="tpu_custom_call" | custom-call | tf_op jit(solution)/shard_map/finish/pallas_call | solution.py:543
  (4 shorter events, 0.0 us)
Async XLA Ops:
  0.6 4.1 %copy-start.1 = (s32[1,16,4,2,3]{1,3,4,2,0:T(2,128)S(1)}, s32[1,16,4,2,3]{1,3,4,2,0:T(2,128)}, u32[]{:S(2)}) copy-start(s32[1,16,4,2,3]{1,3,4,2,0:T(2,128)} %param.12) | copy-start | bytes 4612
  1.7 3.0 %copy-start.2 = (s32[1,16,4]{1,2,0:T(4,128)S(1)}, s32[1,16,4]{1,2,0:T(4,128)}, u32[]{:S(2)}) copy-start(s32[1,16,4]{1,2,0:T(4,128)} %param.13) | copy-start | bytes 772
  1.8 5.2 %collective-permute-start.6 = (bf16[2,64,128]{2,1,0:T(8,128)(2,1)S(1)}, bf16[2,64,128]{2,1,0:T(8,128)(2,1)S(1)}, u32[]{:S(2)}, u32[]{:S(2)}) collective-permute-start(bf16[2,64,128]{2,1,0:T(8,128)(2,1)S(1)} %get-tuple-element.75), channel_id=1, source_target_pairs={{0,2},{2,0},{1,3},{3,1},{4,6},{6,4},{5,7},{7,5},{8,10},{10,8},{9,1... | collective-permute-start | bytes 98312 | tf_op jit(solution)/shard_map/ppermute | solution.py:371
  6.9 5.5 %copy-start.3 = (bf16[1,16,1,2,4,128]{5,4,3,2,1,0:T(4,128)(2,1)S(1)}, bf16[1,16,1,2,4,128]{5,4,3,2,1,0:T(4,128)(2,1)}, u32[]{:S(2)}) copy-start(bf16[1,16,1,2,4,128]{5,4,3,2,1,0:T(4,128)(2,1)} %param.11) | copy-start | bytes 98308
  7.0 5.6 %copy-start = (bf16[16,4,16,128]{3,2,1,0:T(8,128)(2,1)S(1)}, bf16[16,4,16,128]{3,2,1,0:T(8,128)(2,1)}, u32[]{:S(2)}) copy-start(bf16[16,4,16,128]{3,2,1,0:T(8,128)(2,1)} %param.10) | copy-start | bytes 786436
  7.6 8.2 %collective-permute-start.7 = (bf16[8,64,128]{2,1,0:T(8,128)(2,1)S(1)}, bf16[8,64,128]{2,1,0:T(8,128)(2,1)S(1)}, u32[]{:S(2)}, u32[]{:S(2)}) collective-permute-start(bf16[8,64,128]{2,1,0:T(8,128)(2,1)S(1)} %get-tuple-element.77), channel_id=1, source_target_pairs={{0,4},{4,8},{8,12},{12,0},{1,5},{5,9},{9,13},{13,1},{2,6},{6,10},{... | collective-permute-start | bytes 393224 | tf_op jit(solution)/shard_map/ppermute | solution.py:408
  9.4 13.4 %collective-permute-start.8 = (bf16[8,64,128]{2,1,0:T(8,128)(2,1)S(1)}, bf16[8,64,128]{2,1,0:T(8,128)(2,1)S(1)}, u32[]{:S(2)}, u32[]{:S(2)}) collective-permute-start(bf16[8,64,128]{2,1,0:T(8,128)(2,1)S(1)} %get-tuple-element.78), channel_id=1, source_target_pairs={{0,12},{4,0},{8,4},{12,8},{1,13},{5,1},{9,5},{13,9},{2,14},{6,2},{... | collective-permute-start | bytes 393224 | tf_op jit(solution)/shard_map/ppermute | solution.py:408
  11.5 11.4 %collective-permute-start.9 = (bf16[8,64,128]{2,1,0:T(8,128)(2,1)S(1)}, bf16[8,64,128]{2,1,0:T(8,128)(2,1)S(1)}, u32[]{:S(2)}, u32[]{:S(2)}) collective-permute-start(bf16[8,64,128]{2,1,0:T(8,128)(2,1)S(1)} %get-tuple-element.79), channel_id=1, source_target_pairs={{0,8},{4,12},{8,0},{12,4},{1,9},{5,13},{9,1},{13,5},{2,10},{6,14},... | collective-permute-start | bytes 393224 | tf_op jit(solution)/shard_map/ppermute | solution.py:408
  25.0 10.7 %collective-permute-start.12 = (bf16[8,64,128]{2,1,0:T(8,128)(2,1)S(1)}, bf16[8,64,128]{2,1,0:T(8,128)(2,1)S(1)}, u32[]{:S(2)}, u32[]{:S(2)}) collective-permute-start(bf16[8,64,128]{2,1,0:T(8,128)(2,1)S(1)} %get-tuple-element.95), channel_id=1, source_target_pairs={{0,8},{4,12},{8,0},{12,4},{1,9},{5,13},{9,1},{13,5},{2,10},{6,14},... | collective-permute-start | bytes 393224 | tf_op jit(solution)/shard_map/ppermute | solution.py:408
  25.0 10.9 %collective-permute-start.10 = (bf16[8,64,128]{2,1,0:T(8,128)(2,1)S(1)}, bf16[8,64,128]{2,1,0:T(8,128)(2,1)S(1)}, u32[]{:S(2)}, u32[]{:S(2)}) collective-permute-start(bf16[8,64,128]{2,1,0:T(8,128)(2,1)S(1)} %get-tuple-element.93), channel_id=1, source_target_pairs={{0,12},{4,0},{8,4},{12,8},{1,13},{5,1},{9,5},{13,9},{2,14},{6,2},{... | collective-permute-start | bytes 393224 | tf_op jit(solution)/shard_map/ppermute | solution.py:408
  27.0 9.0 %collective-permute-start.11 = (bf16[8,64,128]{2,1,0:T(8,128)(2,1)S(1)}, bf16[8,64,128]{2,1,0:T(8,128)(2,1)S(1)}, u32[]{:S(2)}, u32[]{:S(2)}) collective-permute-start(bf16[8,64,128]{2,1,0:T(8,128)(2,1)S(1)} %get-tuple-element.94), channel_id=1, source_target_pairs={{0,4},{4,8},{8,12},{12,0},{1,5},{5,9},{9,13},{13,1},{2,6},{6,10},{... | collective-permute-start | bytes 393224 | tf_op jit(solution)/shard_map/ppermute | solution.py:408
  36.2 4.0 %collective-permute-start.13 = (bf16[2,64,128]{2,1,0:T(8,128)(2,1)S(1)}, bf16[2,64,128]{2,1,0:T(8,128)(2,1)S(1)}, u32[]{:S(2)}, u32[]{:S(2)}) collective-permute-start(bf16[2,64,128]{2,1,0:T(8,128)(2,1)S(1)} %edges.1), channel_id=1, source_target_pairs={{0,2},{2,0},{1,3},{3,1},{4,6},{6,4},{5,7},{7,5},{8,10},{10,8},{9,1... | collective-permute-start | bytes 98312 | tf_op jit(solution)/shard_map/ppermute | solution.py:371
